TPU v7x, 32 devices: a whole 2x2x4 slice. The times are simulated.
32 devices in a mesh: section: 4 (over y, x), batch: 8 (over z, core).
Axes of the slice: x: 2, y: 2, z: 4, core: 2. Of those that a mesh axis runs over, the one named last changes fastest.
Arguments:
- tokens: bfloat16 [4096, 768], P('batch'), may hold values from -6 to 6
- key_tokens: bfloat16 [4096, 768], P('batch'), may hold values from -6 to 6
- cotangent: bfloat16 [4096, 768], P('batch'), may hold values from -6 to 6
- lengths: int32 [16, 4], P('batch'), may hold values from 0 to 256, as said below
- query_mats: float32 [2, 768, 9216], P(None, 'batch')
- query_small: float32 [2, 8448], replicated
- key_mats: float32 [2, 768, 9216], P(None, 'batch')
- key_small: float32 [2, 8448], replicated
Outputs:
- activations: bfloat16 [4096, 768], P('batch', 'section')
- pooled_query: float32 [16, 4, 768], P('batch', None, 'section')
- pooled_key: float32 [16, 4, 768], P('batch', None, 'section')
- input_grad: bfloat16 [4096, 768], P('batch', 'section')
- grad_mats: float32 [2, 768, 9216], P(None, 'batch')
- grad_small: float32 [2, 8448], P(None, 'batch')
- key_mats_step: float32 [2, 768, 9216], P(None, 'batch')
- key_small_step: float32 [2, 8448], replicated
Inputs may be any that keep to these rules, and one draw needn't show every extreme that they name: `lengths`: each row lists its crops' token counts in order, each from 64 to 256, then zeros; a row's counts sum to 256 or less, and the tokens after them are padding.
All inputs are finite; a program needn't handle non-finite values.
Results may differ from a plain program's by a relative error of at most 0.018.
Values may be sent and summed in bfloat16 or wider, within the bound.
No kernel may reach another device: no remote copies, remote signals or barrier semaphores. Data moves between devices by JAX's collectives and lax.ppermute only.
A program may use at most 576 MiB of HBM per device.

v0:
```python
from functools import partial

import jax
import jax.numpy as jnp
from jax import lax
from jax.sharding import PartitionSpec as P

HEADS = 12
HEAD_DIM = 64
D = 768
LAYERS = 2
MICRO = 2
ROW = 256
CROPS = 4


epsilon = 1e-05
keep_rate = 0.9995


def passed_along(block, axis, distance):
    devices = range(lax.axis_size(axis))
    route = [(i - distance, i) for i in devices if i - distance in devices]
    return lax.ppermute(block, axis, route)


def spread_2(value, axis, source):
    kept = jnp.where(lax.axis_index(axis) == source, value, 0).astype(value.dtype)
    return lax.psum(kept, axis)


def layout(lens_row):
    boundary = jnp.cumsum(lens_row)
    position = jnp.arange(ROW, dtype=jnp.int32)
    segment = jnp.sum((position[:, None] >= boundary[None, :]).astype(jnp.int32), axis=1)
    filled = position < boundary[-1]
    allowed = (segment[:, None] == segment[None, :]) & filled[None, :] | (
        position[:, None] == position[None, :]
    )
    member = (
        (segment[:, None] == jnp.arange(CROPS, dtype=jnp.int32)[None, :]) & filled[:, None]
    ).astype(jnp.float32)
    return (allowed, member)


def normalize(summed, norm_gain, norm_shift):
    centre = summed - jnp.mean(summed, axis=-1, keepdims=True)
    spread = jnp.mean(centre * centre, axis=-1, keepdims=True)
    return centre * lax.rsqrt(spread + epsilon) * norm_gain + norm_shift


def by_head(block):
    return block.reshape(block.shape[0], HEADS, HEAD_DIM)


def contract_cols(left, right):
    return lax.dot_general(
        left, right, (((1,), (1,)), ((), ())), preferred_element_type=jnp.float32
    )


def contract_rows(left, right):
    return lax.dot_general(
        left, right, (((0,), (0,)), ((), ())), preferred_element_type=jnp.float32
    )


def attend(query, key_rows, values, allowed):
    score_scale = HEAD_DIM ** (-0.5)
    scores = (
        jnp.einsum(
            "qhd,khd->hqk", by_head(query), by_head(key_rows), preferred_element_type=jnp.float32
        )
        * score_scale
    )
    scores = jnp.where(allowed[None], scores, -1e30)
    row_max = jnp.max(scores, axis=-1, keepdims=True)
    exp_terms = jnp.exp(scores - row_max)
    attn_prob = exp_terms / jnp.sum(exp_terms, axis=-1, keepdims=True)
    mixed = jnp.einsum(
        "hqk,khd->qhd",
        attn_prob.astype(jnp.bfloat16),
        by_head(values),
        preferred_element_type=jnp.float32,
    )
    return (mixed.reshape(query.shape), attn_prob)


def attend_back(query, key_rows, values, attn_prob, grad_mixed):
    score_scale = HEAD_DIM ** (-0.5)
    grad_heads = by_head(grad_mixed)
    grad_values = jnp.einsum(
        "hqk,qhd->khd",
        attn_prob.astype(jnp.bfloat16),
        grad_heads,
        preferred_element_type=jnp.float32,
    )
    grad_prob = jnp.einsum(
        "qhd,khd->hqk", grad_heads, by_head(values), preferred_element_type=jnp.float32
    )
    grad_scores = attn_prob * (grad_prob - jnp.sum(grad_prob * attn_prob, axis=-1, keepdims=True))
    grad_scores = grad_scores.astype(jnp.bfloat16)
    grad_query = (
        jnp.einsum(
            "hqk,khd->qhd", grad_scores, by_head(key_rows), preferred_element_type=jnp.float32
        )
        * score_scale
    )
    grad_keys = (
        jnp.einsum("hqk,qhd->khd", grad_scores, by_head(query), preferred_element_type=jnp.float32)
        * score_scale
    )
    out_shape = query.shape
    return (
        grad_query.reshape(out_shape).astype(jnp.bfloat16),
        grad_keys.reshape(out_shape).astype(jnp.bfloat16),
        grad_values.reshape(out_shape).astype(jnp.bfloat16),
    )


def attention_forward(inputs, weights, small, allowed):
    project = jnp.dot(inputs, weights[:, : 3 * D], preferred_element_type=jnp.float32)
    query = project[:, :D].astype(jnp.bfloat16)
    key_rows = project[:, D : 2 * D].astype(jnp.bfloat16)
    values = (project[:, 2 * D : 3 * D] + small[:D]).astype(jnp.bfloat16)
    mixed, attn_prob = attend(query, key_rows, values, allowed)
    mixed = mixed.astype(jnp.bfloat16)
    branch = contract_cols(mixed, weights[:, 3 * D : 4 * D]) + small[D : 2 * D]
    summed = inputs.astype(jnp.float32) + branch
    return (summed, (query, key_rows, values, attn_prob, mixed))


def attention_backward(inputs, weights, small, allowed, grad_out):
    summed, saved = attention_forward(inputs, weights, small, allowed)
    query, key_rows, values, attn_prob, mixed = saved
    unused, norm_back = jax.vjp(normalize, summed, small[2 * D : 3 * D], small[3 * D : 4 * D])
    grad_summed, grad_gain, grad_shift = norm_back(grad_out.astype(jnp.float32))
    grad_branch = grad_summed.astype(jnp.bfloat16)
    grad_out_proj = contract_rows(grad_branch, mixed)
    grad_mixed = jnp.dot(
        grad_branch, weights[:, 3 * D : 4 * D], preferred_element_type=jnp.float32
    ).astype(jnp.bfloat16)
    grad_query, grad_keys, grad_values = attend_back(query, key_rows, values, attn_prob, grad_mixed)
    grad_proj = jnp.concatenate([grad_query, grad_keys, grad_values], axis=1)
    grad_in_proj = contract_rows(inputs, grad_proj)
    grad_inputs = grad_summed + contract_cols(grad_proj, weights[:, : 3 * D])
    col_width = weights.shape[1]
    grad_weights = jnp.concatenate(
        [grad_in_proj, grad_out_proj, jnp.zeros((D, col_width - 4 * D), jnp.float32)], axis=1
    )
    grad_small = jnp.concatenate(
        [
            jnp.sum(grad_values.astype(jnp.float32), axis=0),
            jnp.sum(grad_branch.astype(jnp.float32), axis=0),
            grad_gain,
            grad_shift,
            jnp.zeros((7 * D,), jnp.float32),
        ]
    )
    return (grad_inputs, grad_weights, grad_small)


def feed_forward(inputs, weights, small, ffn_base):
    hidden = (
        jnp.dot(inputs, weights[:, ffn_base : ffn_base + 4 * D], preferred_element_type=jnp.float32)
        + small[4 * D : 8 * D]
    )
    active = jax.nn.gelu(hidden, approximate=False).astype(jnp.bfloat16)
    branch = (
        contract_cols(active, weights[:, ffn_base + 4 * D : ffn_base + 8 * D])
        + small[8 * D : 9 * D]
    )
    summed = inputs.astype(jnp.float32) + branch
    return (summed, hidden, active)


def feed_backward(inputs, weights, small, ffn_base, grad_out):
    summed, hidden, active = feed_forward(inputs, weights, small, ffn_base)
    unused, norm_back = jax.vjp(normalize, summed, small[9 * D : 10 * D], small[10 * D :])
    grad_summed, grad_gain, grad_shift = norm_back(grad_out.astype(jnp.float32))
    grad_branch = grad_summed.astype(jnp.bfloat16)
    grad_down = contract_rows(grad_branch, active)
    grad_active = jnp.dot(
        grad_branch,
        weights[:, ffn_base + 4 * D : ffn_base + 8 * D],
        preferred_element_type=jnp.float32,
    )
    unused_value, gelu_back = jax.vjp(partial(jax.nn.gelu, approximate=False), hidden)
    grad_hidden = gelu_back(grad_active)[0].astype(jnp.bfloat16)
    grad_up = contract_rows(inputs, grad_hidden)
    grad_inputs = grad_summed + contract_cols(grad_hidden, weights[:, ffn_base : ffn_base + 4 * D])
    col_width = weights.shape[1]
    grad_weights = jnp.concatenate(
        [
            jnp.zeros((D, ffn_base), jnp.float32),
            grad_up,
            grad_down,
            jnp.zeros((D, col_width - ffn_base - 8 * D), jnp.float32),
        ],
        axis=1,
    )
    grad_small = jnp.concatenate(
        [
            jnp.zeros((4 * D,), jnp.float32),
            jnp.sum(grad_hidden.astype(jnp.float32), axis=0),
            jnp.sum(grad_branch.astype(jnp.float32), axis=0),
            grad_gain,
            grad_shift,
        ]
    )
    return (grad_inputs, grad_weights, grad_small)


def pick(stack, index):
    return lax.dynamic_index_in_dim(stack, index, 0, keepdims=False)


def put(stack, index, value, in_use):
    return lax.dynamic_update_index_in_dim(
        stack, jnp.where(in_use, value, pick(stack, index)), index, 0
    )


def on_device(tokens, key_tokens, cotangent, lengths, query_mats, query_small, key_mats, key_small):
    section_count = lax.axis_size("section")
    section_idx = lax.axis_index("section")
    layer_idx = section_idx // 2
    parity = section_idx % 2
    offset = parity * 0
    col_width = 12 * D
    ffn_base = 4 * D

    def take(mats):
        rows_here = pick(mats, layer_idx)
        return rows_here.astype(jnp.bfloat16)

    query_weights, key_weights = (
        lax.all_gather(take(query_mats), "batch", axis=0, tiled=True),
        lax.all_gather(take(key_mats), "batch", axis=0, tiled=True),
    )
    small_q = pick(query_small, layer_idx)
    small_k = pick(key_small, layer_idx)
    allowed_all, member_all = jax.vmap(layout)(lengths)
    own_q = tokens.reshape(MICRO, ROW, D)
    own_k = key_tokens.reshape(MICRO, ROW, D)

    def attention_pair(operands):
        first_in, second_in, allowed = operands
        first_sum, first_saved = attention_forward(first_in, query_weights, small_q, allowed)
        second_sum, second_saved = attention_forward(second_in, key_weights, small_k, allowed)
        first_out = normalize(first_sum, small_q[2 * D : 3 * D], small_q[3 * D : 4 * D]).astype(
            jnp.bfloat16
        )
        second_out = normalize(second_sum, small_k[2 * D : 3 * D], small_k[3 * D : 4 * D]).astype(
            jnp.bfloat16
        )
        return (first_out, second_out)

    def feed_pair(operands):
        first_in, second_in, allowed = operands
        first_sum, first_hidden, first_active = feed_forward(
            first_in, query_weights, small_q, ffn_base
        )
        second_sum, second_hidden, second_active = feed_forward(
            second_in, key_weights, small_k, ffn_base
        )
        first_out = normalize(first_sum, small_q[9 * D : 10 * D], small_q[10 * D :]).astype(
            jnp.bfloat16
        )
        second_out = normalize(second_sum, small_k[9 * D : 10 * D], small_k[10 * D :]).astype(
            jnp.bfloat16
        )
        return (first_out, second_out)

    kept = jnp.zeros((MICRO, ROW, D), jnp.bfloat16)
    final_q = jnp.zeros((MICRO, ROW, D), jnp.bfloat16)
    final_k = jnp.zeros((MICRO, ROW, D), jnp.bfloat16)
    sent_q = jnp.zeros((ROW, D), jnp.bfloat16)
    sent_k = jnp.zeros((ROW, D), jnp.bfloat16)
    tick_count = MICRO + section_count - 1
    for time_step in range(tick_count):
        if time_step > 0:
            arrived_q, arrived_k = passed_along((sent_q, sent_k), "section", 1)
        else:
            arrived_q, arrived_k = (sent_q, sent_k)
        micro_idx = time_step - section_idx
        in_use = (micro_idx >= 0) & (micro_idx < MICRO)
        slot_idx = jnp.clip(micro_idx, 0, MICRO - 1)
        input_q = jnp.where(section_idx == 0, pick(own_q, slot_idx), arrived_q)
        input_k = jnp.where(section_idx == 0, pick(own_k, slot_idx), arrived_k)
        kept = put(kept, slot_idx, input_q, in_use)
        allowed = pick(allowed_all, slot_idx)
        sent_q, sent_k = lax.cond(
            parity == 0, attention_pair, feed_pair, (input_q, input_k, allowed)
        )
        at_end = in_use & (section_idx == section_count - 1)
        final_q = put(final_q, slot_idx, sent_q, at_end)
        final_k = put(final_k, slot_idx, sent_k, at_end)

    def attention_grads(operands):
        inputs, grad_out, allowed = operands
        return attention_backward(inputs, query_weights, small_q, allowed, grad_out)

    def feed_grads(operands):
        inputs, grad_out, allowed = operands
        return feed_backward(inputs, query_weights, small_q, ffn_base, grad_out)

    upstream = cotangent.reshape(MICRO, ROW, D)
    grad_weights = jnp.zeros((D, col_width), jnp.float32)
    grad_small = jnp.zeros((11 * D,), jnp.float32)
    grad_first = jnp.zeros((MICRO, ROW, D), jnp.bfloat16)
    grad_send = jnp.zeros((ROW, D), jnp.bfloat16)
    for time_step in range(tick_count):
        if time_step > 0:
            arrived = passed_along(grad_send, "section", -1)
        else:
            arrived = grad_send
        micro_idx = time_step - (section_count - 1 - section_idx)
        in_use = (micro_idx >= 0) & (micro_idx < MICRO)
        slot_idx = jnp.clip(micro_idx, 0, MICRO - 1)
        grad_out = jnp.where(section_idx == section_count - 1, pick(upstream, slot_idx), arrived)
        allowed = pick(allowed_all, slot_idx)
        grad_inputs, step_weights, step_small = lax.cond(
            parity == 0, attention_grads, feed_grads, (pick(kept, slot_idx), grad_out, allowed)
        )
        grad_weights = grad_weights + jnp.where(in_use, step_weights, 0.0)
        grad_small = grad_small + jnp.where(in_use, step_small, 0.0)
        grad_send = grad_inputs.astype(jnp.bfloat16)
        grad_first = put(grad_first, slot_idx, grad_send, in_use & (section_idx == 0))
    rows_local = query_mats.shape[1]
    small_full = lax.dynamic_update_slice(
        jnp.zeros((LAYERS, 11 * D), jnp.float32), grad_small[None], (layer_idx, 0)
    )
    summed_weights, summed_small = (
        lax.psum_scatter(
            grad_weights.astype(jnp.bfloat16), "batch", scatter_dimension=0, tiled=True
        ).astype(jnp.float32),
        lax.psum_scatter(
            small_full.astype(jnp.bfloat16), "batch", scatter_dimension=1, tiled=True
        ).astype(jnp.float32),
    )
    placed = lax.dynamic_update_slice(
        jnp.zeros((LAYERS, rows_local, 12 * D), jnp.float32),
        summed_weights[None],
        (layer_idx, 0, offset),
    )
    grad_mats, grad_small_out = (
        lax.psum(placed.astype(jnp.bfloat16), "section").astype(jnp.float32),
        lax.psum(summed_small.astype(jnp.bfloat16), "section").astype(jnp.float32),
    )
    done_q, done_k = (
        spread_2(final_q, "section", section_count - 1),
        spread_2(final_k, "section", section_count - 1),
    )
    grad_tokens = spread_2(grad_first, "section", 0)
    col_part = D // section_count
    col_start = section_idx * col_part
    part_q = lax.dynamic_slice_in_dim(done_q, col_start, col_part, 2)
    part_k = lax.dynamic_slice_in_dim(done_k, col_start, col_part, 2)
    part_grad = lax.dynamic_slice_in_dim(grad_tokens, col_start, col_part, 2)
    member_low = member_all.astype(jnp.bfloat16)
    counts = jnp.maximum(lengths.astype(jnp.float32), 1.0)[:, :, None]
    pooled_query = (
        jnp.einsum("mpc,mpd->mcd", member_low, part_q, preferred_element_type=jnp.float32) / counts
    )
    pooled_key = (
        jnp.einsum("mpc,mpd->mcd", member_low, part_k, preferred_element_type=jnp.float32) / counts
    )
    activations = part_q.reshape(MICRO * ROW, col_part)
    input_grad = part_grad.reshape(MICRO * ROW, col_part)
    key_mats_step = (query_mats - key_mats) * (1.0 - keep_rate)
    key_small_step = (query_small - key_small) * (1.0 - keep_rate)
    return (
        activations,
        pooled_query,
        pooled_key,
        input_grad,
        grad_mats,
        grad_small_out,
        key_mats_step,
        key_small_step,
    )


def solution(mesh):
    in_specs = (
        P("batch", None),
        P("batch", None),
        P("batch", None),
        P("batch", None),
        P(None, "batch", None),
        P(),
        P(None, "batch", None),
        P(),
    )
    out_specs = (
        P("batch", "section"),
        P("batch", None, "section"),
        P("batch", None, "section"),
        P("batch", "section"),
        P(None, "batch", None),
        P(None, "batch"),
        P(None, "batch", None),
        P(),
    )
    return jax.shard_map(
        on_device, mesh=mesh, in_specs=in_specs, out_specs=out_specs, check_vma=False
    )
```

profile of v0, /device:TPU:8, one launch (start us, length us, event | category | flops | bytes accessed | tf_op | source)
XLA Modules:
  0.0 1334.1 jit_solution(4249642558330174525)
XLA Ops:
  19.5 119.1 %all-gather.5.cloned.1.call-done = bf16[1,768,9216]{2,1,0:T(8,128)(2,1)} async-done(((bf16[1,96,9216]{2,1,0:T(8,128)(2,1)}), bf16[1,768,9216]{2,1,0:T(8,128)(2,1)}) %all-gather.5.cloned.1.call-update) | async-done | bytes 14155792 | tf_op jit(solution)/shard_map/all_gather | solution.py:238
  138.6 130.1 %all-gather.7.cloned.1.call-done = bf16[1,768,9216]{2,1,0:T(8,128)(2,1)} async-done(((bf16[1,96,9216]{2,1,0:T(8,128)(2,1)}), bf16[1,768,9216]{2,1,0:T(8,128)(2,1)}) %all-gather.7.cloned.1.call-update) | async-done | bytes 14155792 | tf_op jit(solution)/shard_map/all_gather | solution.py:239
  268.7 41.9 %conditional.30 = (bf16[256,768]{0,1:T(8,128)(2,1)}, bf16[256,768]{0,1:T(8,128)(2,1)S(1)}) conditional(s32[]{:T(128)} %convert_element_type.1053, (bf16[256,768]{0,1:T(8,128)(2,1)S(1)}, bf16[768,9216]{1,0:T(8,128)(2,1)}, f32[8448]{0:T(1024)S(1)}, bf16[256,768]{0,1:T(8,128)(2,1)S(1)}, bf16[768,9216]{1,0:T(8,128)(2,1)}, ...), branch_computations={%region_2.7_spmd, %region_7.16_spmd} | conditional | flops 4940366336 | bytes 55453744
  329.7 42.4 %conditional.31 = (bf16[256,768]{0,1:T(8,128)(2,1)S(1)}, bf16[256,768]{0,1:T(8,128)(2,1)S(1)}) conditional(s32[]{:T(128)} %convert_element_type.1053, (bf16[256,768]{0,1:T(8,128)(2,1)S(1)}, bf16[768,9216]{1,0:T(8,128)(2,1)}, f32[8448]{0:T(1024)S(1)}, bf16[256,768]{0,1:T(8,128)(2,1)S(1)}, bf16[768,9216]{1,0:T(8,128)(2,1)}, ...), branch_computations={%region_16.21_spmd, %region_21.30_spmd} | conditional | flops 4940366336 | bytes 58599528
  391.7 42.6 %conditional.32 = (bf16[256,768]{0,1:T(8,128)(2,1)S(1)}, bf16[256,768]{0,1:T(8,128)(2,1)S(1)}) conditional(s32[]{:T(128)} %convert_element_type.1053, (bf16[256,768]{0,1:T(8,128)(2,1)S(1)}, bf16[768,9216]{1,0:T(8,128)(2,1)}, f32[8448]{0:T(1024)S(1)}, bf16[256,768]{0,1:T(8,128)(2,1)S(1)}, bf16[768,9216]{1,0:T(8,128)(2,1)}, ...), branch_computations={%region_30.35_spmd, %region_35.44_spmd} | conditional | flops 4940366336 | bytes 58599528
  436.3 13.8 %collective-permute-start.4 = (bf16[256,768]{0,1:T(8,128)(2,1)S(1)}, bf16[256,768]{0,1:T(8,128)(2,1)}, u32[]{:S(2)}, u32[]{:S(2)}) collective-permute-start(bf16[256,768]{0,1:T(8,128)(2,1)S(1)} %get-tuple-element.1027), channel_id=1, source_target_pairs={{0,8},{8,16},{16,24},{1,9},{9,17},{17,25},{2,10},{10,18},{18,26},{... | collective-permute-start | bytes 1179656 | tf_op jit(solution)/shard_map/ppermute | solution.py:24
  456.4 40.4 %conditional.33 = (bf16[256,768]{0,1:T(8,128)(2,1)}, bf16[256,768]{0,1:T(8,128)(2,1)S(1)}) conditional(s32[]{:T(128)} %convert_element_type.1053, (bf16[256,768]{0,1:T(8,128)(2,1)S(1)}, bf16[768,9216]{1,0:T(8,128)(2,1)}, f32[8448]{0:T(1024)S(1)}, bf16[256,768]{0,1:T(8,128)(2,1)S(1)}, bf16[768,9216]{1,0:T(8,128)(2,1)}, ...), branch_computations={%region_44.49_spmd, %region_49.58_spmd} | conditional | flops 4940366336 | bytes 55453744
  506.9 83.1 %conditional.35 = (f32[8448]{0:T(1024)S(1)}, bf16[256,768]{1,0:T(8,128)(2,1)}, f32[768,9216]{1,0:T(8,128)}, bf16[256,768]{0,1:T(8,128)(2,1)S(1)}) conditional(s32[]{:T(128)} %convert_element_type.1053, (bf16[768,9216]{1,0:T(8,128)(2,1)}, bf16[256,768]{1,0:T(8,128)(2,1)S(1)}, f32[8448]{0:T(1024)S(1)}, bf16[256,768]{0,1:T(8,128)(2,1)S(1)}) %tuple.679, ...), branch_computations={%region_74.83_spmd, %region_83.95_spmd} | conditional | flops 7332491776 | bytes 237370464
  548.8 12.3 maximum_maximum_fusion
  561.2 27.7 %copy.708 = f32[768,9216]{1,0:T(8,128)} copy(f32[768,9216]{0,1:T(8,128)} %maximum_maximum_fusion) | data formatting | bytes 56623104 | tf_op jit(solution)/shard_map/conditional.15
  592.6 18.8 %collective-permute-done.8 = bf16[256,768]{1,0:T(8,128)(2,1)S(1)} collective-permute-done((bf16[256,768]{1,0:T(8,128)(2,1)}, bf16[256,768]{1,0:T(8,128)(2,1)S(1)}, u32[]{:S(2)}, u32[]{:S(2)}) %collective-permute-start.8) | collective-permute-done | bytes 393248 | tf_op jit(solution)/shard_map/ppermute | solution.py:24
  611.4 83.0 %conditional.36 = (f32[8448]{0:T(1024)S(1)}, bf16[256,768]{1,0:T(8,128)(2,1)}, f32[768,9216]{1,0:T(8,128)}, bf16[256,768]{0,1:T(8,128)(2,1)S(1)}) conditional(s32[]{:T(128)} %convert_element_type.1053, (bf16[768,9216]{1,0:T(8,128)(2,1)}, bf16[256,768]{1,0:T(8,128)(2,1)S(1)}, f32[8448]{0:T(1024)S(1)}, ...), branch_computations={%region_95.104_spmd, %region_104.116_spmd} | conditional | flops 7332491776 | bytes 230293568
  665.5 27.7 %copy.712 = f32[768,9216]{1,0:T(8,128)} copy(f32[768,9216]{0,1:T(8,128)} %maximum_maximum_fusion.1) | data formatting | bytes 56623104 | tf_op jit(solution)/shard_map/conditional.16
  704.4 83.2 %conditional.37 = (f32[8448]{0:T(1024)S(1)}, bf16[256,768]{1,0:T(8,128)(2,1)}, f32[768,9216]{1,0:T(8,128)}, bf16[256,768]{0,1:T(8,128)(2,1)S(1)}) conditional(s32[]{:T(128)} %convert_element_type.1053, (bf16[768,9216]{1,0:T(8,128)(2,1)}, bf16[256,768]{1,0:T(8,128)(2,1)S(1)}, f32[8448]{0:T(1024)S(1)}, ...), branch_computations={%region_116.125_spmd, %region_125.137_spmd} | conditional | flops 7332491776 | bytes 230293568
  758.6 27.8 %copy.716 = f32[768,9216]{1,0:T(8,128)} copy(f32[768,9216]{0,1:T(8,128)} %maximum_maximum_fusion.2) | data formatting | bytes 56623104 | tf_op jit(solution)/shard_map/conditional.17
  797.5 82.9 %conditional.38 = (f32[8448]{0:T(1024)S(1)}, bf16[256,768]{1,0:T(8,128)(2,1)}, f32[768,9216]{1,0:T(8,128)}, bf16[256,768]{0,1:T(8,128)(2,1)S(1)}) conditional(s32[]{:T(128)} %convert_element_type.1053, (bf16[768,9216]{1,0:T(8,128)(2,1)}, bf16[256,768]{1,0:T(8,128)(2,1)S(1)}, f32[8448]{0:T(1024)S(1)}, ...), branch_computations={%region_137.146_spmd, %region_146.158_spmd} | conditional | flops 7332491776 | bytes 230293568
  851.5 27.7 %copy.720 = f32[768,9216]{1,0:T(8,128)} copy(f32[768,9216]{0,1:T(8,128)} %maximum_maximum_fusion.3) | data formatting | bytes 56623104 | tf_op jit(solution)/shard_map/conditional.18
  890.3 76.5 %conditional.39 = (f32[8448]{0:T(1024)S(1)}, f32[768,9216]{1,0:T(8,128)}, bf16[256,768]{0,1:T(8,128)(2,1)S(1)}) conditional(s32[]{:T(128)} %convert_element_type.1053, (bf16[768,9216]{1,0:T(8,128)(2,1)}, bf16[256,768]{1,0:T(8,128)(2,1)S(1)}, f32[8448]{0:T(1024)S(1)}, bf16[256,768]{1,0:T(8,128)(2,1)S(1)}) %tuple.677, ...), branch_computations={%region_158.167_spmd, %region_167.179_spmd} | conditional | flops 7332491776 | bytes 236585056
  935.5 27.7 %copy.724 = f32[768,9216]{1,0:T(8,128)} copy(f32[768,9216]{0,1:T(8,128)} %maximum_maximum_fusion.4) | data formatting | bytes 56623104 | tf_op jit(solution)/shard_map/conditional.19
  966.8 25.9 %add_convert_fusion.35 = bf16[768,9216]{1,0:T(8,128)(2,1)} fusion(f32[768,9216]{1,0:T(8,128)} %get-tuple-element.1041, f32[768,9216]{1,0:T(8,128)} %get-tuple-element.1039, f32[768,9216]{1,0:T(8,128)} %get-tuple-element.1037, f32[768,9216]{1,0:T(8,128)} %get-tuple-element.1035, f32[768,9216]{1,0:T(8,128)} %get-tuple-element.1033, pred[]{:T(512)S(6)} %and.111, ...), kind=kLoop, calls=%fused_computation.1735 | loop fusion | flops 70778880 | bytes 155713536 | tf_op jit(solution)/shard_map/convert_element_type | solution.py:336
  1010.0 42.8 %conditional.34 = (bf16[256,768]{0,1:T(8,128)(2,1)}, bf16[256,768]{0,1:T(8,128)(2,1)S(1)}) conditional(s32[]{:T(128)} %convert_element_type.1053, (bf16[256,768]{0,1:T(8,128)(2,1)S(1)}, bf16[768,9216]{1,0:T(8,128)(2,1)}, f32[8448]{0:T(1024)S(1)}, bf16[256,768]{0,1:T(8,128)(2,1)S(1)}, bf16[768,9216]{1,0:T(8,128)(2,1)}, ...), branch_computations={%region_58.63_spmd, %region_63.72_spmd} | conditional | flops 4940366336 | bytes 55490692
  1061.7 77.7 %reduce-scatter.5.cloned.1.call-done = bf16[96,9216]{1,0:T(8,128)(2,1)} async-done(((bf16[768,9216]{1,0:T(8,128)(2,1)}), bf16[96,9216]{1,0:T(8,128)(2,1)}) %reduce-scatter.5.cloned.1.call-update) | async-done | bytes 1769488 | tf_op jit(solution)/shard_map/reduce_scatter | solution.py:335
  1153.7 21.1 %reduce-scatter.7.cloned.1.call-done = bf16[1056,2]{1,0:T(8,128)(2,1)} async-done(((bf16[8448,2]{1,0:T(8,128)(2,1)}), bf16[1056,2]{1,0:T(8,128)(2,1)}) %reduce-scatter.7.cloned.1.call-update) | async-done | bytes 4240
  1186.6 128.4 %all-reduce.3.cloned.1.call-done = (bf16[2,256,768]{1,2,0:T(8,128)(2,1)}, bf16[2,256,768]{1,2,0:T(8,128)(2,1)}, bf16[2,256,768]{1,2,0:T(8,128)(2,1)}, bf16[2,96,9216]{2,1,0:T(8,128)(2,1)}) async-done(((bf16[2,256,768]{1,2,0:T(8,128)(2,1)}, bf16[2,256,768]{1,2,0:T(8,128)(2,1)}, bf16[2,256,768]{1,2,0:T(8,128)(2,1)}, bf16[2,96,9216]{2,1,0:T(8,128)(2,1)}), (bf16[2,256,768]{1,2,0:T(8,128)(2,1)}, ...) | async-done | bytes 5898256 | tf_op jit(solution)/shard_map/psum | solution.py:29
  (691 shorter events, 551.9 us)
Async XLA Ops:
  7.2 131.5 %all-gather.5.cloned.1.call-start = ((), (), s32[]{:S(2)}) async-start(), calls=%async_computation.3 | async-start | bytes 15925248 | tf_op jit(solution)/shard_map/all_gather | solution.py:238
  10.7 258.1 %all-gather.7.cloned.1.call-start = ((), (), s32[]{:S(2)}) async-start(), calls=%async_computation.4 | async-start | bytes 15925248 | tf_op jit(solution)/shard_map/all_gather | solution.py:239
  14.3 1125.2 %reduce-scatter.5.cloned.1.call-start = ((), (), s32[]{:S(2)}) async-start(), calls=%async_computation.2 | async-start | bytes 15925248 | tf_op jit(solution)/shard_map/reduce_scatter | solution.py:335
  17.4 439.0 %copy-start.17 = (f32[8448]{0:T(1024)}, f32[8448]{0:T(1024)S(1)}, u32[]{:S(2)}) copy-start(f32[8448]{0:T(1024)S(1)} %get-tuple-element.1472) | copy-start | bytes 101380
  310.6 10.7 collective-permute-start.1
  312.7 16.8 %collective-permute-start = (bf16[256,768]{0,1:T(8,128)(2,1)}, bf16[256,768]{0,1:T(8,128)(2,1)}, u32[]{:S(2)}, u32[]{:S(2)}) collective-permute-start(bf16[256,768]{0,1:T(8,128)(2,1)} %get-tuple-element.1023), channel_id=1, source_target_pairs={{0,8},{8,16},{16,24},{1,9},{9,17},{17,25},{2,10},{10,18},{18,26},{... | collective-permute-start | bytes 1179656 | tf_op jit(solution)/shard_map/ppermute | solution.py:24
  372.1 12.9 collective-permute-start.3
  374.2 17.3 %collective-permute-start.2 = (bf16[256,768]{0,1:T(8,128)(2,1)S(1)}, bf16[256,768]{0,1:T(8,128)(2,1)}, u32[]{:S(2)}, u32[]{:S(2)}) collective-permute-start(bf16[256,768]{0,1:T(8,128)(2,1)S(1)} %get-tuple-element.1025), channel_id=1, source_target_pairs={{0,8},{8,16},{16,24},{1,9},{9,17},{17,25},{2,10},{10,18},{18,26},{... | collective-permute-start | bytes 1179656 | tf_op jit(solution)/shard_map/ppermute | solution.py:24
  391.7 58.5 %copy-start.21 = (bf16[1,256,768]{2,1,0:T(8,128)(2,1)S(1)}, bf16[1,256,768]{2,1,0:T(8,128)(2,1)}, u32[]{:S(2)}) copy-start(bf16[1,256,768]{2,1,0:T(8,128)(2,1)} %get-tuple-element.1470) | copy-start | bytes 1179652
  391.7 58.7 %copy-start.20 = (bf16[1,256,768]{2,1,0:T(8,128)(2,1)S(1)}, bf16[1,256,768]{2,1,0:T(8,128)(2,1)}, u32[]{:S(2)}) copy-start(bf16[1,256,768]{2,1,0:T(8,128)(2,1)} %get-tuple-element.1456) | copy-start | bytes 1179652
  434.3 16.3 %collective-permute-start.5 = (bf16[256,768]{0,1:T(8,128)(2,1)S(1)}, bf16[256,768]{0,1:T(8,128)(2,1)}, u32[]{:S(2)}, u32[]{:S(2)}) collective-permute-start(bf16[256,768]{0,1:T(8,128)(2,1)S(1)} %get-tuple-element.1028), channel_id=1, source_target_pairs={{0,8},{8,16},{16,24},{1,9},{9,17},{17,25},{2,10},{10,18},{18,26},{... | collective-permute-start | bytes 1179656 | tf_op jit(solution)/shard_map/ppermute | solution.py:24
  436.3 19.8 %collective-permute-start.4 = (bf16[256,768]{0,1:T(8,128)(2,1)S(1)}, bf16[256,768]{0,1:T(8,128)(2,1)}, u32[]{:S(2)}, u32[]{:S(2)}) collective-permute-start(bf16[256,768]{0,1:T(8,128)(2,1)S(1)} %get-tuple-element.1027), channel_id=1, source_target_pairs={{0,8},{8,16},{16,24},{1,9},{9,17},{17,25},{2,10},{10,18},{18,26},{... | collective-permute-start | bytes 1179656 | tf_op jit(solution)/shard_map/ppermute | solution.py:24
  456.4 41.8 %copy-start.9 = (bf16[512,768]{1,0:T(8,128)(2,1)S(1)}, bf16[512,768]{1,0:T(8,128)(2,1)}, u32[]{:S(2)}) copy-start(bf16[512,768]{1,0:T(8,128)(2,1)} %param.30) | copy-start | bytes 2359300
  496.8 7.7 collective-permute-start.6
  590.1 21.3 %collective-permute-start.8 = (bf16[256,768]{1,0:T(8,128)(2,1)}, bf16[256,768]{1,0:T(8,128)(2,1)S(1)}, u32[]{:S(2)}, u32[]{:S(2)}) collective-permute-start(bf16[256,768]{1,0:T(8,128)(2,1)} %get-tuple-element.698), channel_id=1, source_target_pairs={{8,0},{16,8},{24,16},{9,1},{17,9},{25,17},{10,2},{18,10},{26,18},{... | collective-permute-start | bytes 1179656 | tf_op jit(solution)/shard_map/ppermute | solution.py:24
  694.4 9.9 collective-permute-start.9
  758.6 29.0 %copy-start.86 = (f32[8448]{0:T(1024)S(1)}, f32[8448]{0:T(1024)}, u32[]{:S(2)}) copy-start(f32[8448]{0:T(1024)} %copy-done.85) | copy-start | bytes 101380 | tf_op jit(solution)/shard_map/conditional.17
  787.6 9.9 collective-permute-start.10
  880.4 9.9 collective-permute-start.11
  992.8 182.1 %reduce-scatter.7.cloned.1.call-start = ((), (), s32[]{:S(2)}) async-start(), calls=%async_computation.5 | async-start | bytes 2433024
  996.0 13.9 %collective-permute-start.7 = (bf16[256,768]{0,1:T(8,128)(2,1)S(1)}, bf16[256,768]{0,1:T(8,128)(2,1)S(1)}, u32[]{:S(2)}, u32[]{:S(2)}) collective-permute-start(bf16[256,768]{0,1:T(8,128)(2,1)S(1)} %copy-done.46), channel_id=1, source_target_pairs={{0,8},{8,16},{16,24},{1,9},{9,17},{17,25},{2,10},{10,18},{18,26},{... | collective-permute-start | bytes 1179656 | tf_op jit(solution)/shard_map/ppermute | solution.py:24
  1061.7 253.3 %all-reduce.3.cloned.1.call-start = ((), (), s32[]{:S(2)}) async-start(), calls=%async_computation.6 | async-start | bytes 11796480 | tf_op jit(solution)/shard_map/psum | solution.py:29
  1144.5 172.1 %copy-start.98 = (s32[2,256]{1,0:T(2,128)S(1)}, s32[2,256]{1,0:T(2,128)}, u32[]{:S(2)}) copy-start(s32[2,256]{1,0:T(2,128)} %copy-done.97) | copy-start | bytes 6148
  1144.5 172.1 %copy-start.101 = (pred[2,256]{1,0:T(4,128)(4,1)S(1)}, pred[2,256]{1,0:T(4,128)(4,1)}, u32[]{:S(2)}) copy-start(pred[2,256]{1,0:T(4,128)(4,1)} %copy-done.100) | copy-start | bytes 1540
  (92 other events, 488.9 us)
Sparse Core Ops, SparseCore 0:
  10.8 127.7 all-gather.4
  140.8 127.8 all-gather.6
  992.9 146.4 reduce-scatter.4
  1141.6 33.2 reduce-scatter.6
  1179.1 135.8 all-reduce.2
where the time goes:
time: 1350 us; the launch traced here: 1330 us
  waiting for transfers between devices  546 us (40%)
  matrix products  256 us (19%)
  local copies, waits for them, and re-layouts  245 us (18%)
  other arithmetic  129 us (10%)
  loops' own time  81 us (6%)
  starting transfers between devices  51.5 us (4%)
  between operations  15.3 us (1%)
    another operation x152, local copies, waits for them, and re-layouts  154 us
    all_gather x1, waiting for transfers between devices, on_device(): lax.all_gather(take(key_mats), 'batch', axis=0, tiled=True)  130 us
    psum x1, waiting for transfers between devices, spread_2(): return lax.psum(kept, axis)  128 us
    all_gather x1, waiting for transfers between devices, on_device(): lax.all_gather(take(query_mats), 'batch', axis=0, tiled=True)  119 us
    unnamed x10, loops' own time  81 us
    reduce_scatter x1, waiting for transfers between devices, on_device(): lax.psum_scatter(grad_weights.astype(jnp.bfloat16), 'batch', scatter_dime...  77.7 us
    ppermute x12, waiting for transfers between devices, passed_along(): return lax.ppermute(block, axis, route)  69.8 us
    concatenate x5, other arithmetic, attention_backward(): jnp.concatenate([grad_in_proj, grad_out_proj, jnp.zeros((D, col_width - 4...  61.7 us
  transfers between devices with their start and end apart: 17, of which 15 were waited for; matrix products, arithmetic and copies ran while one was open for 6% of the time, Pallas kernels for 0%

commit v1 on v0

v1 whole, which is shorter than its diff:
```python
from functools import partial

import jax
import jax.numpy as jnp
from jax import lax
from jax.experimental import pallas as pl
from jax.experimental.pallas import tpu as pltpu
from jax.sharding import PartitionSpec as P

HEADS = 12
HEAD_DIM = 64
D = 768
LAYERS = 2
MICRO = 2
ROW = 256
CROPS = 4
TOK = MICRO * ROW
SMALL = 11 * D

epsilon = 1e-05
keep_rate = 0.9995
score_scale = HEAD_DIM ** (-0.5)
bf16 = jnp.bfloat16
f32 = jnp.float32

AT_BV, AT_BO, AT_G1, AT_S1, AT_B1, AT_B2, AT_G2, AT_S2 = (
    0,
    D,
    2 * D,
    3 * D,
    4 * D,
    8 * D,
    9 * D,
    10 * D,
)


def swap_x(block):
    return lax.ppermute(block, "section", [(0, 1), (1, 0), (2, 3), (3, 2)])


def swap_y(block):
    return lax.ppermute(block, "section", [(0, 2), (2, 0), (1, 3), (3, 1)])


def swap_core(block):
    count = lax.axis_size("batch")
    return lax.ppermute(block, "batch", [(i, i ^ 1) for i in range(count)])


def shift_z(block, distance):
    count = lax.axis_size("batch")
    return lax.ppermute(block, "batch", [(i, (i + 2 * distance) % count) for i in range(count)])


def add_low(left, right):
    return (left.astype(f32) + right.astype(f32)).astype(bf16)


def sum_parts(part_0, part_1):
    here_0, here_1 = swap_x(part_0), swap_y(part_1)
    half_0, half_1 = add_low(part_0, here_0), add_low(part_1, here_1)
    return (half_0, swap_y(half_0), half_1, swap_x(half_1))


def gather_rows(block):
    places = lax.axis_size("batch") // 2
    me = lax.axis_index("batch")
    z, core = me // 2, me % 2
    found = [block] + [shift_z(block, d) for d in range(1, places)]
    order = (z - jnp.arange(places)) % places
    stacked = jnp.stack(found)
    other = swap_core(stacked)
    both = jnp.where(core == 0, jnp.stack([stacked, other], 1), jnp.stack([other, stacked], 1))
    whole = jnp.take(both, (z - jnp.arange(places)) % places, axis=0)
    return whole.reshape(places * 2 * block.shape[0], block.shape[1])


def scatter_rows(block, rows):
    places = lax.axis_size("batch") // 2
    me = lax.axis_index("batch")
    z, core = me // 2, me % 2
    parted = block.reshape(places, 2, rows, block.shape[1])
    mine = lax.dynamic_index_in_dim(parted, core, 1, keepdims=False)
    other = lax.dynamic_index_in_dim(parted, 1 - core, 1, keepdims=False)
    chip = add_low(mine, swap_core(other))
    total = lax.dynamic_index_in_dim(chip, z, 0, keepdims=False).astype(f32)
    for d in range(1, places):
        leaving = lax.dynamic_index_in_dim(chip, (z + d) % places, 0, keepdims=False)
        total = total + shift_z(leaving, d).astype(f32)
    return total.astype(bf16)


def gather_section(block):
    count = lax.axis_size("section")
    me = lax.axis_index("section")
    found = [block] + [
        lax.ppermute(block, "section", [(i, i ^ k) for i in range(count)]) for k in range(1, count)
    ]
    stacked = jnp.stack(found)
    return jnp.take(stacked, me ^ jnp.arange(count), axis=0)


def dot_nn(left, right):
    return jnp.dot(left, right, preferred_element_type=f32)


def dot_nt(left, right):
    return lax.dot_general(left, right, (((1,), (1,)), ((), ())), preferred_element_type=f32)


def dot_tn(left, right):
    return lax.dot_general(left, right, (((0,), (0,)), ((), ())), preferred_element_type=f32)


def ends_of(lens_ref, row):
    ends, total = [], 0
    for c in range(CROPS):
        total = total + lens_ref[row, c]
        ends.append(total)
    return ends


def segments(ends, shape, dim):
    position = lax.broadcasted_iota(jnp.int32, shape, dim)
    segment = jnp.zeros(shape, jnp.int32)
    for end in ends:
        segment = segment + (position >= end).astype(jnp.int32)
    return position, segment


def allowed_of(lens_ref, row):
    ends = ends_of(lens_ref, row)
    pos_q, seg_q = segments(ends, (ROW, 1), 0)
    pos_k, seg_k = segments(ends, (1, ROW), 1)
    seg_k = jnp.where(pos_k < ends[-1], seg_k, -1)
    return (seg_q == seg_k) | (pos_q == pos_k)


def pooled_of(lens_ref, row, values):
    ends = ends_of(lens_ref, row)
    pos, seg = segments(ends, (1, ROW), 1)
    crop = lax.broadcasted_iota(jnp.int32, (8, 1), 0)
    seg = jnp.where(pos < ends[-1], seg, -1)
    member = (seg == crop).astype(f32).astype(bf16)
    counts = jnp.ones((8, 1), f32)
    for c in range(CROPS):
        counts = jnp.where(crop == c, jnp.maximum(lens_ref[row, c], 1).astype(f32), counts)
    return (dot_nn(member, values) / counts)[:CROPS]


def standard(summed):
    centre = summed - jnp.mean(summed, axis=-1, keepdims=True)
    spread = jnp.mean(centre * centre, axis=-1, keepdims=True)
    rate = lax.rsqrt(spread + epsilon)
    return centre * rate, rate


def small_at(small_ref, layer, offset, width=D):
    return small_ref[layer : layer + 1, offset : offset + width]


def rows_of(row):
    return slice(row * ROW, (row + 1) * ROW)


def norm_in(layer, gain_at, shift_at, bias_at, base_ref, sums, small_ref, row):
    half, other = sums[2 * row], sums[2 * row + 1]
    branch = half[...].astype(f32) + other[...].astype(f32) + small_at(small_ref, layer, bias_at)
    hat, rate = standard(base_ref[rows_of(row), :].astype(f32) + branch)
    out = hat * small_at(small_ref, layer, gain_at) + small_at(small_ref, layer, shift_at)
    return out.astype(bf16), hat, rate


def attention_kernel(layer, first, keep, *refs):
    refs = list(refs)
    if first:
        base_ref = refs.pop(0)
    else:
        base_ref, sums, small_ref = refs[0], refs[1:5], refs[5]
        refs = refs[6:]
    weights_ref, bv_ref, lens_ref = refs[:3]
    outs = refs[3:]
    part_refs, outs = outs[:2], outs[2:]
    if not first:
        y_ref, outs = outs[0], outs[1:]
        if keep:
            hat_ref, rate_ref = outs[:2]
            outs = outs[2:]
    if keep:
        q_ref, k_ref, v_ref, mixed_ref, prob_ref = outs
    part = HEADS // 4 * HEAD_DIM
    lane = lax.broadcasted_iota(jnp.int32, (1, part), 1)
    for row in range(MICRO):
        here = rows_of(row)
        if first:
            inputs = base_ref[here, :]
        else:
            inputs, hat, rate = norm_in(
                layer - 1, AT_G2, AT_S2, AT_B2, base_ref, sums, small_ref, row
            )
            y_ref[here, :] = inputs
            if keep:
                hat_ref[here, :] = hat
                rate_ref[here, :] = jnp.broadcast_to(rate, (ROW, 128))
        project = dot_nn(inputs, weights_ref[:, : 3 * part])
        query = project[:, :part]
        key_rows = project[:, part : 2 * part].astype(bf16)
        values = (project[:, 2 * part :] + bv_ref[layer : layer + 1, :]).astype(bf16)
        allowed = allowed_of(lens_ref, row)
        mixed = jnp.zeros((ROW, part), f32)
        for head in range(part // HEAD_DIM):
            inside = (lane >= head * HEAD_DIM) & (lane < (head + 1) * HEAD_DIM)
            head_q = jnp.where(inside, query, 0.0).astype(bf16)
            scores = jnp.where(allowed, dot_nt(head_q, key_rows) * score_scale, -1e30)
            terms = jnp.exp(scores - jnp.max(scores, axis=-1, keepdims=True))
            prob = terms / jnp.sum(terms, axis=-1, keepdims=True)
            if keep:
                prob_ref[row, head] = prob
            mixed = jnp.where(inside, dot_nn(prob.astype(bf16), values), mixed)
        mixed = mixed.astype(bf16)
        part_refs[row][...] = dot_nt(mixed, weights_ref[:, 3 * part :]).astype(bf16)
        if keep:
            q_ref[here, :] = query.astype(bf16)
            k_ref[here, :] = key_rows
            v_ref[here, :] = values
            mixed_ref[here, :] = mixed


def feed_kernel(layer, keep, *refs):
    base_ref, sums, small_ref = refs[0], refs[1:5], refs[5]
    weights_ref, b1_ref = refs[6:8]
    part_refs, y_ref = refs[8:10], refs[10]
    if keep:
        hat_ref, rate_ref, hidden_ref, active_ref = refs[11:]
    for row in range(MICRO):
        here = rows_of(row)
        inputs, hat, rate = norm_in(layer, AT_G1, AT_S1, AT_BO, base_ref, sums, small_ref, row)
        y_ref[here, :] = inputs
        hidden = dot_nn(inputs, weights_ref[:, :D]) + b1_ref[layer : layer + 1, :]
        active = (0.5 * hidden * (1.0 + lax.erf(hidden * (0.5**0.5)))).astype(bf16)
        part_refs[row][...] = dot_nt(active, weights_ref[:, D:]).astype(bf16)
        if keep:
            hat_ref[here, :] = hat
            rate_ref[here, :] = jnp.broadcast_to(rate, (ROW, 128))
            hidden_ref[here, :] = hidden
            active_ref[here, :] = active


def last_kernel(layer, base_ref, *refs):
    sums, small_ref, lens_ref, pooled_ref = refs[:4], refs[4], refs[5], refs[6]
    for row in range(MICRO):
        out, hat, rate = norm_in(layer, AT_G2, AT_S2, AT_B2, base_ref, sums, small_ref, row)
        pooled_ref[row] = pooled_of(lens_ref, row, out)


def norm_back(grad_out, hat, rate, gain):
    inner = grad_out * gain
    grad = rate * (
        inner
        - jnp.mean(inner, axis=-1, keepdims=True)
        - hat * jnp.mean(inner * hat, axis=-1, keepdims=True)
    )
    return grad


def row_sum(block):
    return jnp.sum(block, axis=0, keepdims=True)


def feed_back_kernel(layer, last, *refs):
    refs = list(refs)
    if last:
        base_ref, sums, cot_ref, lens_ref = refs[0], refs[1:5], refs[5], refs[6]
        refs = refs[7:]
    else:
        base_ref, sums, hat_ref, rate_ref = refs[0], refs[1:5], refs[5], refs[6]
        refs = refs[7:]
    small_ref, weights_ref, hidden_ref = refs[:3]
    part_refs = refs[3:5]
    carry_ref, branch_ref, grad_hidden_ref, sums_ref, bias_ref = refs[5:10]
    if last:
        y_ref, pooled_ref = refs[10:]
    gain = small_at(small_ref, layer, AT_G2)
    totals = [jnp.zeros((1, D), f32) for _ in range(4)]
    for row in range(MICRO):
        here = rows_of(row)
        if last:
            out, hat, rate = norm_in(layer, AT_G2, AT_S2, AT_B2, base_ref, sums, small_ref, row)
            y_ref[here, :] = out
            pooled_ref[row] = pooled_of(lens_ref, row, out)
            grad_out = cot_ref[here, :].astype(f32)
        else:
            hat, rate = hat_ref[here, :], rate_ref[here, :1]
            grad_out = base_ref[here, :] + (
                sums[2 * row][...].astype(f32) + sums[2 * row + 1][...].astype(f32)
            )
            grad_out = grad_out.astype(bf16).astype(f32)
        grad = norm_back(grad_out, hat, rate, gain)
        carry_ref[here, :] = grad
        branch = grad.astype(bf16)
        branch_ref[here, :] = branch
        grad_active = dot_nn(branch, weights_ref[:, D:])
        hidden = hidden_ref[here, :]
        slope = 0.5 * (1.0 + lax.erf(hidden * (0.5**0.5))) + hidden * (
            jnp.exp(-0.5 * hidden * hidden) * 0.3989422804014327
        )
        grad_hidden = (grad_active * slope).astype(bf16)
        grad_hidden_ref[here, :] = grad_hidden
        part_refs[row][...] = dot_nt(grad_hidden, weights_ref[:, :D]).astype(bf16)
        totals[0] += row_sum(branch.astype(f32))
        totals[1] += row_sum(grad_out * hat)
        totals[2] += row_sum(grad_out)
        totals[3] += row_sum(grad_hidden.astype(f32))
    for i in range(3):
        sums_ref[i : i + 1, :] = totals[i]
    bias_ref[...] = totals[3]


def attention_back_kernel(layer, *refs):
    base_ref, sums, hat_ref, rate_ref = refs[0], refs[1:5], refs[5], refs[6]
    small_ref, weights_ref, q_ref, k_ref, v_ref, prob_ref = refs[7:13]
    part_refs = refs[13:15]
    carry_ref, branch_ref, grad_proj_ref, sums_ref, bias_ref = refs[15:]
    part = HEADS // 4 * HEAD_DIM
    lane = lax.broadcasted_iota(jnp.int32, (1, part), 1)
    gain = small_at(small_ref, layer, AT_G1)
    totals = [jnp.zeros((1, D), f32) for _ in range(3)] + [jnp.zeros((1, part), f32)]
    for row in range(MICRO):
        here = rows_of(row)
        hat, rate = hat_ref[here, :], rate_ref[here, :1]
        grad_out = base_ref[here, :] + (
            sums[2 * row][...].astype(f32) + sums[2 * row + 1][...].astype(f32)
        )
        grad_out = grad_out.astype(bf16).astype(f32)
        grad = norm_back(grad_out, hat, rate, gain)
        carry_ref[here, :] = grad
        branch = grad.astype(bf16)
        branch_ref[here, :] = branch
        grad_mixed = dot_nn(branch, weights_ref[:, 3 * part :])
        low_mixed = grad_mixed.astype(bf16)
        query, key_rows, values = q_ref[here, :], k_ref[here, :], v_ref[here, :]
        grads = [jnp.zeros((ROW, part), f32) for _ in range(3)]
        for head in range(part // HEAD_DIM):
            inside = (lane >= head * HEAD_DIM) & (lane < (head + 1) * HEAD_DIM)
            prob = prob_ref[row, head]
            head_mixed = jnp.where(inside, grad_mixed, 0.0).astype(bf16)
            grad_prob = dot_nt(head_mixed, values)
            grad_scores = prob * (
                grad_prob - jnp.sum(grad_prob * prob, axis=-1, keepdims=True)
            )
            grad_scores = grad_scores.astype(bf16)
            grad_q = dot_nn(grad_scores, key_rows) * score_scale
            grad_k = dot_tn(grad_scores, query) * score_scale
            grad_v = dot_tn(prob.astype(bf16), low_mixed)
            grads = [
                jnp.where(inside, new, old) for new, old in zip((grad_q, grad_k, grad_v), grads)
            ]
        grad_proj = jnp.concatenate(grads, axis=1).astype(bf16)
        grad_proj_ref[here, :] = grad_proj
        part_refs[row][...] = dot_nt(grad_proj, weights_ref[:, : 3 * part]).astype(bf16)
        totals[0] += row_sum(branch.astype(f32))
        totals[1] += row_sum(grad_out * hat)
        totals[2] += row_sum(grad_out)
        totals[3] += row_sum(grads[2].astype(bf16).astype(f32))
    for i in range(3):
        sums_ref[i : i + 1, :] = totals[i]
    bias_ref[...] = totals[3]


VMEM = pl.BlockSpec(memory_space=pltpu.VMEM)
SMEM = pl.BlockSpec(memory_space=pltpu.SMEM)


def shaped(shape, kind):
    return jax.ShapeDtypeStruct(shape, kind)


def call(body, name, flops, operands, outs):
    specs = [SMEM if a.dtype == jnp.int32 else VMEM for a in operands]
    moved = sum(a.size * a.dtype.itemsize for a in (*operands, *outs))
    return pl.pallas_call(
        body,
        name=name,
        in_specs=specs,
        out_specs=[VMEM] * len(outs),
        out_shape=list(outs),
        cost_estimate=pl.CostEstimate(flops=flops, bytes_accessed=moved, transcendentals=0),
        compiler_params=pltpu.CompilerParams(vmem_limit_bytes=40 * 2**20),
    )(*operands)


part_out = [shaped((ROW, D), bf16)] * 2
rows_out = shaped((TOK, D), bf16)
wide_out = shaped((TOK, D), f32)
rate_out = shaped((TOK, 128), f32)


def heads_part():
    return D // lax.axis_size("section")


def attention(layer, inputs, sums, small, weights, bv, lengths, keep, tag):
    first, part = sums is None, heads_part()
    operands = [inputs] if first else [inputs, *sums, small]
    operands += [weights, bv, lengths]
    outs = list(part_out)
    if not first:
        outs += [rows_out] + ([wide_out, rate_out] if keep else [])
    if keep:
        outs += [shaped((TOK, part), bf16)] * 4
        outs += [shaped((MICRO, part // HEAD_DIM, ROW, ROW), f32)]
    return call(
        partial(attention_kernel, layer, first, keep),
        f"attention_{tag}{layer}",
        2 * TOK * part * (4 * D + 4 * ROW),
        operands,
        outs,
    )


def feed(layer, inputs, sums, small, weights, b1, keep, tag):
    outs = list(part_out) + [rows_out]
    if keep:
        outs += [wide_out, rate_out, wide_out, rows_out]
    return call(
        partial(feed_kernel, layer, keep),
        f"feed_{tag}{layer}",
        4 * TOK * D * D,
        [inputs, *sums, small, weights, b1],
        outs,
    )


def on_device(tokens, key_tokens, cotangent, lengths, query_mats, query_small, key_mats, key_small):
    sections = lax.axis_size("section")
    section = lax.axis_index("section")
    batches = lax.axis_size("batch")
    part = heads_part()
    rows = query_mats.shape[1]

    def own_cols(mats, layer):
        attn = jnp.concatenate(
            [
                lax.dynamic_slice(mats, (layer, 0, j * D + section * part), (1, rows, part))[0]
                for j in range(4)
            ],
            axis=1,
        ).astype(bf16)
        ffn = jnp.concatenate(
            [
                lax.dynamic_slice(
                    mats, (layer, 0, (4 + 4 * j) * D + section * D), (1, rows, D)
                )[0]
                for j in range(2)
            ],
            axis=1,
        ).astype(bf16)
        return attn, ffn

    def own_small(small):
        bv = lax.dynamic_slice(small, (0, section * part), (LAYERS, part))
        b1 = lax.dynamic_slice(small, (0, AT_B1 + section * D), (LAYERS, D))
        return bv, b1

    bv_q, b1_q = own_small(query_small)
    bv_k, b1_k = own_small(key_small)
    attn_q, feed_q = [], []
    for layer in range(LAYERS):
        attn, ffn = own_cols(query_mats, layer)
        attn_q.append(gather_rows(attn))
        feed_q.append(gather_rows(ffn))
    attn_k, feed_k = [], []
    for layer in range(LAYERS):
        attn, ffn = own_cols(key_mats, layer)
        both = gather_rows(jnp.concatenate([attn, ffn], axis=1))
        attn_k.append(both[:, : 4 * part])
        feed_k.append(both[:, 4 * part :])

    kept = []
    inputs, sums = tokens, None
    for layer in range(LAYERS):
        found = attention(
            layer, inputs, sums, query_small, attn_q[layer], bv_q, lengths, True, "q"
        )
        parts, found = found[:2], found[2:]
        if layer > 0:
            inputs, hat, rate = found[:3]
            kept[-1] += (hat, rate)
            found = found[3:]
        sums = sum_parts(*parts)
        attn_in, attn_kept = inputs, tuple(found)
        p0, p1, inputs, hat, rate, hidden, active = feed(
            layer, inputs, sums, query_small, feed_q[layer], b1_q, True, "q"
        )
        sums = sum_parts(p0, p1)
        kept.append((attn_in, attn_kept, hat, rate, inputs, hidden, active))

    inputs_k, sums_k = key_tokens, None
    for layer in range(LAYERS):
        found = attention(
            layer, inputs_k, sums_k, key_small, attn_k[layer], bv_k, lengths, False, "k"
        )
        if layer > 0:
            inputs_k = found[2]
        sums_k = sum_parts(*found[:2])
        p0, p1, inputs_k = feed(
            layer, inputs_k, sums_k, key_small, feed_k[layer], b1_k, False, "k"
        )
        sums_k = sum_parts(p0, p1)
    pooled_k = call(
        partial(last_kernel, LAYERS - 1),
        "last_k",
        2 * TOK * D * 8,
        [inputs_k, *sums_k, key_small, lengths],
        [shaped((MICRO, CROPS, D), f32)],
    )[0]

    grad_feed, grad_attn, small_parts = [None] * LAYERS, [None] * LAYERS, [None] * LAYERS
    sums_out, bias_out = shaped((3, D), f32), shaped((1, D), f32)
    for layer in reversed(range(LAYERS)):
        attn_in, attn_kept, hat1, rate1, feed_in, hidden, active, *rest = kept[layer]
        last = layer == LAYERS - 1
        if last:
            operands = [feed_in, *sums, cotangent, lengths]
        else:
            operands = [carry, *sums, *rest]
        outs = [*part_out, wide_out, rows_out, rows_out, sums_out, bias_out]
        if last:
            outs += [rows_out, shaped((MICRO, CROPS, D), f32)]
        p0, p1, carry, branch, grad_hidden, sums_2, db1, *tail = call(
            partial(feed_back_kernel, layer, last),
            f"feed_back{layer}",
            4 * TOK * D * D,
            [*operands, query_small, feed_q[layer], hidden],
            outs,
        )
        if last:
            out_q, pooled_q = tail
        sums = sum_parts(p0, p1)
        grad_feed[layer] = jnp.concatenate(
            [dot_tn(feed_in, grad_hidden), dot_tn(branch, active)], axis=1
        ).astype(bf16)
        q, k, v, mixed, prob = attn_kept
        p0, p1, carry, branch, grad_proj, sums_1, dbv = call(
            partial(attention_back_kernel, layer),
            f"attention_back{layer}",
            2 * TOK * part * (4 * D + 10 * ROW),
            [carry, *sums, hat1, rate1, query_small, attn_q[layer], q, k, v, prob],
            [
                *part_out,
                wide_out,
                rows_out,
                shaped((TOK, 3 * part), bf16),
                sums_out,
                shaped((1, part), f32),
            ],
        )
        grad_attn[layer] = jnp.concatenate(
            [dot_tn(attn_in, grad_proj), dot_tn(branch, mixed)], axis=1
        ).astype(bf16)
        sums = sum_parts(p0, p1)
        own = section == 0
        vector = jnp.concatenate(
            [
                jnp.zeros((D,), f32),
                jnp.where(own, sums_1.reshape(-1), 0.0),
                jnp.zeros((4 * D,), f32),
                jnp.where(own, sums_2.reshape(-1), 0.0),
            ]
        )
        vector = lax.dynamic_update_slice(vector, dbv[0], (section * part,))
        small_parts[layer] = lax.dynamic_update_slice(vector, db1[0], (AT_B1 + section * D,))

    small_cols = LAYERS * SMALL // D
    chunk = SMALL // batches
    small_rows = jnp.stack(small_parts).reshape(LAYERS, batches, chunk).transpose(1, 0, 2)
    small_rows = small_rows.reshape(D, small_cols)
    small_rows = jnp.pad(small_rows, ((0, 0), (0, 128 - small_cols))).astype(bf16)
    got_feed, got_attn = [None] * LAYERS, [None] * LAYERS
    for layer in reversed(range(LAYERS)):
        got_feed[layer] = gather_section(scatter_rows(grad_feed[layer], rows))
        block = grad_attn[layer]
        if layer == 0:
            block = jnp.concatenate([block, small_rows], axis=1)
        got_attn[layer] = gather_section(scatter_rows(block, rows))

    grad_layers = []
    for layer in range(LAYERS):
        attn = got_attn[layer][:, :, : 4 * part].reshape(sections, rows, 4, part)
        attn = attn.transpose(1, 2, 0, 3).reshape(rows, 4 * D)
        ffn = got_feed[layer].reshape(sections, rows, 2, D).transpose(1, 2, 0, 3)
        grad_layers.append(jnp.concatenate([attn, ffn.reshape(rows, 8 * D)], axis=1))
    grad_mats = jnp.stack(grad_layers).astype(f32)
    small_sum = jnp.sum(got_attn[0][:, :, 4 * part : 4 * part + small_cols].astype(f32), axis=0)
    grad_small = small_sum.reshape(LAYERS, chunk)

    def own_part(block):
        return lax.dynamic_slice_in_dim(block, section * part, part, block.ndim - 1)

    total = jnp.concatenate([add_f32(sums[0], sums[1]), add_f32(sums[2], sums[3])], axis=0)
    input_grad = own_part((carry + total).astype(bf16))
    return (
        own_part(out_q),
        own_part(pooled_q),
        own_part(pooled_k),
        input_grad,
        grad_mats,
        grad_small,
        (query_mats - key_mats) * (1.0 - keep_rate),
        (query_small - key_small) * (1.0 - keep_rate),
    )


def add_f32(left, right):
    return left.astype(f32) + right.astype(f32)


def solution(mesh):
    in_specs = (
        P("batch", None),
        P("batch", None),
        P("batch", None),
        P("batch", None),
        P(None, "batch", None),
        P(),
        P(None, "batch", None),
        P(),
    )
    out_specs = (
        P("batch", "section"),
        P("batch", None, "section"),
        P("batch", None, "section"),
        P("batch", "section"),
        P(None, "batch", None),
        P(None, "batch"),
        P(None, "batch", None),
        P(),
    )
    return jax.shard_map(
        on_device, mesh=mesh, in_specs=in_specs, out_specs=out_specs, check_vma=False
    )
```

time: 1350 us -> 592 us (0.44)
  waiting for transfers between devices: 546 us -> 213 us
  matrix products: 256 us -> 7.3 us
  local copies, waits for them, and re-layouts: 245 us -> 110 us
  loops' own time: 81 us -> 0 us
  starting transfers between devices: 51.5 us -> 105 us
  Pallas kernels: 0 us -> 48.2 us
  other arithmetic: 129 us -> 100 us
    all_gather x2 -> x0, waiting for transfers between devices: 249 us -> none  [the longest x1 130 us: on_device(): lax.all_gather(take(key_mats), 'batch', axis=0, tiled=True)]
    dot_general x87 -> x8, matrix products: 205 us -> 7.3 us  [dot_tn(): lax.dot_general(left, right, (((0,), (0,)), ((), ())), preferred_element_...]
    another operation x152 -> x7, local copies, waits for them, and re-layouts: 154 us -> 4.41 us
    ppermute x12 -> x100, waiting for transfers between devices: 69.8 us -> 213 us  [the longest x30 152 us: shift_z(): lax.ppermute(block, 'batch', [(i, (i + 2 * distance) % count) for i in ra...]
    psum x1 -> x0, waiting for transfers between devices: 128 us -> none  [spread_2(): return lax.psum(kept, axis)]
    unnamed x10 -> x0, loops' own time: 81 us -> none
    reduce_scatter x1 -> x0, waiting for transfers between devices: 77.7 us -> none  [on_device(): lax.psum_scatter(grad_weights.astype(jnp.bfloat16), 'batch', scatter_dime...]
    concatenate x5 -> x6, other arithmetic: 61.7 us -> 3.23 us  [the longest x2 1.47 us: own_cols(): jnp.concatenate([lax.dynamic_slice(mats, (layer, 0, (4 + 4 * j) * D + sec...]
  transfers between devices with their start and end apart: 17 -> 100, of which waited for: 15 -> 39; matrix products, arithmetic and copies ran while one was open for 6% -> 27% of each run, Pallas kernels for 0% -> 8%
where the time goes in v1:
time: 592 us; the launch traced here: 586 us
  waiting for transfers between devices  213 us (36%)
  local copies, waits for them, and re-layouts  110 us (19%)
  starting transfers between devices  105 us (18%)
  other arithmetic  100 us (17%)
  Pallas kernels  48.2 us (8%)
  matrix products  7.3 us (1%)
    ppermute x30, waiting for transfers between devices, shift_z(): lax.ppermute(block, 'batch', [(i, (i + 2 * distance) % count) for i in ra...  152 us
    pallas_call x13, Pallas kernels, call(): pl.pallas_call(body, name=name, in_specs=specs, out_specs=[VMEM] * len(ou...  48.2 us
    unnamed x232, local copies, waits for them, and re-layouts  39.6 us
    ppermute x30, starting transfers between devices, shift_z(): lax.ppermute(block, 'batch', [(i, (i + 2 * distance) % count) for i in ra...  34.7 us
    ppermute x24, starting transfers between devices, swap_y(): return lax.ppermute(block, 'section', [(0, 2), (2, 0), (1, 3), (3, 1)])  33.1 us
    ppermute x24, waiting for transfers between devices, swap_y(): return lax.ppermute(block, 'section', [(0, 2), (2, 0), (1, 3), (3, 1)])  32 us
    ppermute x24, starting transfers between devices, swap_x(): return lax.ppermute(block, 'section', [(0, 1), (1, 0), (2, 3), (3, 2)])  22.1 us
    convert_element_type x28, other arithmetic, add_low(): return (left.astype(f32) + right.astype(f32)).astype(bf16)  21.8 us
  transfers between devices with their start and end apart: 100, of which 39 were waited for; matrix products, arithmetic and copies ran while one was open for 27% of the time, Pallas kernels for 8%

profile of v1, /device:TPU:8, one launch (start us, length us, event | category | flops | bytes accessed | tf_op | source)
XLA Modules:
  0.0 585.7 jit_solution(16141442369484494801)
XLA Ops:
  21.1 16.2 %collective-permute-done.2 = bf16[96,768]{1,0:T(8,128)(2,1)S(1)} collective-permute-done((bf16[96,768]{1,0:T(8,128)(2,1)S(1)}, bf16[96,768]{1,0:T(8,128)(2,1)S(1)}, u32[]{:S(2)}, u32[]{:S(2)}) %collective-permute-start.2) | collective-permute-done | bytes 147488 | tf_op jit(solution)/shard_map/ppermute | solution.py:53
  39.9 15.1 %collective-permute-done.17 = bf16[96,768]{1,0:T(8,128)(2,1)S(1)} collective-permute-done((bf16[96,768]{1,0:T(8,128)(2,1)}, bf16[96,768]{1,0:T(8,128)(2,1)S(1)}, u32[]{:S(2)}, u32[]{:S(2)}) %collective-permute-start.17) | collective-permute-done | bytes 147488 | tf_op jit(solution)/shard_map/ppermute | solution.py:53
  67.2 6.1 %collective-permute-done.24 = bf16[96,1536]{1,0:T(8,128)(2,1)S(1)} collective-permute-done((bf16[96,1536]{1,0:T(8,128)(2,1)S(1)}, bf16[96,1536]{1,0:T(8,128)(2,1)S(1)}, u32[]{:S(2)}, u32[]{:S(2)}) %collective-permute-start.24) | collective-permute-done | bytes 294944 | tf_op jit(solution)/shard_map/ppermute | solution.py:53
  73.2 8.2 %collective-permute-done.25 = bf16[96,1536]{1,0:T(8,128)(2,1)S(1)} collective-permute-done((bf16[96,1536]{1,0:T(8,128)(2,1)S(1)}, bf16[96,1536]{1,0:T(8,128)(2,1)S(1)}, u32[]{:S(2)}, u32[]{:S(2)}) %collective-permute-start.25) | collective-permute-done | bytes 294944 | tf_op jit(solution)/shard_map/ppermute | solution.py:53
  81.5 20.6 %collective-permute-done.26 = bf16[96,1536]{1,0:T(8,128)(2,1)S(1)} collective-permute-done((bf16[96,1536]{1,0:T(8,128)(2,1)S(1)}, bf16[96,1536]{1,0:T(8,128)(2,1)S(1)}, u32[]{:S(2)}, u32[]{:S(2)}) %collective-permute-start.26) | collective-permute-done | bytes 294944 | tf_op jit(solution)/shard_map/ppermute | solution.py:53
  104.4 5.6 collective-permute-done.32
  112.5 7.0 %collective-permute-done.33 = bf16[96,2304]{1,0:T(8,128)(2,1)S(1)} collective-permute-done((bf16[96,2304]{1,0:T(8,128)(2,1)S(1)}, bf16[96,2304]{1,0:T(8,128)(2,1)S(1)}, u32[]{:S(2)}, u32[]{:S(2)}) %collective-permute-start.33) | collective-permute-done | bytes 442400 | tf_op jit(solution)/shard_map/ppermute | solution.py:53
  122.9 17.1 %collective-permute-done.34 = bf16[96,2304]{1,0:T(8,128)(2,1)S(1)} collective-permute-done((bf16[96,2304]{1,0:T(8,128)(2,1)S(1)}, bf16[96,2304]{1,0:T(8,128)(2,1)S(1)}, u32[]{:S(2)}, u32[]{:S(2)}) %collective-permute-start.34) | collective-permute-done | bytes 442400 | tf_op jit(solution)/shard_map/ppermute | solution.py:53
  195.5 8.6 %collective-permute-done.14 = bf16[256,768]{1,0:T(8,128)(2,1)S(1)} collective-permute-done((bf16[256,768]{1,0:T(8,128)(2,1)S(1)}, bf16[256,768]{1,0:T(8,128)(2,1)S(1)}, u32[]{:S(2)}, u32[]{:S(2)}) %collective-permute-start.14) | collective-permute-done | bytes 393248 | tf_op jit(solution)/shard_map/ppermute | solution.py:43
  210.8 4.8 gather_fusion.6
  215.6 5.6 maximum_select_fusion.1
  221.2 4.7 gather_fusion.7
  225.9 5.6 broadcast_select_fusion
  237.2 9.3 %subtract_multiply_fusion = f32[2,96,9216]{2,1,0:T(8,128)} fusion(f32[2,96,9216]{2,1,0:T(8,128)} %param.20, f32[2,96,9216]{2,1,0:T(8,128)} %param.22), kind=kLoop, calls=%fused_computation.10 | loop fusion | flops 3538944 | bytes 21233664 | tf_op jit(solution)/shard_map/mul | solution.py:610
  261.6 7.7 %collective-permute-done.22 = bf16[256,768]{1,0:T(8,128)(2,1)S(1)} collective-permute-done((bf16[256,768]{1,0:T(8,128)(2,1)S(1)}, bf16[256,768]{1,0:T(8,128)(2,1)S(1)}, u32[]{:S(2)}, u32[]{:S(2)}) %collective-permute-start.22) | collective-permute-done | bytes 393248 | tf_op jit(solution)/shard_map/ppermute | solution.py:43
  272.2 5.8 collective-permute-done.39.refs_4_
  300.7 5.3 collective-permute-done.30
  365.4 6.9 %attention_back1.1 = (bf16[256,768]{1,0:T(8,128)(2,1)}, bf16[256,768]{1,0:T(8,128)(2,1)}, f32[512,768]{1,0:T(8,128)S(1)}, bf16[512,768]{1,0:T(8,128)(2,1)S(1)}, ...) custom-call(f32[512,768]{1,0:T(8,128)S(1)} %copy-done.32, ...), custom_call_target="tpu_custom_call" | custom-call | flops 1107296256 | bytes 12136192 | tf_op jit(solution)/shard_map/attention_back1/pallas_call | solution.py:382
  397.1 15.0 %collective-permute-done.95 = bf16[96,1536]{1,0:T(8,128)(2,1)S(1)} collective-permute-done((bf16[96,1536]{1,0:T(8,128)(2,1)S(1)}, bf16[96,1536]{1,0:T(8,128)(2,1)S(1)}, u32[]{:S(2)}, u32[]{:S(2)}) %collective-permute-start.95) | collective-permute-done | bytes 294944 | tf_op jit(solution)/shard_map/ppermute | solution.py:53
  412.4 6.9 %collective-permute-done.96 = bf16[96,1536]{1,0:T(8,128)(2,1)S(1)} collective-permute-done((bf16[96,1536]{1,0:T(8,128)(2,1)S(1)}, bf16[96,1536]{1,0:T(8,128)(2,1)S(1)}, u32[]{:S(2)}, u32[]{:S(2)}) %collective-permute-start.96) | collective-permute-done | bytes 294944 | tf_op jit(solution)/shard_map/ppermute | solution.py:53
  426.0 6.3 %collective-permute-done.88 = bf16[96,768]{1,0:T(8,128)(2,1)S(1)} collective-permute-done((bf16[96,768]{1,0:T(8,128)(2,1)S(1)}, bf16[96,768]{1,0:T(8,128)(2,1)S(1)}, u32[]{:S(2)}, u32[]{:S(2)}) %collective-permute-start.88) | collective-permute-done | bytes 147488 | tf_op jit(solution)/shard_map/ppermute | solution.py:53
  479.8 4.8 attention_back0.1
  508.1 11.8 %collective-permute-start.69 = (bf16[256,768]{1,0:T(8,128)(2,1)S(1)}, bf16[256,768]{1,0:T(8,128)(2,1)S(1)}, u32[]{:S(2)}, u32[]{:S(2)}) collective-permute-start(bf16[256,768]{1,0:T(8,128)(2,1)S(1)} %add_convert_fusion.1), channel_id=1, source_target_pairs={{0,16},{16,0},{8,24},{24,8},{1,17},{17,1},{9,25},{25,9},{2,18},{18... | collective-permute-start | bytes 1179656 | tf_op jit(solution)/shard_map/ppermute | solution.py:43
  531.2 5.0 collective-permute-done.73
  (581 shorter events, 373.3 us)
Async XLA Ops:
  5.0 32.3 %collective-permute-start.2 = (bf16[96,768]{1,0:T(8,128)(2,1)S(1)}, bf16[96,768]{1,0:T(8,128)(2,1)S(1)}, u32[]{:S(2)}, u32[]{:S(2)}) collective-permute-start(bf16[96,768]{1,0:T(8,128)(2,1)S(1)} %pad_maximum_fusion.12), channel_id=1, source_target_pairs={{0,6},{1,7},{2,0},{3,1},{4,2},{5,3},{6,4},{7,5},{8,14},{9,15},{10,... | collective-permute-start | bytes 442376 | tf_op jit(solution)/shard_map/ppermute | solution.py:53
  9.0 51.4 %collective-permute-start.8 = (bf16[96,1536]{1,0:T(8,128)(2,1)}, bf16[96,1536]{1,0:T(8,128)(2,1)S(1)}, u32[]{:S(2)}, u32[]{:S(2)}) collective-permute-start(bf16[96,1536]{1,0:T(8,128)(2,1)} %pad_maximum_fusion.10), channel_id=1, source_target_pairs={{0,2},{1,3},{2,4},{3,5},{4,6},{5,7},{6,0},{7,1},{8,10},{9,11},{10,... | collective-permute-start | bytes 884744 | tf_op jit(solution)/shard_map/ppermute | solution.py:53
  17.4 45.0 %collective-permute-start.9 = (bf16[96,1536]{1,0:T(8,128)(2,1)}, bf16[96,1536]{1,0:T(8,128)(2,1)S(1)}, u32[]{:S(2)}, u32[]{:S(2)}) collective-permute-start(bf16[96,1536]{1,0:T(8,128)(2,1)} %pad_maximum_fusion.10), channel_id=1, source_target_pairs={{0,4},{1,5},{2,6},{3,7},{4,0},{5,1},{6,2},{7,3},{8,12},{9,13},{10,... | collective-permute-start | bytes 884744 | tf_op jit(solution)/shard_map/ppermute | solution.py:53
  21.0 34.1 %collective-permute-start.17 = (bf16[96,768]{1,0:T(8,128)(2,1)}, bf16[96,768]{1,0:T(8,128)(2,1)S(1)}, u32[]{:S(2)}, u32[]{:S(2)}) collective-permute-start(bf16[96,768]{1,0:T(8,128)(2,1)} %pad_maximum_fusion.13), channel_id=1, source_target_pairs={{0,4},{1,5},{2,6},{3,7},{4,0},{5,1},{6,2},{7,3},{8,12},{9,13},{10,... | collective-permute-start | bytes 442376 | tf_op jit(solution)/shard_map/ppermute | solution.py:53
  60.5 41.6 %collective-permute-start.26 = (bf16[96,1536]{1,0:T(8,128)(2,1)S(1)}, bf16[96,1536]{1,0:T(8,128)(2,1)S(1)}, u32[]{:S(2)}, u32[]{:S(2)}) collective-permute-start(bf16[96,1536]{1,0:T(8,128)(2,1)S(1)} %copy-done.109), channel_id=1, source_target_pairs={{0,6},{1,7},{2,0},{3,1},{4,2},{5,3},{6,4},{7,5},{8,14},{9,15},{10,... | collective-permute-start | bytes 884744 | tf_op jit(solution)/shard_map/ppermute | solution.py:53
  62.5 47.5 %collective-permute-start.32 = (bf16[96,2304]{1,0:T(8,128)(2,1)S(1)}, bf16[96,2304]{1,0:T(8,128)(2,1)S(1)}, u32[]{:S(2)}, u32[]{:S(2)}) collective-permute-start(bf16[96,2304]{1,0:T(8,128)(2,1)S(1)} %concatenate.128), channel_id=1, source_target_pairs={{0,2},{1,3},{2,4},{3,5},{4,6},{5,7},{6,0},{7,1},{8,10},{9,11},{10,... | collective-permute-start | bytes 1327112 | tf_op jit(solution)/shard_map/ppermute | solution.py:53
  62.6 56.9 %collective-permute-start.33 = (bf16[96,2304]{1,0:T(8,128)(2,1)S(1)}, bf16[96,2304]{1,0:T(8,128)(2,1)S(1)}, u32[]{:S(2)}, u32[]{:S(2)}) collective-permute-start(bf16[96,2304]{1,0:T(8,128)(2,1)S(1)} %concatenate.128), channel_id=1, source_target_pairs={{0,4},{1,5},{2,6},{3,7},{4,0},{5,1},{6,2},{7,3},{8,12},{9,13},{10,... | collective-permute-start | bytes 1327112 | tf_op jit(solution)/shard_map/ppermute | solution.py:53
  73.2 66.7 %collective-permute-start.34 = (bf16[96,2304]{1,0:T(8,128)(2,1)S(1)}, bf16[96,2304]{1,0:T(8,128)(2,1)S(1)}, u32[]{:S(2)}, u32[]{:S(2)}) collective-permute-start(bf16[96,2304]{1,0:T(8,128)(2,1)S(1)} %concatenate.128), channel_id=1, source_target_pairs={{0,6},{1,7},{2,0},{3,1},{4,2},{5,3},{6,4},{7,5},{8,14},{9,15},{10,... | collective-permute-start | bytes 1327112 | tf_op jit(solution)/shard_map/ppermute | solution.py:53
  81.5 60.7 %collective-permute-start.3 = (bf16[4,96,768]{2,1,0:T(8,128)(2,1)S(1)}, bf16[4,96,768]{2,1,0:T(8,128)(2,1)S(1)}, u32[]{:S(2)}, u32[]{:S(2)}) collective-permute-start(bf16[4,96,768]{2,1,0:T(8,128)(2,1)S(1)} %pad_maximum_fusion.7), channel_id=1, source_target_pairs={{0,1},{1,0},{2,3},{3,2},{4,5},{5,4},{6,7},{7,6},{8,9},{9,8},{10,11... | collective-permute-start | bytes 1769480 | tf_op jit(solution)/shard_map/ppermute | solution.py:48
  102.1 40.4 %collective-permute-start.19 = (bf16[4,96,768]{2,1,0:T(8,128)(2,1)S(1)}, bf16[4,96,768]{2,1,0:T(8,128)(2,1)S(1)}, u32[]{:S(2)}, u32[]{:S(2)}) collective-permute-start(bf16[4,96,768]{2,1,0:T(8,128)(2,1)S(1)} %pad_maximum_fusion.8), channel_id=1, source_target_pairs={{0,1},{1,0},{2,3},{3,2},{4,5},{5,4},{6,7},{7,6},{8,9},{9,8},{10,11... | collective-permute-start | bytes 1769480 | tf_op jit(solution)/shard_map/ppermute | solution.py:48
  110.0 42.6 %collective-permute-start.44 = (bf16[96,2304]{1,0:T(8,128)(2,1)}, bf16[96,2304]{1,0:T(8,128)(2,1)}, u32[]{:S(2)}, u32[]{:S(2)}) collective-permute-start(bf16[96,2304]{1,0:T(8,128)(2,1)} %concatenate.129), channel_id=1, source_target_pairs={{0,2},{1,3},{2,4},{3,5},{4,6},{5,7},{6,0},{7,1},{8,10},{9,11},{10,... | collective-permute-start | bytes 1327112 | tf_op jit(solution)/shard_map/ppermute | solution.py:53
  119.5 36.3 %collective-permute-start.45 = (bf16[96,2304]{1,0:T(8,128)(2,1)}, bf16[96,2304]{1,0:T(8,128)(2,1)}, u32[]{:S(2)}, u32[]{:S(2)}) collective-permute-start(bf16[96,2304]{1,0:T(8,128)(2,1)} %concatenate.129), channel_id=1, source_target_pairs={{0,4},{1,5},{2,6},{3,7},{4,0},{5,1},{6,2},{7,3},{8,12},{9,13},{10,... | collective-permute-start | bytes 1327112 | tf_op jit(solution)/shard_map/ppermute | solution.py:53
  142.2 30.2 %collective-permute-start.11 = (bf16[4,96,1536]{2,1,0:T(8,128)(2,1)}, bf16[4,96,1536]{2,1,0:T(8,128)(2,1)}, u32[]{:S(2)}, u32[]{:S(2)}) collective-permute-start(bf16[4,96,1536]{2,1,0:T(8,128)(2,1)} %pad_maximum_fusion.2), channel_id=1, source_target_pairs={{0,1},{1,0},{2,3},{3,2},{4,5},{5,4},{6,7},{7,6},{8,9},{9,8},{10,11... | collective-permute-start | bytes 3538952 | tf_op jit(solution)/shard_map/ppermute | solution.py:48
  142.4 35.9 %collective-permute-start.27 = (bf16[4,96,1536]{2,1,0:T(8,128)(2,1)}, bf16[4,96,1536]{2,1,0:T(8,128)(2,1)}, u32[]{:S(2)}, u32[]{:S(2)}) collective-permute-start(bf16[4,96,1536]{2,1,0:T(8,128)(2,1)} %pad_maximum_fusion.3), channel_id=1, source_target_pairs={{0,1},{1,0},{2,3},{3,2},{4,5},{5,4},{6,7},{7,6},{8,9},{9,8},{10,11... | collective-permute-start | bytes 3538952 | tf_op jit(solution)/shard_map/ppermute | solution.py:48
  152.6 54.3 %collective-permute-start.35 = (bf16[4,96,2304]{2,1,0:T(8,128)(2,1)}, bf16[4,96,2304]{2,1,0:T(8,128)(2,1)}, u32[]{:S(2)}, u32[]{:S(2)}) collective-permute-start(bf16[4,96,2304]{2,1,0:T(8,128)(2,1)} %get-tuple-element.207), channel_id=1, source_target_pairs={{0,1},{1,0},{2,3},{3,2},{4,5},{5,4},{6,7},{7,6},{8,9},{9,8},{10,11... | collective-permute-start | bytes 5308424 | tf_op jit(solution)/shard_map/ppermute | solution.py:48
  165.2 50.4 %collective-permute-start.47 = (bf16[4,96,2304]{2,1,0:T(8,128)(2,1)}, bf16[4,96,2304]{2,1,0:T(8,128)(2,1)}, u32[]{:S(2)}, u32[]{:S(2)}) collective-permute-start(bf16[4,96,2304]{2,1,0:T(8,128)(2,1)} %get-tuple-element.205), channel_id=1, source_target_pairs={{0,1},{1,0},{2,3},{3,2},{4,5},{5,4},{6,7},{7,6},{8,9},{9,8},{10,11... | collective-permute-start | bytes 5308424 | tf_op jit(solution)/shard_map/ppermute | solution.py:48
  204.9 43.3 %collective-permute-start.15 = (bf16[256,768]{1,0:T(8,128)(2,1)}, bf16[256,768]{1,0:T(8,128)(2,1)}, u32[]{:S(2)}, u32[]{:S(2)}) collective-permute-start(bf16[256,768]{1,0:T(8,128)(2,1)} %add_convert_fusion.20.refs_3_), channel_id=1, source_target_pairs={{0,8},{8,0},{16,24},{24,16},{1,9},{9,1},{17,25},{25,17},{2,10},{10... | collective-permute-start | bytes 1179656 | tf_op jit(solution)/shard_map/ppermute | solution.py:39
  206.3 41.9 %collective-permute-start.13 = (bf16[256,768]{1,0:T(8,128)(2,1)}, bf16[256,768]{1,0:T(8,128)(2,1)}, u32[]{:S(2)}, u32[]{:S(2)}) collective-permute-start(bf16[256,768]{1,0:T(8,128)(2,1)} %add_convert_fusion.21.refs_1_), channel_id=1, source_target_pairs={{0,16},{16,0},{8,24},{24,8},{1,17},{17,1},{9,25},{25,9},{2,18},{18... | collective-permute-start | bytes 1179656 | tf_op jit(solution)/shard_map/ppermute | solution.py:43
  345.8 37.4 %collective-permute-start.93 = (bf16[4,96,1536]{2,1,0:T(8,128)(2,1)}, bf16[4,96,1536]{2,1,0:T(8,128)(2,1)}, u32[]{:S(2)}, u32[]{:S(2)}) collective-permute-start(bf16[4,96,1536]{2,1,0:T(8,128)(2,1)} %fusion.7), channel_id=1, source_target_pairs={{0,1},{1,0},{2,3},{3,2},{4,5},{5,4},{6,7},{7,6},{8,9},{9,8},{10,11... | collective-permute-start | bytes 3538952 | tf_op jit(solution)/shard_map/ppermute | solution.py:48
  381.0 38.3 %collective-permute-start.55 = (bf16[256,768]{1,0:T(8,128)(2,1)S(1)}, bf16[256,768]{1,0:T(8,128)(2,1)S(1)}, u32[]{:S(2)}, u32[]{:S(2)}) collective-permute-start(bf16[256,768]{1,0:T(8,128)(2,1)S(1)} %add_convert_fusion.8.refs_2_), channel_id=1, source_target_pairs={{0,8},{8,0},{16,24},{24,16},{1,9},{9,1},{17,25},{25,17},{2,10},{10... | collective-permute-start | bytes 1179656 | tf_op jit(solution)/shard_map/ppermute | solution.py:39
  383.1 36.2 %collective-permute-start.53 = (bf16[256,768]{1,0:T(8,128)(2,1)S(1)}, bf16[256,768]{1,0:T(8,128)(2,1)S(1)}, u32[]{:S(2)}, u32[]{:S(2)}) collective-permute-start(bf16[256,768]{1,0:T(8,128)(2,1)S(1)} %add_convert_fusion.9.refs_0_), channel_id=1, source_target_pairs={{0,16},{16,0},{8,24},{24,8},{1,17},{17,1},{9,25},{25,9},{2,18},{18... | collective-permute-start | bytes 1179656 | tf_op jit(solution)/shard_map/ppermute | solution.py:43
  396.5 39.5 %collective-permute-start.63 = (bf16[256,768]{1,0:T(8,128)(2,1)S(1)}, bf16[256,768]{1,0:T(8,128)(2,1)S(1)}, u32[]{:S(2)}, u32[]{:S(2)}) collective-permute-start(bf16[256,768]{1,0:T(8,128)(2,1)S(1)} %add_convert_fusion.4.refs_3_), channel_id=1, source_target_pairs={{0,8},{8,0},{16,24},{24,16},{1,9},{9,1},{17,25},{25,17},{2,10},{10... | collective-permute-start | bytes 1179656 | tf_op jit(solution)/shard_map/ppermute | solution.py:39
  457.5 38.7 %collective-permute-start.79 = (bf16[4,96,1536]{2,1,0:T(8,128)(2,1)}, bf16[4,96,1536]{2,1,0:T(8,128)(2,1)}, u32[]{:S(2)}, u32[]{:S(2)}) collective-permute-start(bf16[4,96,1536]{2,1,0:T(8,128)(2,1)} %fusion.11), channel_id=1, source_target_pairs={{0,1},{1,0},{2,3},{3,2},{4,5},{5,4},{6,7},{7,6},{8,9},{9,8},{10,11... | collective-permute-start | bytes 3538952 | tf_op jit(solution)/shard_map/ppermute | solution.py:48
  493.1 35.5 %collective-permute-start.72 = (bf16[4,96,896]{2,1,0:T(8,128)(2,1)S(1)}, bf16[4,96,896]{2,1,0:T(8,128)(2,1)S(1)}, u32[]{:S(2)}, u32[]{:S(2)}) collective-permute-start(bf16[4,96,896]{2,1,0:T(8,128)(2,1)S(1)} %dynamic-slice_bitcast_fusion), channel_id=1, source_target_pairs={{0,1},{1,0},{2,3},{3,2},{4,5},{5,4},{6,7},{7,6},{8,9},{9,8},{10,11... | collective-permute-start | bytes 2064392 | tf_op jit(solution)/shard_map/ppermute | solution.py:48
  (191 other events, 2478.6 us)

commit v2 on v1

v2 whole, which is shorter than its diff:
```python
from functools import partial

import jax
import jax.numpy as jnp
from jax import lax
from jax.experimental import pallas as pl
from jax.experimental.pallas import tpu as pltpu
from jax.sharding import PartitionSpec as P

HEADS = 12
HEAD_DIM = 64
D = 768
LAYERS = 2
MICRO = 2
ROW = 256
CROPS = 4
TOK = MICRO * ROW
SMALL = 11 * D

epsilon = 1e-05
keep_rate = 0.9995
score_scale = HEAD_DIM ** (-0.5)
bf16 = jnp.bfloat16
f32 = jnp.float32

AT_BV, AT_BO, AT_G1, AT_S1, AT_B1, AT_B2, AT_G2, AT_S2 = (
    0,
    D,
    2 * D,
    3 * D,
    4 * D,
    8 * D,
    9 * D,
    10 * D,
)


def swap_x(block):
    return lax.ppermute(block, "section", [(0, 1), (1, 0), (2, 3), (3, 2)])


def swap_y(block):
    return lax.ppermute(block, "section", [(0, 2), (2, 0), (1, 3), (3, 1)])


def swap_core(block):
    count = lax.axis_size("batch")
    return lax.ppermute(block, "batch", [(i, i ^ 1) for i in range(count)])


def shift_z(block, distance):
    count = lax.axis_size("batch")
    return lax.ppermute(block, "batch", [(i, (i + 2 * distance) % count) for i in range(count)])


def put_after(value, *others):
    return lax.optimization_barrier((value, *others))[0] if others else value


def sum_parts(name, part_0, part_1, beside=None, begun=(), later=()):
    with jax.named_scope(f"sum_{name}_first"):
        here_0, here_1 = swap_x(part_0), swap_y(put_after(part_1, *begun))
    with jax.named_scope(f"sum_{name}_second"):
        half_0, half_1 = add_parts(part_0, here_0), add_parts(part_1, here_1, later)
        there_0, there_1 = swap_y(half_0), swap_x(half_1)
    done = beside((half_0, half_1)) if beside is not None else ()
    return (half_0, there_0, half_1, there_1), done


def sum_own_cols(name, place, sent, kept):
    wide = kept.shape[1] // 2
    with jax.named_scope(f"sum_{name}"):
        came = swap_y(sent)
        sent, kept = call(
            half_kernel, "own_half", [place, kept, came], [shaped((TOK, wide), bf16)] * 2
        )
        return kept, swap_x(sent)


def sum_in_steps(name, part_0, part_1):
    with jax.named_scope(f"sum_{name}_first"):
        here_0, here_1 = swap_x(part_0), swap_y(part_1)
    after = yield (part_0,)
    with jax.named_scope(f"sum_{name}_second"):
        half_0 = add_parts(part_0, here_0, after)
        half_1 = add_parts(part_1, here_1, after)
        sums = (half_0, swap_y(half_0), half_1, swap_x(half_1))
    after = yield (half_0, half_1)
    return sums, after


def pass_z(block, step, first=0):
    count = lax.axis_size("batch")
    last = count // 2 - 1
    sources = range(first, last) if step > 0 else range(1, last + 1 - first)
    pairs = [(2 * z + c, 2 * (z + step) + c) for z in sources for c in range(2)]
    return lax.ppermute(block, "batch", pairs)


def pass_ends(block):
    pairs = [(2 * z + c, 2 * t + c) for z, t in ((2, 3), (1, 0)) for c in range(2)]
    return lax.ppermute(block, "batch", pairs)


def gather_rows(place, block, at_once=False, then=(), onward=()):
    places = lax.axis_size("batch") // 2
    apart = block.shape[0] % 16 == 0
    if places == 4 and apart and not at_once:
        left, right = pass_z(block, 1), pass_z(block, -1)
        left_2 = pass_z(put_after(left, *onward), 1, 1)
        right_2 = pass_z(put_after(right, *onward), -1, 1)
        second = call(
            second_kernel, "second", [place, left_2, right_2], [shaped(block.shape, bf16)]
        )[0]
        own, kind = [block, left, right, second, pass_ends(second)], "line"
    else:
        own, kind = [block] + [shift_z(block, d) for d in range(1, places)], "circle"
    other = [swap_core(put_after(chunk, *then)) for chunk in own]
    if apart:
        return own + other, kind
    me = lax.axis_index("batch")
    z, core = me // 2, me % 2
    pair = jnp.stack([jnp.stack(own), jnp.stack(other)], 1)
    pair = jnp.where(core == 0, pair, pair[:, ::-1])
    whole = jnp.take(pair, (z - jnp.arange(places)) % places, axis=0)
    return [whole.reshape(places * 2 * block.shape[0], block.shape[1])], "whole"


def landed(found):
    chunks, kind = found
    if kind == "whole":
        return ()
    return tuple(chunks[1:] if kind == "circle" else chunks[4:5])


def steps_of(found):
    chunks, kind = found
    return [(chunks[i],) for i in (1, 3, 4)] if kind == "line" else [(), (), ()]


def gather_section(block, in_turn=False, after=()):
    count = lax.axis_size("section")
    found = [block]
    for k in range(1, count):
        if in_turn:
            after = (*after, *found[1:][-1:])
        pairs = [(i, i ^ k) for i in range(count)]
        found.append(lax.ppermute(put_after(block, *after), "section", pairs))
    return found


def dot_nn(left, right):
    return jnp.dot(left, right, preferred_element_type=f32)


def dot_nt(left, right):
    return lax.dot_general(left, right, (((1,), (1,)), ((), ())), preferred_element_type=f32)


def dot_tn(left, right):
    return lax.dot_general(left, right, (((0,), (0,)), ((), ())), preferred_element_type=f32)


def add_low(left, right):
    return (left.astype(f32) + right.astype(f32)).astype(bf16)


def ends_of(lens_ref, row):
    ends, total = [], 0
    for c in range(CROPS):
        total = total + lens_ref[row, c]
        ends.append(total)
    return ends


def segments(ends, shape, dim):
    position = lax.broadcasted_iota(jnp.int32, shape, dim)
    segment = jnp.zeros(shape, jnp.int32)
    for end in ends:
        segment = segment + (position >= end).astype(jnp.int32)
    return position, segment


def allowed_of(lens_ref, row):
    ends = ends_of(lens_ref, row)
    pos_q, seg_q = segments(ends, (ROW, 1), 0)
    pos_k, seg_k = segments(ends, (1, ROW), 1)
    seg_k = jnp.where(pos_k < ends[-1], seg_k, -1)
    return (seg_q == seg_k) | (pos_q == pos_k)


def pooled_of(lens_ref, row, values):
    ends = ends_of(lens_ref, row)
    pos, seg = segments(ends, (1, ROW), 1)
    crop = lax.broadcasted_iota(jnp.int32, (8, 1), 0)
    seg = jnp.where(pos < ends[-1], seg, -1)
    member = (seg == crop).astype(f32).astype(bf16)
    counts = jnp.ones((8, 1), f32)
    for c in range(CROPS):
        counts = jnp.where(crop == c, jnp.maximum(lens_ref[row, c], 1).astype(f32), counts)
    return (dot_nn(member, values) / counts)[:CROPS]


def standard(summed):
    centre = summed - jnp.mean(summed, axis=-1, keepdims=True)
    spread = jnp.mean(centre * centre, axis=-1, keepdims=True)
    rate = lax.rsqrt(spread + epsilon)
    return centre * rate, rate


def small_at(small_ref, layer, offset, width=D):
    return small_ref[layer : layer + 1, offset : offset + width]


def own_cols(block, section, part):
    value = block[:, :part]
    for k in range(1, block.shape[1] // part):
        value = jnp.where(section == k, block[:, k * part : (k + 1) * part], value)
    return value


def rows_of(row):
    return slice(row * ROW, (row + 1) * ROW)


def norm_in(layer, gain_at, shift_at, bias_at, base_ref, sums, small_ref, row):
    half, other = sums[2 * row], sums[2 * row + 1]
    branch = half[...].astype(f32) + other[...].astype(f32) + small_at(small_ref, layer, bias_at)
    hat, rate = standard(base_ref[rows_of(row), :].astype(f32) + branch)
    out = hat * small_at(small_ref, layer, gain_at) + small_at(small_ref, layer, shift_at)
    return out.astype(bf16), hat, rate


def add_kernel(left_ref, right_ref, out_ref):
    out_ref[...] = add_low(left_ref[...], right_ref[...])


def take_kernel(units, place_ref, query_ref, key_ref, *refs):
    outs, (held, sems) = refs[: len(units)], refs[len(units) :]
    section = place_ref[0]
    part = D // SECTIONS
    first = (section * part) // 128 * 128
    at, copies = 0, []
    for out_ref, pieces in zip(outs, units):
        to = 0
        for encoder, layer, kind in pieces:
            mats_ref = query_ref if encoder == "query" else key_ref
            for j in range(4 if kind == "attention" else 2):
                if kind == "attention":
                    source, wide, got = j * D + first, 256, part
                else:
                    source, wide, got = (4 + 4 * j + section) * D, D, D
                source = mats_ref.at[layer, :, pl.ds(pl.multiple_of(source, 128), wide)]
                copy = pltpu.make_async_copy(
                    source, held.at[:, at : at + wide], sems.at[len(copies)]
                )
                copy.start()
                copies.append((copy, at, wide, out_ref, to, got))
                at, to = at + wide, to + got
    for copy, at, wide, out_ref, to, got in copies:
        copy.wait()
        block = held[:, at : at + wide]
        if wide == 256:
            block = jnp.where(section % 2 == 1, pltpu.roll(block, 192, 1), block)
        out_ref[:, to : to + got] = block[:, :got].astype(bf16)


class Columns:
    def __init__(self, ref, at):
        self.ref, self.at = ref, at

    def __getitem__(self, index):
        start, stop = index[1].start or 0, index[1].stop
        return self.ref[:, self.at + start : self.at + stop]


def second_kernel(place_ref, left_ref, right_ref, out_ref):
    right_half = place_ref[1] >= 4
    out_ref[...] = jnp.where(right_half, left_ref[...], right_ref[...])


def place_rows(kind, refs, at, place_ref, whole_ref):
    wide = whole_ref.shape[1]
    rows, count = refs[0].shape[0], len(refs) // 2
    z, core = place_ref[1] // 2, place_ref[1] % 2

    def put(i, source):
        for chunk, its in ((refs[i], core), (refs[count + i], 1 - core)):
            start = pl.multiple_of((source * 2 + its) * rows, 16)
            whole_ref[pl.ds(start, rows), :] = chunk[:, at : at + wide]

    if kind == "circle":
        for i in range(count):
            put(i, lax.rem(z + count - i, count))
        return
    put(0, z)
    put(1, jnp.where(z == 0, 3, z - 1))
    put(2, jnp.where(z == 3, 0, z + 1))
    put(3, jnp.where(z >= 2, z - 2, z + 2))

    @pl.when((z == 0) | (z == 3))
    def _():
        put(4, 3 - z)


def weights_in(kind, refs, at, place_ref, whole_ref):
    if len(refs) == 1:
        return Columns(refs[0], at)
    place_rows(kind, refs, at, place_ref, whole_ref)
    return whole_ref


def attention_kernel(layer, first, keep, kind, count, at, *refs):
    refs = list(refs)
    place_ref, lens_ref, small_ref = refs[:3]
    chunk_refs, refs = refs[3 : 3 + count], refs[3 + count :]
    base_ref, refs = refs[0], refs[1:]
    if not first:
        sums, refs = refs[:4], refs[4:]
    part_refs, outs = refs[:2], refs[2:]
    whole_ref, outs = outs[-1], outs[:-1]
    weights_ref = weights_in(kind, chunk_refs, at, place_ref, whole_ref)
    if not first:
        y_ref, outs = outs[0], outs[1:]
        if keep:
            hat_ref, rate_ref = outs[:2]
            outs = outs[2:]
    if keep:
        q_ref, k_ref, v_ref, mixed_ref, prob_ref = outs
    part = D // SECTIONS
    bv = own_cols(small_at(small_ref, layer, AT_BV), place_ref[0], part)
    lane = lax.broadcasted_iota(jnp.int32, (1, part), 1)
    for row in range(MICRO):
        here = rows_of(row)
        if first:
            inputs = base_ref[here, :]
        else:
            inputs, hat, rate = norm_in(
                layer - 1, AT_G2, AT_S2, AT_B2, base_ref, sums, small_ref, row
            )
            y_ref[here, :] = inputs
            if keep:
                hat_ref[here, :] = hat
                rate_ref[here, :] = jnp.broadcast_to(rate, (ROW, 128))
        project = dot_nn(inputs, weights_ref[:, : 3 * part])
        query = project[:, :part]
        key_rows = project[:, part : 2 * part].astype(bf16)
        values = (project[:, 2 * part :] + bv).astype(bf16)
        allowed = allowed_of(lens_ref, row)
        mixed = jnp.zeros((ROW, part), f32)
        for head in range(part // HEAD_DIM):
            inside = (lane >= head * HEAD_DIM) & (lane < (head + 1) * HEAD_DIM)
            head_q = jnp.where(inside, query, 0.0).astype(bf16)
            scores = jnp.where(allowed, dot_nt(head_q, key_rows) * score_scale, -1e30)
            terms = jnp.exp(scores - jnp.max(scores, axis=-1, keepdims=True))
            prob = terms / jnp.sum(terms, axis=-1, keepdims=True)
            if keep:
                prob_ref[row, head] = prob
            mixed = jnp.where(inside, dot_nn(prob.astype(bf16), values), mixed)
        mixed = mixed.astype(bf16)
        part_refs[row][...] = dot_nt(mixed, weights_ref[:, 3 * part : 4 * part]).astype(bf16)
        if keep:
            q_ref[here, :] = query.astype(bf16)
            k_ref[here, :] = key_rows
            v_ref[here, :] = values
            mixed_ref[here, :] = mixed


def feed_kernel(layer, keep, kind, count, at, place_ref, small_ref, base_ref, *refs):
    sums, chunk_refs, refs = refs[:4], refs[4 : 4 + count], refs[4 + count :]
    part_refs, y_ref, whole_ref = refs[:2], refs[2], refs[-1]
    weights_ref = weights_in(kind, chunk_refs, at, place_ref, whole_ref)
    if keep:
        hat_ref, rate_ref, hidden_ref, active_ref = refs[3:7]
    b1 = own_cols(small_at(small_ref, layer, AT_B1, 4 * D), place_ref[0], D)
    for row in range(MICRO):
        here = rows_of(row)
        inputs, hat, rate = norm_in(layer, AT_G1, AT_S1, AT_BO, base_ref, sums, small_ref, row)
        y_ref[here, :] = inputs
        hidden = dot_nn(inputs, weights_ref[:, :D]) + b1
        active = (0.5 * hidden * (1.0 + lax.erf(hidden * (0.5**0.5)))).astype(bf16)
        part_refs[row][...] = dot_nt(active, weights_ref[:, D : 2 * D]).astype(bf16)
        if keep:
            hat_ref[here, :] = hat
            rate_ref[here, :] = jnp.broadcast_to(rate, (ROW, 128))
            hidden_ref[here, :] = hidden
            active_ref[here, :] = active


def last_kernel(layer, place_ref, lens_ref, small_ref, base_ref, *refs):
    sums, pooled_ref = refs[:4], refs[4]
    for row in range(MICRO):
        out, hat, rate = norm_in(layer, AT_G2, AT_S2, AT_B2, base_ref, sums, small_ref, row)
        part = pooled_ref.shape[-1]
        pooled_ref[row] = own_cols(pooled_of(lens_ref, row, out), place_ref[0], part)


def norm_back(grad_out, hat, rate, gain):
    inner = grad_out * gain
    return rate * (
        inner
        - jnp.mean(inner, axis=-1, keepdims=True)
        - hat * jnp.mean(inner * hat, axis=-1, keepdims=True)
    )


def row_sum(block):
    return jnp.sum(block, axis=0, keepdims=True)


def arrived_grad(base_ref, sums, row):
    grad = base_ref[rows_of(row), :] + (
        sums[2 * row][...].astype(f32) + sums[2 * row + 1][...].astype(f32)
    )
    return grad.astype(bf16)


def feed_back_kernel(layer, last, place_ref, small_ref, weights_ref, hidden_ref, base_ref, *refs):
    sums, refs = refs[:4], refs[4:]
    if last:
        cot_ref, lens_ref = refs[:2]
    else:
        hat_ref, rate_ref = refs[:2]
    part_refs = refs[2:4]
    carry_ref, branch_ref, grad_hidden_ref, sums_ref, bias_ref = refs[4:9]
    if last:
        y_ref, pooled_ref = refs[9:]
    gain = small_at(small_ref, layer, AT_G2)
    totals = [jnp.zeros((1, D), f32) for _ in range(4)]
    for row in range(MICRO):
        here = rows_of(row)
        if last:
            out, hat, rate = norm_in(layer, AT_G2, AT_S2, AT_B2, base_ref, sums, small_ref, row)
            part = y_ref.shape[1]
            y_ref[here, :] = own_cols(out, place_ref[0], part)
            pooled_ref[row] = own_cols(pooled_of(lens_ref, row, out), place_ref[0], part)
            grad_out = cot_ref[here, :].astype(f32)
        else:
            hat, rate = hat_ref[here, :], rate_ref[here, :1]
            grad_out = arrived_grad(base_ref, sums, row).astype(f32)
        grad = norm_back(grad_out, hat, rate, gain)
        carry_ref[here, :] = grad
        branch = grad.astype(bf16)
        branch_ref[here, :] = branch
        grad_active = dot_nn(branch, weights_ref[:, D : 2 * D])
        hidden = hidden_ref[here, :]
        slope = 0.5 * (1.0 + lax.erf(hidden * (0.5**0.5))) + hidden * (
            jnp.exp(-0.5 * hidden * hidden) * 0.3989422804014327
        )
        grad_hidden = (grad_active * slope).astype(bf16)
        grad_hidden_ref[here, :] = grad_hidden
        part_refs[row][...] = dot_nt(grad_hidden, weights_ref[:, :D]).astype(bf16)
        totals[0] += row_sum(branch.astype(f32))
        totals[1] += row_sum(grad_out * hat)
        totals[2] += row_sum(grad_out)
        totals[3] += row_sum(grad_hidden.astype(f32))
    for i in range(3):
        sums_ref[i : i + 1, :] = totals[i]
    bias_ref[...] = totals[3]


def attention_back_kernel(layer, small_ref, place_ref, weights_ref, base_ref, *refs):
    sums, hat_ref, rate_ref = refs[:4], refs[4], refs[5]
    q_ref, k_ref, v_ref, prob_ref = refs[6:10]
    part_refs = refs[10:12]
    carry_ref, branch_ref, grad_proj_ref, sums_ref, bias_ref = refs[12:]
    part = q_ref.shape[1]
    lane = lax.broadcasted_iota(jnp.int32, (1, part), 1)
    gain = small_at(small_ref, layer, AT_G1)
    totals = [jnp.zeros((1, D), f32) for _ in range(3)] + [jnp.zeros((1, part), f32)]
    for row in range(MICRO):
        here = rows_of(row)
        hat, rate = hat_ref[here, :], rate_ref[here, :1]
        grad_out = arrived_grad(base_ref, sums, row).astype(f32)
        grad = norm_back(grad_out, hat, rate, gain)
        carry_ref[here, :] = grad
        branch = grad.astype(bf16)
        branch_ref[here, :] = branch
        grad_mixed = dot_nn(branch, weights_ref[:, 3 * part : 4 * part])
        low_mixed = grad_mixed.astype(bf16)
        query, key_rows, values = q_ref[here, :], k_ref[here, :], v_ref[here, :]
        grads = [jnp.zeros((ROW, part), f32) for _ in range(3)]
        for head in range(part // HEAD_DIM):
            inside = (lane >= head * HEAD_DIM) & (lane < (head + 1) * HEAD_DIM)
            prob = prob_ref[row, head]
            head_mixed = jnp.where(inside, grad_mixed, 0.0).astype(bf16)
            grad_prob = dot_nt(head_mixed, values)
            grad_scores = prob * (
                grad_prob - jnp.sum(grad_prob * prob, axis=-1, keepdims=True)
            )
            grad_scores = grad_scores.astype(bf16)
            grad_q = dot_nn(grad_scores, key_rows) * score_scale
            grad_k = dot_tn(grad_scores, query) * score_scale
            grad_v = dot_tn(prob.astype(bf16), low_mixed)
            grads = [
                jnp.where(inside, new, old) for new, old in zip((grad_q, grad_k, grad_v), grads)
            ]
        grad_proj = jnp.concatenate(grads, axis=1).astype(bf16)
        grad_proj_ref[here, :] = grad_proj
        parted = dot_nt(grad_proj, weights_ref[:, : 3 * part]).astype(bf16)
        if layer > 0:
            part_refs[row][...] = parted
        else:
            half, upper = D // 2, place_ref[0] >= 2
            part_refs[0][here, :] = jnp.where(upper, parted[:, :half], parted[:, half:])
            part_refs[1][here, :] = jnp.where(upper, parted[:, half:], parted[:, :half])
        totals[0] += row_sum(branch.astype(f32))
        totals[1] += row_sum(grad_out * hat)
        totals[2] += row_sum(grad_out)
        totals[3] += row_sum(grads[2].astype(bf16).astype(f32))
    for i in range(3):
        sums_ref[i : i + 1, :] = totals[i]
    bias_ref[...] = totals[3]


def half_kernel(place_ref, kept_ref, came_ref, sent_out, kept_out):
    total = add_low(kept_ref[...], came_ref[...])
    wide = kept_out.shape[1]
    odd = place_ref[0] % 2 == 1
    kept_out[...] = jnp.where(odd, total[:, wide:], total[:, :wide])
    sent_out[...] = jnp.where(odd, total[:, :wide], total[:, wide:])


def input_kernel(place_ref, base_ref, kept_ref, came_ref, out_ref):
    base = own_cols(base_ref[...], place_ref[0], out_ref.shape[1])
    total = kept_ref[...].astype(f32) + came_ref[...].astype(f32)
    out_ref[...] = (base + total).astype(bf16)


def pack_kernel(rows, place_ref, *refs):
    ins, (out_ref, vector_ref, piece_ref) = refs[: 4 * LAYERS], refs[4 * LAYERS :]
    section = place_ref[0]
    own = section == 0
    slot = rows // LAYERS
    share = SMALL // (D // rows)
    out_ref[...] = jnp.zeros(out_ref.shape, bf16)
    piece_ref[...] = jnp.zeros(piece_ref.shape, f32)
    for layer in range(LAYERS):
        norm_1, value_bias, norm_2, hidden_bias = ins[4 * layer : 4 * layer + 4]
        part = value_bias.shape[1]
        for k in range(SECTIONS):
            mine = section == k
            vector_ref[:, k * part : (k + 1) * part] = jnp.where(mine, value_bias[...], 0.0)
            at = AT_B1 + k * D
            vector_ref[:, at : at + D] = jnp.where(mine, hidden_bias[...], 0.0)
        for i in range(3):
            vector_ref[:, AT_BO + i * D : AT_BO + (i + 1) * D] = jnp.where(
                own, norm_1[i : i + 1, :], 0.0
            )
            vector_ref[:, AT_B2 + i * D : AT_B2 + (i + 1) * D] = jnp.where(
                own, norm_2[i : i + 1, :], 0.0
            )
        for i in range(SMALL // 128):
            piece_ref[i : i + 1, :] = vector_ref[:, i * 128 : (i + 1) * 128]
        for b in range(D // rows):
            first = b * share // 128
            last = (b * share + share - 1) // 128 + 1
            start = b * rows + layer * slot
            out_ref[start : start + last - first, :] = piece_ref[first:last, :].astype(bf16)


def grad_kernel(rows, count, place_ref, *refs):
    mine_ref, other_ref, whole_ref = refs[-3:]
    at = 0
    for left_ref, right_ref in zip(refs[: 2 * count : 2], refs[1 : 2 * count : 2]):
        wide = right_ref.shape[1]
        whole_ref[:, at : at + wide] = dot_tn(left_ref[...], right_ref[...]).astype(bf16)
        at += wide
    if at < whole_ref.shape[1]:
        whole_ref[:, at:] = refs[2 * count][...]
    core = place_ref[1] % 2
    for out, owner in ((other_ref, 1 - core), (mine_ref, core)):
        for z in range(mine_ref.shape[0]):
            start = pl.multiple_of((2 * z + owner) * rows, 16)
            out[z] = whole_ref[pl.ds(start, rows), :]


def chip_kernel(place_ref, mine_ref, came_ref, *refs):
    places = mine_ref.shape[0]
    z = place_ref[1] // 2
    for d, out in enumerate(refs):
        owner = lax.rem(z + d, places)
        out[...] = add_low(mine_ref[owner], came_ref[owner])


def total_kernel(*refs):
    total = refs[0][...].astype(f32)
    for ref in refs[1:-1]:
        total = total + ref[...].astype(f32)
    refs[-1][...] = total.astype(bf16)


def place_kernel(copies, place_ref, *refs):
    out_ref, small_ref, vector_ref = refs[-3:]
    section = place_ref[0]
    part = D // SECTIONS
    rows = out_ref.buffer.shape[1]
    share = small_ref.shape[1]

    def owned(group, start, stop):
        found = []
        for slot in range(SECTIONS):
            value = group[0][:, start:stop]
            for k in range(1, SECTIONS):
                value = jnp.where(section ^ slot == k, group[k][:, start:stop], value)
            found.append(value.astype(f32))
        return found

    groups = [refs[i * SECTIONS : (i + 1) * SECTIONS] for i in range(3)]
    for copy in copies:
        copy.wait()
    for layer in reversed(range(LAYERS)):
        if layer > 0:
            attn, ffn = owned(groups[2], 0, D), owned(groups[2], D, 3 * D)
        else:
            attn, ffn = owned(groups[0], 0, D), owned(groups[1], 0, 2 * D)
        for j in range(4):
            columns = [a[:, j * part : (j + 1) * part] for a in attn]
            out_ref[layer, :, j * D : (j + 1) * D] = jnp.concatenate(columns, axis=1)
        for slot, block in enumerate(ffn):
            for j in range(2):
                start = (4 + 4 * j + slot) * D
                out_ref[layer, :, start : start + D] = block[:, j * D : (j + 1) * D]
        out_ref.push(layer)
    for layer in range(LAYERS):
        slot = rows // LAYERS
        at, count = layer * slot, min(16, slot)
        total = jnp.zeros((count, 128), f32)
        for k in range(SECTIONS):
            total = total + refs[k][at : at + count, 4 * part :].astype(f32)
        for i in range(vector_ref.shape[1] // 128):
            vector_ref[:, i * 128 : (i + 1) * 128] = total[i : i + 1, :]
        wide = vector_ref.shape[1]
        inside = lax.rem(place_ref[1] * share, 128)
        moved = pltpu.roll(jnp.broadcast_to(vector_ref[...], (8, wide)), wide - inside, 1)
        small_ref[layer : layer + 1, :] = moved[:1, :share]


def momentum_kernel(layer, query_ref, key_ref, query_small, key_small, *refs):
    out_ref, small_out, q_buf, k_buf, out_buf, in_sems, out_sems = refs[-7:]
    rows = query_ref.shape[1]
    depth, step = q_buf.shape[0], q_buf.shape[1]
    blocks = [(layer, pl.ds(j, step)) for j in range(0, rows, step)]

    def fetch(n):
        i, j = blocks[n]
        pair = [
            pltpu.make_async_copy(ref.at[i, j], buf.at[n % depth], in_sems.at[m, n % depth])
            for m, (ref, buf) in enumerate(((query_ref, q_buf), (key_ref, k_buf)))
        ]
        for copy in pair:
            copy.start()
        return pair

    small_out[...] = (query_small[...] - key_small[...]) * (1.0 - keep_rate)
    coming = [fetch(n) for n in range(min(depth, len(blocks)))]
    leaving = []
    for n, (i, j) in enumerate(blocks):
        for copy in coming[n]:
            copy.wait()
        if n >= depth:
            leaving[n - depth].wait()
        at = n % depth
        out_buf[at] = (q_buf[at] - k_buf[at]) * (1.0 - keep_rate)
        leaving.append(pltpu.make_async_copy(out_buf.at[at], out_ref.at[i, j], out_sems.at[at]))
        leaving[-1].start()
        if n + depth < len(blocks):
            coming.append(fetch(n + depth))
    for copy in leaving[-depth:]:
        copy.wait()


VMEM = pl.BlockSpec(memory_space=pltpu.VMEM)
SMEM = pl.BlockSpec(memory_space=pltpu.SMEM)
ANY = pl.BlockSpec(memory_space=pl.ANY)
SECTIONS = 4


def shaped(shape, kind):
    return jax.ShapeDtypeStruct(shape, kind)


class Raw:
    def __init__(self, value):
        self.value = value


class Leaving:
    def __init__(self, target, buffer, sems):
        self.buffer, self.target, self.sems, self.copies = buffer, target, sems, []

    def __setitem__(self, index, value):
        self.buffer[index] = value

    def push(self, part):
        sem = self.sems.at[len(self.copies)]
        copy = pltpu.make_async_copy(self.buffer.at[part], self.target.at[part], sem)
        copy.start()
        self.copies.append(copy)


def call(body, name, operands, outs, after=(), scratch=(), limit=12, aliases=None):
    arrays = [a.value if isinstance(a, Raw) else a for a in operands]
    results = [a.value if isinstance(a, Raw) else a for a in outs]
    specs = []
    for given, array in zip(operands, arrays):
        specs.append(ANY if isinstance(given, Raw) else SMEM if array.dtype == jnp.int32 else VMEM)
    count, skipped = len(operands), len(after)

    def kernel(*refs):
        body(*refs[:count], *refs[count + skipped :])

    return pl.pallas_call(
        kernel,
        name=name,
        in_specs=specs + [ANY] * len(after),
        out_specs=[ANY if isinstance(a, Raw) else VMEM for a in outs],
        out_shape=results,
        scratch_shapes=list(scratch),
        input_output_aliases=aliases or {},
        cost_estimate=pl.CostEstimate(flops=1, bytes_accessed=1, transcendentals=0),
        compiler_params=pltpu.CompilerParams(vmem_limit_bytes=limit * 2**20),
    )(*arrays, *after)


part_out = [shaped((ROW, D), bf16)] * 2
rows_out = shaped((TOK, D), bf16)
wide_out = shaped((TOK, D), f32)
rate_out = shaped((TOK, 128), f32)


def add_parts(left, right, after=()):
    return call(add_kernel, "add_parts", [left, right], [shaped(left.shape, bf16)], after)[0]


def momentum(layer, query, key, query_small, key_small, into, after):
    depth, step = 3, 24
    block = (depth, step, query.shape[2])
    return call(
        partial(momentum_kernel, layer),
        f"momentum{layer}",
        [Raw(query), Raw(key), query_small, key_small] + [Raw(a) for a in into],
        [Raw(shaped(query.shape, f32)), shaped(query_small.shape, f32)],
        after,
        [pltpu.VMEM(block, f32)] * 3
        + [pltpu.SemaphoreType.DMA((2, depth)), pltpu.SemaphoreType.DMA((depth,))],
        58,
        {4: 0} if into else {},
    )


def take(place, query_mats, key_mats, units, after=()):
    rows = query_mats.shape[1]
    kinds = [[kind for _, _, kind in pieces] for pieces in units]
    cols = [sum(D if kind == "attention" else 2 * D for kind in found) for found in kinds]
    held = sum(4 * 256 if kind == "attention" else 2 * D for found in kinds for kind in found)
    count = sum(4 if kind == "attention" else 2 for found in kinds for kind in found)
    return call(
        partial(take_kernel, units),
        "take",
        [place, Raw(query_mats), Raw(key_mats)],
        [shaped((rows, c), bf16) for c in cols],
        after,
        [pltpu.VMEM((rows, held), f32), pltpu.SemaphoreType.DMA((count,))],
        limit=58,
    )


def attention(layer, inputs, sums, shared, weights, keep, tag, after=()):
    (chunks, kind), at = weights
    part = D // SECTIONS
    operands = [*shared, *chunks, inputs] + ([] if sums is None else list(sums))
    outs = list(part_out)
    if sums is not None:
        outs += [rows_out] + ([wide_out, rate_out] if keep else [])
    if keep:
        outs += [shaped((TOK, part), bf16)] * 4
        outs += [shaped((MICRO, part // HEAD_DIM, ROW, ROW), f32)]
    shape = (D, 4 * part)
    return call(
        partial(attention_kernel, layer, sums is None, keep, kind, len(chunks), at),
        f"attention_{tag}{layer}",
        operands,
        outs + ([shaped(shape, bf16)] if keep else []),
        after,
        [] if keep else [pltpu.VMEM(shape, bf16)],
    )


def feed(layer, inputs, sums, shared, weights, keep, tag, after=()):
    (chunks, kind), at = weights
    place, lengths, small = shared
    shape = (D, 2 * D)
    outs = [*part_out, rows_out]
    outs += [wide_out, rate_out, wide_out, rows_out, shaped(shape, bf16)] if keep else []
    return call(
        partial(feed_kernel, layer, keep, kind, len(chunks), at),
        f"feed_{tag}{layer}",
        [place, small, inputs, *sums, *chunks],
        outs,
        after,
        [] if keep else [pltpu.VMEM(shape, bf16)],
    )


def grad_over_batch(place, rows, pairs, extra=None, after=(), begin=(), in_turn=False):
    places = lax.axis_size("batch") // 2
    wide = sum(right.shape[1] for _, right in pairs)
    cols = wide + (0 if extra is None else extra.shape[1])
    chunk = shaped((rows, cols), bf16)
    if rows % 16 == 0:
        mine, other = call(
            partial(grad_kernel, rows, len(pairs)),
            "grad",
            [place, *(x for pair in pairs for x in pair)] + ([] if extra is None else [extra]),
            [shaped((places, rows, cols), bf16)] * 2,
            begin,
            [pltpu.VMEM((D, cols), bf16)],
        )
        chunks = call(
            chip_kernel, "chip_sum", [place, mine, swap_core(other)], [chunk] * places, after
        )
    else:
        me = lax.axis_index("batch")
        z, core = me // 2, me % 2
        block = jnp.concatenate([dot_tn(l, r).astype(bf16) for l, r in pairs], axis=1)
        if extra is not None:
            block = jnp.concatenate([block, extra], axis=1)
        parted = block.reshape(places, 2, rows, cols)
        mine = lax.dynamic_index_in_dim(parted, core, 1, keepdims=False)
        other = lax.dynamic_index_in_dim(parted, 1 - core, 1, keepdims=False)
        chip = add_low(mine, swap_core(other))
        chunks = [
            lax.dynamic_index_in_dim(chip, (z + d) % places, 0, keepdims=False)
            for d in range(places)
        ]
    came = {}
    for d in sorted(range(1, places), key=lambda d: min(d, places - d)):
        came[d] = shift_z(put_after(chunks[d], *(list(came.values())[-1:] if in_turn else ())), d)
    total = call(total_kernel, "total", [chunks[0], *came.values()], [chunk])[0]
    return total, (*came.values(), chunks[0])


def on_device(tokens, key_tokens, cotangent, lengths, query_mats, query_small, key_mats, key_small):
    section, batch = lax.axis_index("section"), lax.axis_index("batch")
    part = D // SECTIONS
    rows = query_mats.shape[1]
    place = jnp.stack([section, batch]).astype(jnp.int32)
    shared_q, shared_k = (place, lengths, query_small), (place, lengths, key_small)
    own_out = shaped((TOK, part), bf16)
    pooled_out = shaped((MICRO, CROPS, part), f32)

    units = [
        [("query", 0, "attention")],
        [("query", 0, "feed"), ("query", 1, "attention")],
        [("query", 1, "feed"), ("key", 0, "attention")],
        [("key", 0, "feed"), ("key", 1, "attention")],
        [("key", 1, "feed")],
    ]
    blocks = take(place, query_mats, key_mats, units[:1])
    blocks += take(place, query_mats, key_mats, units[1:], (blocks[0],))
    both = (query_mats, key_mats, query_small, key_small)
    mats_step, early_step = momentum(0, *both, (), (blocks[1],))
    with jax.named_scope("weights_unit_0"):
        chunks = [gather_rows(place, blocks[0], True, (early_step,))]
    attn_q = [(chunks[0], 0)]
    found_0 = attention(0, tokens, None, shared_q, attn_q[0], True, "q")
    for n in range(1, len(units)):
        with jax.named_scope(f"weights_unit_{n}"):
            before = landed(chunks[-1])
            if n == 1:
                before = (*chunks[0][0][1 : len(chunks[0][0]) // 2], early_step)
            block = put_after(blocks[n], *before)
            chunks.append(gather_rows(place, block, onward=found_0[:1] if n == 1 else ()))
    attn_q.append((chunks[1], 2 * D))
    feed_q = [(chunks[1], 0), (chunks[2], 0)]
    attn_k = [(chunks[2], 2 * D), (chunks[3], 2 * D)]
    feed_k = [(chunks[3], 0), (chunks[4], 0)]

    def key_encoder():
        after = yield
        inputs, sums = key_tokens, None
        for layer in range(LAYERS):
            found = attention(layer, inputs, sums, shared_k, attn_k[layer], False, "k", after)
            inputs = found[2] if layer > 0 else inputs
            sums, after = yield from sum_in_steps(f"k{2 * layer}", *found[:2])
            p0, p1, inputs = feed(layer, inputs, sums, shared_k, feed_k[layer], False, "k", after)
            sums, after = yield from sum_in_steps(f"k{2 * layer + 1}", p0, p1)
        key_end.append((inputs, sums))
        yield ()

    key_end = []
    steps = key_encoder()
    next(steps)

    def beside(arrays):
        return () if key_end else steps.send(arrays)

    lines = [steps_of(found) for found in chunks[1:]]

    kept, weights = [], []
    inputs, sums = tokens, None
    done = ()
    gates = [((), ()), ((), lines[1][0]), (lines[1][1], lines[1][2]), (lines[2][0], lines[2][1])]
    for layer in range(LAYERS):
        found = found_0
        if layer > 0:
            found = attention(layer, inputs, sums, shared_q, attn_q[layer], True, "q", done)
        parts, found, attn_w = found[:2], found[2:-1], found[-1]
        if layer > 0:
            inputs, hat, rate = found[:3]
            kept[-1] += (hat, rate)
            found = found[3:]
        along = beside if layer > 0 else None
        sums, done = sum_parts(f"q{2 * layer}", *parts, along, *gates[2 * layer])
        attn_in, attn_kept = inputs, tuple(found)
        p0, p1, inputs, hat, rate, hidden, active, feed_w = feed(
            layer, inputs, sums, shared_q, feed_q[layer], True, "q", done
        )
        sums, done = sum_parts(f"q{2 * layer + 1}", p0, p1, along, *gates[2 * layer + 1])
        if chunks[0][1] == "whole":
            attn_w, feed_w = (
                found[0][:, at : at + wide]
                for ((found, _), at), wide in ((attn_q[layer], D), (feed_q[layer], 2 * D))
            )
        weights.append((attn_w, feed_w))
        kept.append((attn_in, attn_kept, hat, rate, inputs, hidden, active))

    small_parts = [None] * LAYERS
    sums_out, turn = shaped((3, D), f32), lines[3][2]
    for layer in reversed(range(LAYERS)):
        attn_in, attn_kept, hat1, rate1, feed_in, hidden, active, *rest = kept[layer]
        attn_w, feed_w = weights[layer]
        last = layer == LAYERS - 1
        operands = [feed_in, *sums, cotangent, lengths] if last else [carry, *sums, *rest]
        outs = [*part_out, wide_out, rows_out, rows_out, sums_out, shaped((1, D), f32)]
        if last:
            outs += [own_out, pooled_out]
        p0, p1, carry, branch, grad_hidden, sums_2, db1, *tail = call(
            partial(feed_back_kernel, layer, last),
            f"feed_back{layer}",
            [place, query_small, feed_w, hidden, *operands],
            outs,
            done,
        )
        if last:
            out_q, pooled_q = tail
        gate = (lines[2][2], lines[3][0]) if last else (turn[:1], turn[1:2])
        sums, done = sum_parts(f"back{2 * layer + 1}", p0, p1, beside, *gate)
        feed_pairs = [(feed_in, grad_hidden), (branch, active)]
        if layer == 0:
            with jax.named_scope("grad_feed0"):
                total_feed, turn_feed = grad_over_batch(
                    place, rows, feed_pairs, None, turn[1:2], sums[::2]
                )
            done = (*done, turn_feed[-1])
        q, k, v, mixed, prob = attn_kept
        p0, p1, carry, branch, grad_proj, sums_1, dbv = call(
            partial(attention_back_kernel, layer),
            f"attention_back{layer}",
            [query_small, place, attn_w, carry, *sums, hat1, rate1, q, k, v, prob],
            [
                *(part_out if layer > 0 else [shaped((TOK, D // 2), bf16)] * 2),
                wide_out,
                rows_out,
                shaped((TOK, 3 * part), bf16),
                sums_out,
                shaped((1, part), f32),
            ],
            done,
        )
        if layer > 0:
            sums, done = sum_parts(f"back{2 * layer}", p0, p1, beside, *lines[3][1:])
        else:
            sums = sum_own_cols("back0", place, p0, p1)
        small_parts[layer] = [sums_1, dbv, sums_2, db1]
        attn_pairs = [(attn_in, grad_proj), (branch, mixed)]
        if layer > 0:
            with jax.named_scope("grad_layer1"):
                total_layer, turn = grad_over_batch(
                    place, rows, attn_pairs + feed_pairs, None, turn, sums[::2], True
                )
    (extra,) = call(
        partial(pack_kernel, rows),
        "pack_small",
        [place, *small_parts[0], *small_parts[1]],
        [shaped((D, 128), bf16)],
        scratch=[pltpu.VMEM((1, SMALL), f32), pltpu.VMEM((72, 128), f32)],
    )
    with jax.named_scope("grad_attention0"):
        total_attn, turn_attn = grad_over_batch(place, rows, attn_pairs, extra)
    with jax.named_scope("place_layer1"):
        got_layer = gather_section(total_layer, True, turn_attn[-1:])
    mats_step, small_step = momentum(1, *both, (mats_step,), turn_attn[-1:])
    with jax.named_scope("place_layer0"):
        got_feed = gather_section(total_feed)
        got_attn = gather_section(total_attn)
    while not key_end:
        beside(())
    inputs_k, sums_k = key_end[0]
    (pooled_k,) = call(
        partial(last_kernel, LAYERS - 1),
        "last_k",
        [place, lengths, key_small, inputs_k, *sums_k],
        [pooled_out],
    )
    (input_grad,) = call(input_kernel, "input_grad", [place, carry, *sums], [own_out])

    share = SMALL // lax.axis_size("batch")
    mats_shape = (LAYERS, rows, 12 * D)
    touched = -(-(share + 127) // 128) * 128

    gathered = [*got_attn, *got_feed, *got_layer]

    def place_body(place_ref, *refs):
        sources, refs = refs[: len(gathered)], refs[len(gathered) :]
        out_ref, small_ref, buffer, vector_ref, sems, in_sems, *held = refs
        copies = [
            pltpu.make_async_copy(source, there, in_sems.at[i])
            for i, (source, there) in enumerate(zip(sources, held))
        ]
        for copy in copies:
            copy.start()
        out = Leaving(out_ref, buffer, sems)
        place_kernel(copies, place_ref, *held, out, small_ref, vector_ref)
        for copy in out.copies:
            copy.wait()

    grad_mats, grad_small = call(
        place_body,
        "place_grads",
        [place, *map(Raw, gathered)],
        [Raw(shaped(mats_shape, f32)), shaped((LAYERS, share), f32)],
        scratch=[
            pltpu.VMEM(mats_shape, f32),
            pltpu.VMEM((1, touched), f32),
            pltpu.SemaphoreType.DMA((LAYERS,)),
            pltpu.SemaphoreType.DMA((len(gathered),)),
            *(pltpu.VMEM(block.shape, bf16) for block in gathered),
        ],
        limit=58,
    )
    return (
        out_q,
        pooled_q,
        pooled_k,
        input_grad,
        grad_mats,
        grad_small,
        mats_step,
        small_step,
    )


def solution(mesh):
    in_specs = (
        P("batch", None),
        P("batch", None),
        P("batch", None),
        P("batch", None),
        P(None, "batch", None),
        P(),
        P(None, "batch", None),
        P(),
    )
    out_specs = (
        P("batch", "section"),
        P("batch", None, "section"),
        P("batch", None, "section"),
        P("batch", "section"),
        P(None, "batch", None),
        P(None, "batch"),
        P(None, "batch", None),
        P(),
    )
    return jax.shard_map(
        on_device, mesh=mesh, in_specs=in_specs, out_specs=out_specs, check_vma=False
    )
```

time: 592 us -> 420 us (0.71)
  the two profiles are of different devices: /device:TPU:8 before, /device:TPU:0 now
where the time goes in v2:
time: 420 us; the launch traced here: 412 us
  waiting for transfers between devices  197 us (47%)
  starting transfers between devices  114 us (27%)
  Pallas kernels  91.5 us (22%)
  local copies, waits for them, and re-layouts  6.51 us (2%)
    pallas_call x56, Pallas kernels, call(): pl.pallas_call(kernel, name=name, in_specs=specs + [ANY] * len(after), ou...  91.5 us
    ppermute x23, waiting for transfers between devices, swap_x(): return lax.ppermute(block, 'section', [(0, 1), (1, 0), (2, 3), (3, 2)])  59.7 us
    ppermute x23, waiting for transfers between devices, swap_y(): return lax.ppermute(block, 'section', [(0, 2), (2, 0), (1, 3), (3, 1)])  48.2 us
    ppermute x16, waiting for transfers between devices, pass_z(): return lax.ppermute(block, 'batch', pairs)  37 us
    ppermute x12, waiting for transfers between devices, shift_z(): lax.ppermute(block, 'batch', [(i, (i + 2 * distance) % count) for i in ra...  36.7 us
    ppermute x23, starting transfers between devices, swap_y(): return lax.ppermute(block, 'section', [(0, 2), (2, 0), (1, 3), (3, 1)])  27.7 us
    ppermute x16, starting transfers between devices, pass_z(): return lax.ppermute(block, 'batch', pairs)  26.8 us
    ppermute x23, starting transfers between devices, swap_x(): return lax.ppermute(block, 'section', [(0, 1), (1, 0), (2, 3), (3, 2)])  25.3 us
  transfers between devices with their start and end apart: 114, of which 46 were waited for; matrix products, arithmetic and copies ran while one was open for 1% of the time, Pallas kernels for 17%

profile of v2, /device:TPU:0, one launch (start us, length us, event | category | flops | bytes accessed | tf_op | source)
XLA Modules:
  0.0 411.8 jit_solution(9297817202855575815)
XLA Ops:
  15.7 6.7 %momentum0.1 = (f32[2,96,9216]{2,1,0:T(8,128)}, f32[2,8448]{1,0:T(2,128)}) custom-call(f32[2,96,9216]{2,1,0:T(8,128)} %refs_0_.7, f32[2,96,9216]{2,1,0:T(8,128)} %refs_1_.31, f32[2,8448]{1,0:T(2,128)} %refs_2_.21, f32[2,8448]{1,0:T(2,128)} %refs_3_.3, bf16[96,2304]{1,0:T(8,128)(2,1)} %get-tuple-element.136.refs_4_.refs_7_.refs_3_), custom_call_target="tpu_custom_call" | custom-call | flops 1 | bytes 1 | tf_op jit(solution)/shard_map/momentum0/pallas_call | solution.py:713
  41.7 9.9 %collective-permute-done.10.refs_2_ = bf16[96,2304]{1,0:T(8,128)(2,1)S(1)} collective-permute-done((bf16[96,2304]{1,0:T(8,128)(2,1)S(1)}, bf16[96,2304]{1,0:T(8,128)(2,1)S(1)}, u32[]{:S(2)}, u32[]{:S(2)}) %collective-permute-start.10) | collective-permute-done | bytes 442400 | tf_op jit(solution)/shard_map/weights_unit_1/ppermute | solution.py:97
  56.3 9.3 %collective-permute-done.19.refs_1_ = bf16[256,768]{1,0:T(8,128)(2,1)S(1)} collective-permute-done((bf16[256,768]{1,0:T(8,128)(2,1)S(1)}, bf16[256,768]{1,0:T(8,128)(2,1)S(1)}, u32[]{:S(2)}, u32[]{:S(2)}) %collective-permute-start.19) | collective-permute-done | bytes 393248 | tf_op jit(solution)/shard_map/sum_q0_first/ppermute | solution.py:43
  122.8 6.6 %collective-permute-done.44.refs_9_.refs_5_ = bf16[96,2304]{1,0:T(8,128)(2,1)S(1)} collective-permute-done((bf16[96,2304]{1,0:T(8,128)(2,1)S(1)}, bf16[96,2304]{1,0:T(8,128)(2,1)S(1)}, u32[]{:S(2)}, u32[]{:S(2)}) %collective-permute-start.44) | collective-permute-done | bytes 442400 | tf_op jit(solution)/shard_map/weights_unit_3/ppermute | solution.py:97
  143.2 5.6 %collective-permute-done.39.refs_1_ = bf16[256,768]{1,0:T(8,128)(2,1)S(1)} collective-permute-done((bf16[256,768]{1,0:T(8,128)(2,1)S(1)}, bf16[256,768]{1,0:T(8,128)(2,1)S(1)}, u32[]{:S(2)}, u32[]{:S(2)}) %collective-permute-start.39) | collective-permute-done | bytes 393248 | tf_op jit(solution)/shard_map/sum_q3_first/ppermute | solution.py:39
  151.3 6.0 %collective-permute-done.47.refs_1_ = bf16[256,768]{1,0:T(8,128)(2,1)S(1)} collective-permute-done((bf16[256,768]{1,0:T(8,128)(2,1)S(1)}, bf16[256,768]{1,0:T(8,128)(2,1)S(1)}, u32[]{:S(2)}, u32[]{:S(2)}) %collective-permute-start.47) | collective-permute-done | bytes 393248 | tf_op jit(solution)/shard_map/sum_k0_first/ppermute | solution.py:39
  158.1 5.5 %collective-permute-done.40.refs_6_ = bf16[256,768]{1,0:T(8,128)(2,1)S(1)} collective-permute-done((bf16[256,768]{1,0:T(8,128)(2,1)S(1)}, bf16[256,768]{1,0:T(8,128)(2,1)S(1)}, u32[]{:S(2)}, u32[]{:S(2)}) %collective-permute-start.40) | collective-permute-done | bytes 393248 | tf_op jit(solution)/shard_map/sum_q3_second/ppermute | solution.py:43
  176.6 5.9 %collective-permute-done.57.refs_1_ = bf16[256,768]{1,0:T(8,128)(2,1)S(1)} collective-permute-done((bf16[256,768]{1,0:T(8,128)(2,1)S(1)}, bf16[256,768]{1,0:T(8,128)(2,1)S(1)}, u32[]{:S(2)}, u32[]{:S(2)}) %collective-permute-start.57) | collective-permute-done | bytes 393248 | tf_op jit(solution)/shard_map/sum_back3_first/ppermute | solution.py:39
  196.9 5.6 %collective-permute-done.66.refs_2_ = bf16[96,1536]{1,0:T(8,128)(2,1)S(1)} collective-permute-done((bf16[96,1536]{1,0:T(8,128)(2,1)S(1)}, bf16[96,1536]{1,0:T(8,128)(2,1)S(1)}, u32[]{:S(2)}, u32[]{:S(2)}) %collective-permute-start.66) | collective-permute-done | bytes 294944 | tf_op jit(solution)/shard_map/weights_unit_4/ppermute | solution.py:97
  203.1 5.4 %attention_back1.1 = (bf16[256,768]{1,0:T(8,128)(2,1)S(1)}, bf16[256,768]{1,0:T(8,128)(2,1)S(1)}, f32[512,768]{1,0:T(8,128)S(1)}, bf16[512,768]{1,0:T(8,128)(2,1...) custom-call(f32[2,8448]{1,0:T(2,128)S(1)} %copy-done.1, s32[2]{0:T(128)S(1)} %copy-done.15, ...), custom_call_target="tpu_custom_call" | custom-call | flops 1 | bytes 1 | tf_op jit(solution)/shard_map/attention_back1/pallas_call | solution.py:713
  212.2 5.5 %collective-permute-done.63.refs_1_ = bf16[256,768]{1,0:T(8,128)(2,1)S(1)} collective-permute-done((bf16[256,768]{1,0:T(8,128)(2,1)S(1)}, bf16[256,768]{1,0:T(8,128)(2,1)S(1)}, u32[]{:S(2)}, u32[]{:S(2)}) %collective-permute-start.63) | collective-permute-done | bytes 393248 | tf_op jit(solution)/shard_map/sum_back2_first/ppermute | solution.py:39
  232.0 10.1 %collective-permute-done.76.refs_1_ = bf16[96,2304]{1,0:T(8,128)(2,1)S(1)} collective-permute-done((bf16[96,2304]{1,0:T(8,128)(2,1)S(1)}, bf16[96,2304]{1,0:T(8,128)(2,1)S(1)}, u32[]{:S(2)}, u32[]{:S(2)}) %collective-permute-start.76) | collective-permute-done | bytes 442400 | tf_op jit(solution)/shard_map/grad_layer1/ppermute | solution.py:53
  242.3 6.1 %collective-permute-done.72.refs_6_ = bf16[256,768]{1,0:T(8,128)(2,1)S(1)} collective-permute-done((bf16[256,768]{1,0:T(8,128)(2,1)S(1)}, bf16[256,768]{1,0:T(8,128)(2,1)S(1)}, u32[]{:S(2)}, u32[]{:S(2)}) %collective-permute-start.72) | collective-permute-done | bytes 393248 | tf_op jit(solution)/shard_map/sum_back2_second/ppermute | solution.py:43
  253.3 8.0 %collective-permute-done.74.refs_1_ = bf16[256,768]{1,0:T(8,128)(2,1)S(1)} collective-permute-done((bf16[256,768]{1,0:T(8,128)(2,1)S(1)}, bf16[256,768]{1,0:T(8,128)(2,1)S(1)}, u32[]{:S(2)}, u32[]{:S(2)}) %collective-permute-start.74) | collective-permute-done | bytes 393248 | tf_op jit(solution)/shard_map/sum_back1_first/ppermute | solution.py:39
  268.8 7.9 %collective-permute-done.69.refs_15_ = bf16[256,768]{1,0:T(8,128)(2,1)S(1)} collective-permute-done((bf16[256,768]{1,0:T(8,128)(2,1)S(1)}, bf16[256,768]{1,0:T(8,128)(2,1)S(1)}, u32[]{:S(2)}, u32[]{:S(2)}) %collective-permute-start.69) | collective-permute-done | bytes 393248 | tf_op jit(solution)/shard_map/sum_k1_second/ppermute | solution.py:43
  285.7 5.3 %attention_back0.1 = (bf16[512,384]{1,0:T(8,128)(2,1)S(1)}, bf16[512,384]{1,0:T(8,128)(2,1)S(1)}, f32[512,768]{1,0:T(8,128)S(1)}, bf16[512,768]{1,0:T(8,128)(2,1...) custom-call(f32[2,8448]{1,0:T(2,128)S(1)} %copy-done.1, s32[2]{0:T(128)S(1)} %copy-done.15, ...), custom_call_target="tpu_custom_call" | custom-call | flops 1 | bytes 1 | tf_op jit(solution)/shard_map/attention_back0/pallas_call | solution.py:713
  295.8 9.3 %collective-permute-done.81.refs_1_ = bf16[256,768]{1,0:T(8,128)(2,1)S(1)} collective-permute-done((bf16[256,768]{1,0:T(8,128)(2,1)S(1)}, bf16[256,768]{1,0:T(8,128)(2,1)S(1)}, u32[]{:S(2)}, u32[]{:S(2)}) %collective-permute-start.81) | collective-permute-done | bytes 393248 | tf_op jit(solution)/shard_map/sum_k2_first/ppermute | solution.py:43
  307.7 10.1 %collective-permute-done.110.refs_3_ = bf16[96,2304]{1,0:T(8,128)(2,1)S(1)} collective-permute-done((bf16[96,2304]{1,0:T(8,128)(2,1)S(1)}, bf16[96,2304]{1,0:T(8,128)(2,1)S(1)}, u32[]{:S(2)}, u32[]{:S(2)}) %collective-permute-start.110) | collective-permute-done | bytes 442400 | tf_op jit(solution)/shard_map/grad_layer1/ppermute | solution.py:53
  332.9 6.9 %collective-permute-done.88.refs_1_ = bf16[256,768]{1,0:T(8,128)(2,1)S(1)} collective-permute-done((bf16[256,768]{1,0:T(8,128)(2,1)S(1)}, bf16[256,768]{1,0:T(8,128)(2,1)S(1)}, u32[]{:S(2)}, u32[]{:S(2)}) %collective-permute-start.88) | collective-permute-done | bytes 393248 | tf_op jit(solution)/shard_map/sum_k3_first/ppermute | solution.py:39
  343.1 11.0 %collective-permute-done.106.refs_3_ = bf16[96,1536]{1,0:T(8,128)(2,1)S(1)} collective-permute-done((bf16[96,1536]{1,0:T(8,128)(2,1)S(1)}, bf16[96,1536]{1,0:T(8,128)(2,1)S(1)}, u32[]{:S(2)}, u32[]{:S(2)}) %collective-permute-start.106) | collective-permute-done | bytes 294944 | tf_op jit(solution)/shard_map/grad_feed0/ppermute | solution.py:53
  367.0 5.5 %collective-permute-done.100.refs_3_ = bf16[96,896]{1,0:T(8,128)(2,1)S(1)} collective-permute-done((bf16[96,896]{1,0:T(8,128)(2,1)S(1)}, bf16[96,896]{1,0:T(8,128)(2,1)S(1)}, u32[]{:S(2)}, u32[]{:S(2)}) %collective-permute-start.100) | collective-permute-done | bytes 172064 | tf_op jit(solution)/shard_map/grad_attention0/ppermute | solution.py:53
  377.5 8.7 %collective-permute-done.96.refs_3_ = bf16[512,192]{1,0:T(8,128)(2,1)S(1)} collective-permute-done((bf16[512,192]{1,0:T(8,128)(2,1)S(1)}, bf16[512,192]{1,0:T(8,128)(2,1)S(1)}, u32[]{:S(2)}, u32[]{:S(2)}) %collective-permute-start.96) | collective-permute-done | bytes 196640 | tf_op jit(solution)/shard_map/sum_back0/ppermute | solution.py:39
  397.5 6.6 %momentum1.1 = (f32[2,96,9216]{2,1,0:T(8,128)}, f32[2,8448]{1,0:T(2,128)}) custom-call(f32[2,96,9216]{2,1,0:T(8,128)} %refs_0_.7, f32[2,96,9216]{2,1,0:T(8,128)} %refs_1_.31, f32[2,8448]{1,0:T(2,128)} %refs_2_.21, f32[2,8448]{1,0:T(2,128)} %refs_3_.3, f32[2,96,9216]{2,1,0:T(8,128)} %get-tuple-element.257.refs_4_, ...), custom_call_target="tpu_custom_call", output_to_operand_aliasing={{0}: (4, {})} | custom-call | flops 1 | bytes 1 | tf_op jit(solution)/shard_map/momentum1/pallas_call | solution.py:713
  404.2 7.1 %place_grads.1 = (f32[2,96,9216]{2,1,0:T(8,128)}, f32[2,1056]{1,0:T(2,128)}) custom-call(s32[2]{0:T(128)} %pad_add_fusion.refs_0_.refs_1_, bf16[96,896]{1,0:T(8,128)(2,1)} %copy-done.13, bf16[96,896]{1,0:T(8,128)(2,1)} %collective-permute-done.101.refs_2_, bf16[96,896]{1,0:T(8,128)(2,1)} %collective-permute-done.102.refs_3_, ...), custom_call_target="tpu_custom_call" | custom-call | flops 1 | bytes 1 | tf_op jit(solution)/shard_map/place_grads/pallas_call | solution.py:713
  (325 shorter events, 234.7 us)
Async XLA Ops:
  4.0 18.5 %collective-permute-start = (bf16[96,768]{1,0:T(8,128)(2,1)}, bf16[96,768]{1,0:T(8,128)(2,1)S(1)}, u32[]{:S(2)}, u32[]{:S(2)}) collective-permute-start(bf16[96,768]{1,0:T(8,128)(2,1)} %take.2.refs_3_), channel_id=1, source_target_pairs={{0,2},{1,3},{2,4},{3,5},{4,6},{5,7},{6,0},{7,1},{8,10},{9,11},{10,... | collective-permute-start | bytes 442376 | tf_op jit(solution)/shard_map/weights_unit_0/ppermute | solution.py:53
  122.1 18.8 %collective-permute-start.43 = (bf16[96,2304]{1,0:T(8,128)(2,1)S(1)}, bf16[96,2304]{1,0:T(8,128)(2,1)S(1)}, u32[]{:S(2)}, u32[]{:S(2)}) collective-permute-start(bf16[96,2304]{1,0:T(8,128)(2,1)S(1)} %collective-permute-done.41.refs_8_.refs_4_), channel_id=1, source_target_pairs={{2,4},{3,5},{4,6},{5,7},{10,12},{11,13},{12,14},{13,15},{18,20},{1... | collective-permute-start | bytes 1327112 | tf_op jit(solution)/shard_map/weights_unit_3/ppermute | solution.py:97
  139.0 18.3 %collective-permute-start.47 = (bf16[256,768]{1,0:T(8,128)(2,1)S(1)}, bf16[256,768]{1,0:T(8,128)(2,1)S(1)}, u32[]{:S(2)}, u32[]{:S(2)}) collective-permute-start(bf16[256,768]{1,0:T(8,128)(2,1)S(1)} %get-tuple-element.154.refs_17_.refs_0_), channel_id=1, source_target_pairs={{0,8},{8,0},{16,24},{24,16},{1,9},{9,1},{17,25},{25,17},{2,10},{10... | collective-permute-start | bytes 1179656 | tf_op jit(solution)/shard_map/sum_k0_first/ppermute | solution.py:39
  157.4 18.4 %collective-permute-start.51 = (bf16[96,2304]{1,0:T(8,128)(2,1)S(1)}, bf16[96,2304]{1,0:T(8,128)(2,1)S(1)}, u32[]{:S(2)}, u32[]{:S(2)}) collective-permute-start(bf16[96,2304]{1,0:T(8,128)(2,1)S(1)} %collective-permute-done.41.refs_8_.refs_4_), channel_id=1, source_target_pairs={{0,1},{1,0},{2,3},{3,2},{4,5},{5,4},{6,7},{7,6},{8,9},{9,8},{10,11... | collective-permute-start | bytes 1327112 | tf_op jit(solution)/shard_map/weights_unit_3/ppermute | solution.py:48
  157.8 18.0 %collective-permute-start.52 = (bf16[96,2304]{1,0:T(8,128)(2,1)S(1)}, bf16[96,2304]{1,0:T(8,128)(2,1)S(1)}, u32[]{:S(2)}, u32[]{:S(2)}) collective-permute-start(bf16[96,2304]{1,0:T(8,128)(2,1)S(1)} %collective-permute-done.44.refs_9_.refs_5_), channel_id=1, source_target_pairs={{0,1},{1,0},{2,3},{3,2},{4,5},{5,4},{6,7},{7,6},{8,9},{9,8},{10,11... | collective-permute-start | bytes 1327112 | tf_op jit(solution)/shard_map/weights_unit_3/ppermute | solution.py:48
  185.4 17.7 %collective-permute-start.61 = (bf16[256,768]{1,0:T(8,128)(2,1)S(1)}, bf16[256,768]{1,0:T(8,128)(2,1)S(1)}, u32[]{:S(2)}, u32[]{:S(2)}) collective-permute-start(bf16[256,768]{1,0:T(8,128)(2,1)S(1)} %add_parts.32.refs_17_.refs_4_), channel_id=1, source_target_pairs={{0,16},{16,0},{8,24},{24,8},{1,17},{17,1},{9,25},{25,9},{2,18},{18... | collective-permute-start | bytes 1179656 | tf_op jit(solution)/shard_map/sum_back3_second/ppermute | solution.py:43
  229.8 18.6 %collective-permute-start.72 = (bf16[256,768]{1,0:T(8,128)(2,1)S(1)}, bf16[256,768]{1,0:T(8,128)(2,1)S(1)}, u32[]{:S(2)}, u32[]{:S(2)}) collective-permute-start(bf16[256,768]{1,0:T(8,128)(2,1)S(1)} %add_parts.34.refs_2_.refs_5_.refs_9_), channel_id=1, source_target_pairs={{0,16},{16,0},{8,24},{24,8},{1,17},{17,1},{9,25},{25,9},{2,18},{18... | collective-permute-start | bytes 1179656 | tf_op jit(solution)/shard_map/sum_back2_second/ppermute | solution.py:43
  242.1 20.1 %collective-permute-start.78 = (bf16[96,2304]{1,0:T(8,128)(2,1)S(1)}, bf16[96,2304]{1,0:T(8,128)(2,1)S(1)}, u32[]{:S(2)}, u32[]{:S(2)}) collective-permute-start(bf16[96,2304]{1,0:T(8,128)(2,1)S(1)} %get-tuple-element.203), channel_id=1, source_target_pairs={{0,6},{1,7},{2,0},{3,1},{4,2},{5,3},{6,4},{7,5},{8,14},{9,15},{10,... | collective-permute-start | bytes 1327112 | tf_op jit(solution)/shard_map/grad_layer1/ppermute | solution.py:53
  264.6 17.9 %collective-permute-start.94 = (bf16[4,96,1536]{2,1,0:T(8,128)(2,1)S(1)}, bf16[4,96,1536]{2,1,0:T(8,128)(2,1)S(1)}, u32[]{:S(2)}, u32[]{:S(2)}) collective-permute-start(bf16[4,96,1536]{2,1,0:T(8,128)(2,1)S(1)} %get-tuple-element.222), channel_id=1, source_target_pairs={{0,1},{1,0},{2,3},{3,2},{4,5},{5,4},{6,7},{7,6},{8,9},{9,8},{10,11... | collective-permute-start | bytes 3538952 | tf_op jit(solution)/shard_map/grad_feed0/ppermute | solution.py:48
  266.7 18.0 %collective-permute-start.92 = (bf16[256,768]{1,0:T(8,128)(2,1)S(1)}, bf16[256,768]{1,0:T(8,128)(2,1)S(1)}, u32[]{:S(2)}, u32[]{:S(2)}) collective-permute-start(bf16[256,768]{1,0:T(8,128)(2,1)S(1)} %add_parts.38.refs_18_.refs_5_.refs_4_), channel_id=1, source_target_pairs={{0,16},{16,0},{8,24},{24,8},{1,17},{17,1},{9,25},{25,9},{2,18},{18... | collective-permute-start | bytes 1179656 | tf_op jit(solution)/shard_map/sum_back1_second/ppermute | solution.py:43
  267.7 18.0 %collective-permute-start.93 = (bf16[256,768]{1,0:T(8,128)(2,1)S(1)}, bf16[256,768]{1,0:T(8,128)(2,1)S(1)}, u32[]{:S(2)}, u32[]{:S(2)}) collective-permute-start(bf16[256,768]{1,0:T(8,128)(2,1)S(1)} %add_parts.39.refs_19_.refs_6_), channel_id=1, source_target_pairs={{0,8},{8,0},{16,24},{24,16},{1,9},{9,1},{17,25},{25,17},{2,10},{10... | collective-permute-start | bytes 1179656 | tf_op jit(solution)/shard_map/sum_back1_second/ppermute | solution.py:39
  293.6 24.3 %collective-permute-start.97 = (bf16[4,96,896]{2,1,0:T(8,128)(2,1)S(1)}, bf16[4,96,896]{2,1,0:T(8,128)(2,1)S(1)}, u32[]{:S(2)}, u32[]{:S(2)}) collective-permute-start(bf16[4,96,896]{2,1,0:T(8,128)(2,1)S(1)} %get-tuple-element.241), channel_id=1, source_target_pairs={{0,1},{1,0},{2,3},{3,2},{4,5},{5,4},{6,7},{7,6},{8,9},{9,8},{10,11... | collective-permute-start | bytes 2064392 | tf_op jit(solution)/shard_map/grad_attention0/ppermute | solution.py:48
  295.2 22.6 %collective-permute-start.110 = (bf16[96,2304]{1,0:T(8,128)(2,1)S(1)}, bf16[96,2304]{1,0:T(8,128)(2,1)S(1)}, u32[]{:S(2)}, u32[]{:S(2)}) collective-permute-start(bf16[96,2304]{1,0:T(8,128)(2,1)S(1)} %get-tuple-element.251), channel_id=1, source_target_pairs={{0,4},{1,5},{2,6},{3,7},{4,0},{5,1},{6,2},{7,3},{8,12},{9,13},{10,... | collective-permute-start | bytes 1327112 | tf_op jit(solution)/shard_map/grad_layer1/ppermute | solution.py:53
  324.9 17.3 %collective-permute-start.105 = (bf16[96,1536]{1,0:T(8,128)(2,1)S(1)}, bf16[96,1536]{1,0:T(8,128)(2,1)S(1)}, u32[]{:S(2)}, u32[]{:S(2)}) collective-permute-start(bf16[96,1536]{1,0:T(8,128)(2,1)S(1)} %get-tuple-element.247), channel_id=1, source_target_pairs={{0,6},{1,7},{2,0},{3,1},{4,2},{5,3},{6,4},{7,5},{8,14},{9,15},{10,... | collective-permute-start | bytes 884744 | tf_op jit(solution)/shard_map/grad_feed0/ppermute | solution.py:53
  332.4 21.6 %collective-permute-start.95 = (bf16[512,384]{1,0:T(8,128)(2,1)S(1)}, bf16[512,384]{1,0:T(8,128)(2,1)S(1)}, u32[]{:S(2)}, u32[]{:S(2)}) collective-permute-start(bf16[512,384]{1,0:T(8,128)(2,1)S(1)} %get-tuple-element.226), channel_id=1, source_target_pairs={{0,16},{16,0},{8,24},{24,8},{1,17},{17,1},{9,25},{25,9},{2,18},{18... | collective-permute-start | bytes 1179656 | tf_op jit(solution)/shard_map/sum_back0/ppermute | solution.py:43
  339.9 22.2 %collective-permute-start.112 = (bf16[96,2304]{1,0:T(8,128)(2,1)S(1)}, bf16[96,2304]{1,0:T(8,128)(2,1)S(1)}, u32[]{:S(2)}, u32[]{:S(2)}) collective-permute-start(bf16[96,2304]{1,0:T(8,128)(2,1)S(1)} %total.5.refs_9_), channel_id=1, source_target_pairs={{0,16},{8,24},{16,0},{24,8},{1,17},{9,25},{17,1},{25,9},{2,18},{10... | collective-permute-start | bytes 1327112 | tf_op jit(solution)/shard_map/place_layer1/ppermute | solution.py:148
  340.6 20.5 %collective-permute-start.89 = (bf16[256,768]{1,0:T(8,128)(2,1)S(1)}, bf16[256,768]{1,0:T(8,128)(2,1)S(1)}, u32[]{:S(2)}, u32[]{:S(2)}) collective-permute-start(bf16[256,768]{1,0:T(8,128)(2,1)S(1)} %add_parts.42.refs_4_), channel_id=1, source_target_pairs={{0,16},{16,0},{8,24},{24,8},{1,17},{17,1},{9,25},{25,9},{2,18},{18... | collective-permute-start | bytes 1179656 | tf_op jit(solution)/shard_map/sum_k3_second/ppermute | solution.py:43
  342.2 19.9 %collective-permute-start.91 = (bf16[256,768]{1,0:T(8,128)(2,1)S(1)}, bf16[256,768]{1,0:T(8,128)(2,1)S(1)}, u32[]{:S(2)}, u32[]{:S(2)}) collective-permute-start(bf16[256,768]{1,0:T(8,128)(2,1)S(1)} %add_parts.43.refs_6_), channel_id=1, source_target_pairs={{0,8},{8,0},{16,24},{24,16},{1,9},{9,1},{17,25},{25,17},{2,10},{10... | collective-permute-start | bytes 1179656 | tf_op jit(solution)/shard_map/sum_k3_second/ppermute | solution.py:39
  363.2 41.0 %collective-permute-start.113 = (bf16[96,2304]{1,0:T(8,128)(2,1)S(1)}, bf16[96,2304]{1,0:T(8,128)(2,1)}, u32[]{:S(2)}, u32[]{:S(2)}) collective-permute-start(bf16[96,2304]{1,0:T(8,128)(2,1)S(1)} %total.5.refs_9_), channel_id=1, source_target_pairs={{0,24},{8,16},{16,8},{24,0},{1,25},{9,17},{17,9},{25,1},{2,26},{10... | collective-permute-start | bytes 1327112 | tf_op jit(solution)/shard_map/place_layer1/ppermute | solution.py:148
  365.8 20.5 %collective-permute-start.96 = (bf16[512,192]{1,0:T(8,128)(2,1)S(1)}, bf16[512,192]{1,0:T(8,128)(2,1)S(1)}, u32[]{:S(2)}, u32[]{:S(2)}) collective-permute-start(bf16[512,192]{1,0:T(8,128)(2,1)S(1)} %get-tuple-element.228), channel_id=1, source_target_pairs={{0,8},{8,0},{16,24},{24,16},{1,9},{9,1},{17,25},{25,17},{2,10},{10... | collective-permute-start | bytes 589832 | tf_op jit(solution)/shard_map/sum_back0/ppermute | solution.py:39
  372.5 31.7 %collective-permute-start.109 = (bf16[96,1536]{1,0:T(8,128)(2,1)S(1)}, bf16[96,1536]{1,0:T(8,128)(2,1)}, u32[]{:S(2)}, u32[]{:S(2)}) collective-permute-start(bf16[96,1536]{1,0:T(8,128)(2,1)S(1)} %total.4.refs_5_), channel_id=1, source_target_pairs={{0,24},{8,16},{16,8},{24,0},{1,25},{9,17},{17,9},{25,1},{2,26},{10... | collective-permute-start | bytes 884744 | tf_op jit(solution)/shard_map/place_layer0/ppermute | solution.py:148
  374.4 29.7 %collective-permute-start.101 = (bf16[96,896]{1,0:T(8,128)(2,1)S(1)}, bf16[96,896]{1,0:T(8,128)(2,1)}, u32[]{:S(2)}, u32[]{:S(2)}) collective-permute-start(bf16[96,896]{1,0:T(8,128)(2,1)S(1)} %total.3.refs_1_), channel_id=1, source_target_pairs={{0,8},{8,0},{16,24},{24,16},{1,9},{9,1},{17,25},{25,17},{2,10},{10... | collective-permute-start | bytes 516104 | tf_op jit(solution)/shard_map/place_layer0/ppermute | solution.py:148
  376.8 27.4 %collective-permute-start.102 = (bf16[96,896]{1,0:T(8,128)(2,1)S(1)}, bf16[96,896]{1,0:T(8,128)(2,1)}, u32[]{:S(2)}, u32[]{:S(2)}) collective-permute-start(bf16[96,896]{1,0:T(8,128)(2,1)S(1)} %total.3.refs_1_), channel_id=1, source_target_pairs={{0,16},{8,24},{16,0},{24,8},{1,17},{9,25},{17,1},{25,9},{2,18},{10... | collective-permute-start | bytes 516104 | tf_op jit(solution)/shard_map/place_layer0/ppermute | solution.py:148
  387.0 17.2 %collective-permute-start.103 = (bf16[96,896]{1,0:T(8,128)(2,1)S(1)}, bf16[96,896]{1,0:T(8,128)(2,1)}, u32[]{:S(2)}, u32[]{:S(2)}) collective-permute-start(bf16[96,896]{1,0:T(8,128)(2,1)S(1)} %total.3.refs_1_), channel_id=1, source_target_pairs={{0,24},{8,16},{16,8},{24,0},{1,25},{9,17},{17,9},{25,1},{2,26},{10... | collective-permute-start | bytes 516104 | tf_op jit(solution)/shard_map/place_layer0/ppermute | solution.py:148
  (121 other events, 1609.3 us)

commit v3 on v2

--- a/solution.py
+++ b/solution.py
@@ -57,24 +57,13 @@
     return lax.optimization_barrier((value, *others))[0] if others else value
 
 
-def sum_parts(name, part_0, part_1, beside=None, begun=(), later=()):
+def sum_parts(name, part_0, part_1, begun=(), later=(), beside=None):
     with jax.named_scope(f"sum_{name}_first"):
         here_0, here_1 = swap_x(part_0), swap_y(put_after(part_1, *begun))
     with jax.named_scope(f"sum_{name}_second"):
         half_0, half_1 = add_parts(part_0, here_0), add_parts(part_1, here_1, later)
-        there_0, there_1 = swap_y(half_0), swap_x(half_1)
-    done = beside((half_0, half_1)) if beside is not None else ()
-    return (half_0, there_0, half_1, there_1), done
-
-
-def sum_own_cols(name, place, sent, kept):
-    wide = kept.shape[1] // 2
-    with jax.named_scope(f"sum_{name}"):
-        came = swap_y(sent)
-        sent, kept = call(
-            half_kernel, "own_half", [place, kept, came], [shaped((TOK, wide), bf16)] * 2
-        )
-        return kept, swap_x(sent)
+        sums = (half_0, swap_y(half_0), half_1, swap_x(half_1))
+    return sums, () if beside is None else beside((half_0, half_1))
 
 
 def sum_in_steps(name, part_0, part_1):
@@ -89,6 +78,16 @@
     return sums, after
 
 
+def sum_own_cols(name, place, sent, kept):
+    wide = kept.shape[1] // 2
+    with jax.named_scope(f"sum_{name}"):
+        came = swap_y(sent)
+        sent, kept = call(
+            half_kernel, "own_half", [place, kept, came], [shaped((TOK, wide), bf16)] * 2
+        )
+        return kept, swap_x(sent)
+
+
 def pass_z(block, step, first=0):
     count = lax.axis_size("batch")
     last = count // 2 - 1
@@ -97,24 +96,35 @@
     return lax.ppermute(block, "batch", pairs)
 
 
+def pass_sums(block, step, turn):
+    count = lax.axis_size("batch")
+    last = count // 2 - 1
+    sources = range(turn) if step > 0 else range(last + 1 - turn, last + 1)
+    pairs = [(2 * z + c, 2 * (z + step) + c) for z in sources for c in range(2)]
+    return lax.ppermute(block, "batch", pairs)
+
+
 def pass_ends(block):
     pairs = [(2 * z + c, 2 * t + c) for z, t in ((2, 3), (1, 0)) for c in range(2)]
     return lax.ppermute(block, "batch", pairs)
 
 
-def gather_rows(place, block, at_once=False, then=(), onward=()):
+def gather_rows(place, block, way, then=()):
     places = lax.axis_size("batch") // 2
     apart = block.shape[0] % 16 == 0
-    if places == 4 and apart and not at_once:
+    if places == 4 and apart and way == "line":
         left, right = pass_z(block, 1), pass_z(block, -1)
-        left_2 = pass_z(put_after(left, *onward), 1, 1)
-        right_2 = pass_z(put_after(right, *onward), -1, 1)
+        left_2, right_2 = pass_z(left, 1, 1), pass_z(right, -1, 1)
         second = call(
             second_kernel, "second", [place, left_2, right_2], [shaped(block.shape, bf16)]
         )[0]
         own, kind = [block, left, right, second, pass_ends(second)], "line"
     else:
-        own, kind = [block] + [shift_z(block, d) for d in range(1, places)], "circle"
+        found = {0: block, 1: shift_z(block, 1), places - 1: shift_z(block, places - 1)}
+        for d in range(2, places - 1):
+            before = (found[d - 1],) if way == "twice" else ()
+            found[d] = shift_z(put_after(block, *before), d)
+        own, kind = [found[d] for d in range(places)], "circle"
     other = [swap_core(put_after(chunk, *then)) for chunk in own]
     if apart:
         return own + other, kind
@@ -126,11 +136,14 @@
     return [whole.reshape(places * 2 * block.shape[0], block.shape[1])], "whole"
 
 
+def near(found):
+    chunks, kind = found
+    return () if kind == "whole" else (chunks[1], chunks[len(chunks) // 2 - 1])
+
+
 def landed(found):
     chunks, kind = found
-    if kind == "whole":
-        return ()
-    return tuple(chunks[1:] if kind == "circle" else chunks[4:5])
+    return () if kind == "whole" else tuple(chunks[1 : len(chunks) // 2])
 
 
 def steps_of(found):
@@ -138,15 +151,10 @@
     return [(chunks[i],) for i in (1, 3, 4)] if kind == "line" else [(), (), ()]
 
 
-def gather_section(block, in_turn=False, after=()):
-    count = lax.axis_size("section")
-    found = [block]
-    for k in range(1, count):
-        if in_turn:
-            after = (*after, *found[1:][-1:])
-        pairs = [(i, i ^ k) for i in range(count)]
-        found.append(lax.ppermute(put_after(block, *after), "section", pairs))
-    return found
+def gather_section(block):
+    over_x = swap_x(block)
+    over_y = swap_y(put_after(block, over_x))
+    return [block, over_x, over_y, swap_y(put_after(over_x, over_y))]
 
 
 def dot_nn(left, right):
@@ -223,9 +231,12 @@
     return slice(row * ROW, (row + 1) * ROW)
 
 
+def summed_row(sums, row):
+    return sums[2 * row][...].astype(f32) + sums[2 * row + 1][...].astype(f32)
+
+
 def norm_in(layer, gain_at, shift_at, bias_at, base_ref, sums, small_ref, row):
-    half, other = sums[2 * row], sums[2 * row + 1]
-    branch = half[...].astype(f32) + other[...].astype(f32) + small_at(small_ref, layer, bias_at)
+    branch = summed_row(sums, row) + small_at(small_ref, layer, bias_at)
     hat, rate = standard(base_ref[rows_of(row), :].astype(f32) + branch)
     out = hat * small_at(small_ref, layer, gain_at) + small_at(small_ref, layer, shift_at)
     return out.astype(bf16), hat, rate
@@ -409,10 +420,7 @@
 
 
 def arrived_grad(base_ref, sums, row):
-    grad = base_ref[rows_of(row), :] + (
-        sums[2 * row][...].astype(f32) + sums[2 * row + 1][...].astype(f32)
-    )
-    return grad.astype(bf16)
+    return (base_ref[rows_of(row), :] + summed_row(sums, row)).astype(bf16)
 
 
 def feed_back_kernel(layer, last, place_ref, small_ref, weights_ref, hidden_ref, base_ref, *refs):
@@ -431,8 +439,8 @@
         here = rows_of(row)
         if last:
             out, hat, rate = norm_in(layer, AT_G2, AT_S2, AT_B2, base_ref, sums, small_ref, row)
-            part = y_ref.shape[1]
-            y_ref[here, :] = own_cols(out, place_ref[0], part)
+            part = y_ref.shape[0]
+            y_ref[:, here] = own_cols(out.astype(f32), place_ref[0], part).T.astype(bf16)
             pooled_ref[row] = own_cols(pooled_of(lens_ref, row, out), place_ref[0], part)
             grad_out = cot_ref[here, :].astype(f32)
         else:
@@ -462,8 +470,9 @@
 def attention_back_kernel(layer, small_ref, place_ref, weights_ref, base_ref, *refs):
     sums, hat_ref, rate_ref = refs[:4], refs[4], refs[5]
     q_ref, k_ref, v_ref, prob_ref = refs[6:10]
-    part_refs = refs[10:12]
-    carry_ref, branch_ref, grad_proj_ref, sums_ref, bias_ref = refs[12:]
+    refs = refs[10:]
+    part_refs = refs[:2]
+    carry_ref, branch_ref, grad_proj_ref, sums_ref, bias_ref = refs[2:]
     part = q_ref.shape[1]
     lane = lax.broadcasted_iota(jnp.int32, (1, part), 1)
     gain = small_at(small_ref, layer, AT_G1)
@@ -522,9 +531,9 @@
 
 
 def input_kernel(place_ref, base_ref, kept_ref, came_ref, out_ref):
-    base = own_cols(base_ref[...], place_ref[0], out_ref.shape[1])
+    base = own_cols(base_ref[...], place_ref[0], out_ref.shape[0])
     total = kept_ref[...].astype(f32) + came_ref[...].astype(f32)
-    out_ref[...] = (base + total).astype(bf16)
+    out_ref[...] = (base + total).T.astype(bf16)
 
 
 def pack_kernel(rows, place_ref, *refs):
@@ -575,27 +584,39 @@
             out[z] = whole_ref[pl.ds(start, rows), :]
 
 
-def chip_kernel(place_ref, mine_ref, came_ref, *refs):
+def line_kernel(turn, place_ref, mine_ref, came_ref, *refs):
     places = mine_ref.shape[0]
     z = place_ref[1] // 2
-    for d, out in enumerate(refs):
-        owner = lax.rem(z + d, places)
-        out[...] = add_low(mine_ref[owner], came_ref[owner])
-
-
-def total_kernel(*refs):
-    total = refs[0][...].astype(f32)
-    for ref in refs[1:-1]:
-        total = total + ref[...].astype(f32)
-    refs[-1][...] = total.astype(bf16)
-
-
-def place_kernel(copies, place_ref, *refs):
-    out_ref, small_ref, vector_ref = refs[-3:]
+
+    def rows_for(chip):
+        return mine_ref[chip].astype(f32) + came_ref[chip].astype(f32)
+
+    outs = refs if turn == 1 else refs[2:]
+    right = rows_for(jnp.minimum(z + places - turn, places - 1))
+    left = rows_for(jnp.maximum(z - places + turn, 0))
+    if turn > 1:
+        right, left = right + refs[0][...].astype(f32), left + refs[1][...].astype(f32)
+    outs[0][...], outs[1][...] = right.astype(bf16), left.astype(bf16)
+    if turn == places - 1:
+        outs[2][...] = rows_for(z).astype(bf16)
+
+
+def total_kernel(counts, *refs):
+    out_ref, at = refs[-1], 0
+    for count in counts:
+        total = refs[0][...].astype(f32)
+        for ref in refs[1:count]:
+            total = total + ref[...].astype(f32)
+        refs = refs[count:]
+        out_ref[:, at : at + total.shape[1]] = total.astype(bf16)
+        at += total.shape[1]
+
+
+def place_kernel(layer, count, attn_at, feed_at, place_ref, *refs):
+    blocks, refs = refs[:SECTIONS], refs[SECTIONS:]
+    out_ref, buffer, sems = refs[count:]
     section = place_ref[0]
     part = D // SECTIONS
-    rows = out_ref.buffer.shape[1]
-    share = small_ref.shape[1]
 
     def owned(group, start, stop):
         found = []
@@ -606,31 +627,40 @@
             found.append(value.astype(f32))
         return found
 
-    groups = [refs[i * SECTIONS : (i + 1) * SECTIONS] for i in range(3)]
+    copies = []
+
+    def push(start, stop):
+        there = out_ref.at[layer, :, start:stop]
+        copies.append(pltpu.make_async_copy(buffer.at[:, start:stop], there, sems.at[len(copies)]))
+        copies[-1].start()
+
+    ffn = owned(blocks, feed_at, feed_at + 2 * D)
+    for j in range(2):
+        for slot, block in enumerate(ffn):
+            start = (4 + 4 * j + slot) * D
+            buffer[:, start : start + D] = block[:, j * D : (j + 1) * D]
+        push((4 + 4 * j) * D, (8 + 4 * j) * D)
+    attn = owned(blocks, attn_at, attn_at + D)
+    for j in range(4):
+        columns = [a[:, j * part : (j + 1) * part] for a in attn]
+        buffer[:, j * D : (j + 1) * D] = jnp.concatenate(columns, axis=1)
+    push(0, 4 * D)
     for copy in copies:
         copy.wait()
-    for layer in reversed(range(LAYERS)):
-        if layer > 0:
-            attn, ffn = owned(groups[2], 0, D), owned(groups[2], D, 3 * D)
-        else:
-            attn, ffn = owned(groups[0], 0, D), owned(groups[1], 0, 2 * D)
-        for j in range(4):
-            columns = [a[:, j * part : (j + 1) * part] for a in attn]
-            out_ref[layer, :, j * D : (j + 1) * D] = jnp.concatenate(columns, axis=1)
-        for slot, block in enumerate(ffn):
-            for j in range(2):
-                start = (4 + 4 * j + slot) * D
-                out_ref[layer, :, start : start + D] = block[:, j * D : (j + 1) * D]
-        out_ref.push(layer)
+
+
+def small_kernel(place_ref, *refs):
+    blocks, (small_ref, vector_ref) = refs[:SECTIONS], refs[SECTIONS:]
+    rows, share = blocks[0].shape[0], small_ref.shape[1]
     for layer in range(LAYERS):
         slot = rows // LAYERS
         at, count = layer * slot, min(16, slot)
         total = jnp.zeros((count, 128), f32)
-        for k in range(SECTIONS):
-            total = total + refs[k][at : at + count, 4 * part :].astype(f32)
-        for i in range(vector_ref.shape[1] // 128):
+        for block in blocks:
+            total = total + block[at : at + count, 3 * D :].astype(f32)
+        wide = vector_ref.shape[1]
+        for i in range(wide // 128):
             vector_ref[:, i * 128 : (i + 1) * 128] = total[i : i + 1, :]
-        wide = vector_ref.shape[1]
         inside = lax.rem(place_ref[1] * share, 128)
         moved = pltpu.roll(jnp.broadcast_to(vector_ref[...], (8, wide)), wide - inside, 1)
         small_ref[layer : layer + 1, :] = moved[:1, :share]
@@ -683,20 +713,6 @@
 class Raw:
     def __init__(self, value):
         self.value = value
-
-
-class Leaving:
-    def __init__(self, target, buffer, sems):
-        self.buffer, self.target, self.sems, self.copies = buffer, target, sems, []
-
-    def __setitem__(self, index, value):
-        self.buffer[index] = value
-
-    def push(self, part):
-        sem = self.sems.at[len(self.copies)]
-        copy = pltpu.make_async_copy(self.buffer.at[part], self.target.at[part], sem)
-        copy.start()
-        self.copies.append(copy)
 
 
 def call(body, name, operands, outs, after=(), scratch=(), limit=12, aliases=None):
@@ -803,12 +819,12 @@
     )
 
 
-def grad_over_batch(place, rows, pairs, extra=None, after=(), begin=(), in_turn=False):
+def grad_over_batch(place, rows, pairs, extra=None, begin=()):
     places = lax.axis_size("batch") // 2
     wide = sum(right.shape[1] for _, right in pairs)
     cols = wide + (0 if extra is None else extra.shape[1])
     chunk = shaped((rows, cols), bf16)
-    if rows % 16 == 0:
+    if places == 4 and rows % 16 == 0:
         mine, other = call(
             partial(grad_kernel, rows, len(pairs)),
             "grad",
@@ -817,28 +833,43 @@
             begin,
             [pltpu.VMEM((D, cols), bf16)],
         )
-        chunks = call(
-            chip_kernel, "chip_sum", [place, mine, swap_core(other)], [chunk] * places, after
-        )
-    else:
-        me = lax.axis_index("batch")
-        z, core = me // 2, me % 2
-        block = jnp.concatenate([dot_tn(l, r).astype(bf16) for l, r in pairs], axis=1)
-        if extra is not None:
-            block = jnp.concatenate([block, extra], axis=1)
-        parted = block.reshape(places, 2, rows, cols)
-        mine = lax.dynamic_index_in_dim(parted, core, 1, keepdims=False)
-        other = lax.dynamic_index_in_dim(parted, 1 - core, 1, keepdims=False)
-        chip = add_low(mine, swap_core(other))
-        chunks = [
-            lax.dynamic_index_in_dim(chip, (z + d) % places, 0, keepdims=False)
-            for d in range(places)
-        ]
-    came = {}
-    for d in sorted(range(1, places), key=lambda d: min(d, places - d)):
-        came[d] = shift_z(put_after(chunks[d], *(list(came.values())[-1:] if in_turn else ())), d)
-    total = call(total_kernel, "total", [chunks[0], *came.values()], [chunk])[0]
-    return total, (*came.values(), chunks[0])
+        came, arrived, shown = swap_core(other), (), []
+        for turn in range(1, places):
+            sent = call(
+                partial(line_kernel, turn),
+                "line_sums",
+                [place, mine, came, *arrived],
+                [chunk] * (3 if turn == places - 1 else 2),
+            )
+            arrived = (pass_sums(sent[0], 1, turn), pass_sums(sent[1], -1, turn))
+            shown.append(arrived)
+        return [sent[2], *arrived], (*shown, (sent[0],))
+    me = lax.axis_index("batch")
+    z, core = me // 2, me % 2
+    block = jnp.concatenate([dot_tn(l, r).astype(bf16) for l, r in pairs], axis=1)
+    if extra is not None:
+        block = jnp.concatenate([block, extra], axis=1)
+    parted = block.reshape(places, 2, rows, cols)
+    mine = lax.dynamic_index_in_dim(parted, core, 1, keepdims=False)
+    other = lax.dynamic_index_in_dim(parted, 1 - core, 1, keepdims=False)
+    chip = add_low(mine, swap_core(other))
+    chunks = [
+        lax.dynamic_index_in_dim(chip, (z + d) % places, 0, keepdims=False) for d in range(places)
+    ]
+    came = [shift_z(chunks[d], d) for d in range(1, places)]
+    return [chunks[0], *came], [()] * 4
+
+
+def total_of(groups, after=()):
+    rows = groups[0][0].shape[0]
+    cols = sum(group[0].shape[1] for group in groups)
+    return call(
+        partial(total_kernel, [len(group) for group in groups]),
+        "total",
+        [block for group in groups for block in group],
+        [shaped((rows, cols), bf16)],
+        after,
+    )[0]
 
 
 def on_device(tokens, key_tokens, cotangent, lengths, query_mats, query_small, key_mats, key_small):
@@ -847,87 +878,75 @@
     rows = query_mats.shape[1]
     place = jnp.stack([section, batch]).astype(jnp.int32)
     shared_q, shared_k = (place, lengths, query_small), (place, lengths, key_small)
-    own_out = shaped((TOK, part), bf16)
+    own_turned = shaped((part, TOK), bf16)
     pooled_out = shaped((MICRO, CROPS, part), f32)
 
     units = [
         [("query", 0, "attention")],
-        [("query", 0, "feed"), ("query", 1, "attention")],
-        [("query", 1, "feed"), ("key", 0, "attention")],
-        [("key", 0, "feed"), ("key", 1, "attention")],
-        [("key", 1, "feed")],
+        [("query", 0, "feed")],
+        [("query", 1, "attention")],
+        [("query", 1, "feed")],
+        [("key", 0, "attention"), ("key", 0, "feed")],
+        [("key", 1, "attention"), ("key", 1, "feed")],
     ]
     blocks = take(place, query_mats, key_mats, units[:1])
     blocks += take(place, query_mats, key_mats, units[1:], (blocks[0],))
     both = (query_mats, key_mats, query_small, key_small)
     mats_step, early_step = momentum(0, *both, (), (blocks[1],))
-    with jax.named_scope("weights_unit_0"):
-        chunks = [gather_rows(place, blocks[0], True, (early_step,))]
-    attn_q = [(chunks[0], 0)]
-    found_0 = attention(0, tokens, None, shared_q, attn_q[0], True, "q")
-    for n in range(1, len(units)):
+
+    def unit(n, way, *after):
         with jax.named_scope(f"weights_unit_{n}"):
-            before = landed(chunks[-1])
-            if n == 1:
-                before = (*chunks[0][0][1 : len(chunks[0][0]) // 2], early_step)
-            block = put_after(blocks[n], *before)
-            chunks.append(gather_rows(place, block, onward=found_0[:1] if n == 1 else ()))
-    attn_q.append((chunks[1], 2 * D))
-    feed_q = [(chunks[1], 0), (chunks[2], 0)]
-    attn_k = [(chunks[2], 2 * D), (chunks[3], 2 * D)]
-    feed_k = [(chunks[3], 0), (chunks[4], 0)]
-
-    def key_encoder():
-        after = yield
-        inputs, sums = key_tokens, None
-        for layer in range(LAYERS):
-            found = attention(layer, inputs, sums, shared_k, attn_k[layer], False, "k", after)
-            inputs = found[2] if layer > 0 else inputs
-            sums, after = yield from sum_in_steps(f"k{2 * layer}", *found[:2])
-            p0, p1, inputs = feed(layer, inputs, sums, shared_k, feed_k[layer], False, "k", after)
-            sums, after = yield from sum_in_steps(f"k{2 * layer + 1}", p0, p1)
-        key_end.append((inputs, sums))
-        yield ()
-
-    key_end = []
-    steps = key_encoder()
-    next(steps)
-
-    def beside(arrays):
-        return () if key_end else steps.send(arrays)
-
-    lines = [steps_of(found) for found in chunks[1:]]
+            then = (early_step,) if n == 0 else ()
+            return gather_rows(place, put_after(blocks[n], *after), way, then)
+
+    chunks = [unit(0, "once")]
+    chunks.append(unit(1, "twice", *landed(chunks[0]), early_step))
+    for n in range(2, 4):
+        chunks.append(unit(n, "twice", *near(chunks[-1])))
+    for n in range(4, 6):
+        chunks.append(unit(n, "line", *landed(chunks[-1])[-1:]))
+    lines = [steps_of(found) for found in chunks[4:]]
+    attn_q, feed_q = [(chunks[0], 0), (chunks[2], 0)], [(chunks[1], 0), (chunks[3], 0)]
 
     kept, weights = [], []
     inputs, sums = tokens, None
-    done = ()
-    gates = [((), ()), ((), lines[1][0]), (lines[1][1], lines[1][2]), (lines[2][0], lines[2][1])]
     for layer in range(LAYERS):
-        found = found_0
-        if layer > 0:
-            found = attention(layer, inputs, sums, shared_q, attn_q[layer], True, "q", done)
+        found = attention(layer, inputs, sums, shared_q, attn_q[layer], True, "q")
         parts, found, attn_w = found[:2], found[2:-1], found[-1]
         if layer > 0:
             inputs, hat, rate = found[:3]
             kept[-1] += (hat, rate)
             found = found[3:]
-        along = beside if layer > 0 else None
-        sums, done = sum_parts(f"q{2 * layer}", *parts, along, *gates[2 * layer])
+        sums, _ = sum_parts(f"q{2 * layer}", *parts)
         attn_in, attn_kept = inputs, tuple(found)
         p0, p1, inputs, hat, rate, hidden, active, feed_w = feed(
-            layer, inputs, sums, shared_q, feed_q[layer], True, "q", done
+            layer, inputs, sums, shared_q, feed_q[layer], True, "q"
         )
-        sums, done = sum_parts(f"q{2 * layer + 1}", p0, p1, along, *gates[2 * layer + 1])
+        gates = ((), lines[0][0]) if layer > 0 else ()
+        sums, _ = sum_parts(f"q{2 * layer + 1}", p0, p1, *gates)
         if chunks[0][1] == "whole":
-            attn_w, feed_w = (
-                found[0][:, at : at + wide]
-                for ((found, _), at), wide in ((attn_q[layer], D), (feed_q[layer], 2 * D))
-            )
+            attn_w, feed_w = attn_q[layer][0][0][0], feed_q[layer][0][0][0]
         weights.append((attn_w, feed_w))
         kept.append((attn_in, attn_kept, hat, rate, inputs, hidden, active))
 
+    attn_k, feed_k = [(chunks[4], 0), (chunks[5], 0)], [(chunks[4], D), (chunks[5], D)]
+
+    def key_attention(layer, inputs, sums, after):
+        return attention(layer, inputs, sums, shared_k, attn_k[layer], False, "k", after)
+
+    def key_feed(layer, inputs, sums, after):
+        return feed(layer, inputs, sums, shared_k, feed_k[layer], False, "k", after)
+
+    def key_steps():
+        after = yield
+        sums, after = yield from sum_in_steps("k0", *key_attention(0, key_tokens, None, after))
+        found.append(key_feed(0, key_tokens, sums, after))
+        yield found[0][:1]
+
+    found, steps = [], key_steps()
+    next(steps)
     small_parts = [None] * LAYERS
-    sums_out, turn = shaped((3, D), f32), lines[3][2]
+    sums_out, turn, done = shaped((3, D), f32), [()] * 4, ()
     for layer in reversed(range(LAYERS)):
         attn_in, attn_kept, hat1, rate1, feed_in, hidden, active, *rest = kept[layer]
         attn_w, feed_w = weights[layer]
@@ -935,7 +954,7 @@
         operands = [feed_in, *sums, cotangent, lengths] if last else [carry, *sums, *rest]
         outs = [*part_out, wide_out, rows_out, rows_out, sums_out, shaped((1, D), f32)]
         if last:
-            outs += [own_out, pooled_out]
+            outs += [own_turned, pooled_out]
         p0, p1, carry, branch, grad_hidden, sums_2, db1, *tail = call(
             partial(feed_back_kernel, layer, last),
             f"feed_back{layer}",
@@ -945,41 +964,34 @@
         )
         if last:
             out_q, pooled_q = tail
-        gate = (lines[2][2], lines[3][0]) if last else (turn[:1], turn[1:2])
-        sums, done = sum_parts(f"back{2 * layer + 1}", p0, p1, beside, *gate)
+        gates = (lines[0][1], lines[0][2]) if last else (lines[1][2], turn[0])
+        sums, done = sum_parts(f"back{2 * layer + 1}", p0, p1, *gates, steps.send)
         feed_pairs = [(feed_in, grad_hidden), (branch, active)]
-        if layer == 0:
-            with jax.named_scope("grad_feed0"):
-                total_feed, turn_feed = grad_over_batch(
-                    place, rows, feed_pairs, None, turn[1:2], sums[::2]
-                )
-            done = (*done, turn_feed[-1])
         q, k, v, mixed, prob = attn_kept
         p0, p1, carry, branch, grad_proj, sums_1, dbv = call(
             partial(attention_back_kernel, layer),
             f"attention_back{layer}",
             [query_small, place, attn_w, carry, *sums, hat1, rate1, q, k, v, prob],
             [
-                *(part_out if layer > 0 else [shaped((TOK, D // 2), bf16)] * 2),
+                *(part_out if last else [shaped((TOK, D // 2), bf16)] * 2),
                 wide_out,
                 rows_out,
                 shaped((TOK, 3 * part), bf16),
                 sums_out,
                 shaped((1, part), f32),
             ],
-            done,
+            (*done, *turn[1]),
         )
-        if layer > 0:
-            sums, done = sum_parts(f"back{2 * layer}", p0, p1, beside, *lines[3][1:])
+        small_parts[layer] = [sums_1, dbv, sums_2, db1]
+        attn_pairs = [(attn_in, grad_proj), (branch, mixed)]
+        if last:
+            sums, done = sum_parts(f"back{2 * layer}", p0, p1, *lines[1][:2], steps.send)
+            with jax.named_scope("grad_layer1"):
+                layer_sums, turn = grad_over_batch(
+                    place, rows, attn_pairs + feed_pairs, None, sums[::2]
+                )
         else:
             sums = sum_own_cols("back0", place, p0, p1)
-        small_parts[layer] = [sums_1, dbv, sums_2, db1]
-        attn_pairs = [(attn_in, grad_proj), (branch, mixed)]
-        if layer > 0:
-            with jax.named_scope("grad_layer1"):
-                total_layer, turn = grad_over_batch(
-                    place, rows, attn_pairs + feed_pairs, None, turn, sums[::2], True
-                )
     (extra,) = call(
         partial(pack_kernel, rows),
         "pack_small",
@@ -987,64 +999,55 @@
         [shaped((D, 128), bf16)],
         scratch=[pltpu.VMEM((1, SMALL), f32), pltpu.VMEM((72, 128), f32)],
     )
-    with jax.named_scope("grad_attention0"):
-        total_attn, turn_attn = grad_over_batch(place, rows, attn_pairs, extra)
+    with jax.named_scope("grad_layer0"):
+        sums_0, turn_0 = grad_over_batch(place, rows, feed_pairs + attn_pairs, extra)
     with jax.named_scope("place_layer1"):
-        got_layer = gather_section(total_layer, True, turn_attn[-1:])
-    mats_step, small_step = momentum(1, *both, (mats_step,), turn_attn[-1:])
+        got_1 = gather_section(total_of([layer_sums]))
+
+    k0, k1, inputs_k = found[0]
+    mats_step, small_step = momentum(1, *both, (mats_step,), (p0,))
+    sums_k, _ = sum_parts("k1", k0, k1, (), (*turn[2], *turn_0[3]))
+    k0, k1, inputs_k = key_attention(1, inputs_k, sums_k, (*turn_0[0], got_1[1], sums[0]))
+    sums_k, _ = sum_parts("k2", k0, k1, (), (*turn_0[1], got_1[2]))
+    (input_grad,) = call(input_kernel, "input_grad", [place, carry, *sums], [own_turned])
+    k0, k1, inputs_k = key_feed(1, inputs_k, sums_k, (*turn_0[2], got_1[3], input_grad))
     with jax.named_scope("place_layer0"):
-        got_feed = gather_section(total_feed)
-        got_attn = gather_section(total_attn)
-    while not key_end:
-        beside(())
-    inputs_k, sums_k = key_end[0]
+        got_0 = gather_section(total_of([sums_0]))
+    sums_k, _ = sum_parts("k3", k0, k1)
     (pooled_k,) = call(
         partial(last_kernel, LAYERS - 1),
         "last_k",
         [place, lengths, key_small, inputs_k, *sums_k],
         [pooled_out],
     )
-    (input_grad,) = call(input_kernel, "input_grad", [place, carry, *sums], [own_out])
-
     share = SMALL // lax.axis_size("batch")
     mats_shape = (LAYERS, rows, 12 * D)
     touched = -(-(share + 127) // 128) * 128
 
-    gathered = [*got_attn, *got_feed, *got_layer]
-
-    def place_body(place_ref, *refs):
-        sources, refs = refs[: len(gathered)], refs[len(gathered) :]
-        out_ref, small_ref, buffer, vector_ref, sems, in_sems, *held = refs
-        copies = [
-            pltpu.make_async_copy(source, there, in_sems.at[i])
-            for i, (source, there) in enumerate(zip(sources, held))
-        ]
-        for copy in copies:
-            copy.start()
-        out = Leaving(out_ref, buffer, sems)
-        place_kernel(copies, place_ref, *held, out, small_ref, vector_ref)
-        for copy in out.copies:
-            copy.wait()
-
-    grad_mats, grad_small = call(
-        place_body,
-        "place_grads",
-        [place, *map(Raw, gathered)],
-        [Raw(shaped(mats_shape, f32)), shaped((LAYERS, share), f32)],
-        scratch=[
-            pltpu.VMEM(mats_shape, f32),
-            pltpu.VMEM((1, touched), f32),
-            pltpu.SemaphoreType.DMA((LAYERS,)),
-            pltpu.SemaphoreType.DMA((len(gathered),)),
-            *(pltpu.VMEM(block.shape, bf16) for block in gathered),
-        ],
-        limit=58,
+    grad_mats = ()
+    for layer, blocks in ((1, got_1), (0, got_0)):
+        attn_at, feed_at = (0, D) if layer > 0 else (2 * D, 0)
+        grad_mats = call(
+            partial(place_kernel, layer, len(grad_mats), attn_at, feed_at),
+            f"place_grads{layer}",
+            [place, *blocks, *map(Raw, grad_mats)],
+            [Raw(shaped(mats_shape, f32))],
+            scratch=[pltpu.VMEM((rows, 12 * D), f32), pltpu.SemaphoreType.DMA((3,))],
+            aliases={1 + len(blocks): 0} if grad_mats else {},
+        )
+    (grad_mats,) = grad_mats
+    (grad_small,) = call(
+        small_kernel,
+        "own_small",
+        [place, *got_0],
+        [shaped((LAYERS, share), f32)],
+        scratch=[pltpu.VMEM((1, touched), f32)],
     )
     return (
-        out_q,
+        out_q.T,
         pooled_q,
         pooled_k,
-        input_grad,
+        input_grad.T,
         grad_mats,
         grad_small,
         mats_step,

time: 420 us -> 403 us (0.960)
  the two profiles are of different devices: /device:TPU:0 before, /device:TPU:8 now
where the time goes in v3:
time: 403 us; the launch traced here: 396 us
  waiting for transfers between devices  164 us (41%)
  starting transfers between devices  136 us (34%)
  Pallas kernels  92.8 us (23%)
    pallas_call x57, Pallas kernels, call(): pl.pallas_call(kernel, name=name, in_specs=specs + [ANY] * len(after), ou...  92.8 us
    ppermute x27, waiting for transfers between devices, swap_y(): return lax.ppermute(block, 'section', [(0, 2), (2, 0), (1, 3), (3, 1)])  53 us
    ppermute x25, waiting for transfers between devices, swap_x(): return lax.ppermute(block, 'section', [(0, 1), (1, 0), (2, 3), (3, 2)])  45.6 us
    ppermute x27, starting transfers between devices, swap_y(): return lax.ppermute(block, 'section', [(0, 2), (2, 0), (1, 3), (3, 1)])  30.2 us
    ppermute x25, starting transfers between devices, swap_x(): return lax.ppermute(block, 'section', [(0, 1), (1, 0), (2, 3), (3, 2)])  27.4 us
    ppermute x12, starting transfers between devices, shift_z(): lax.ppermute(block, 'batch', [(i, (i + 2 * distance) % count) for i in ra...  26.6 us
    ppermute x12, starting transfers between devices, pass_sums(): return lax.ppermute(block, 'batch', pairs)  22.5 us
    ppermute x8, starting transfers between devices, pass_z(): return lax.ppermute(block, 'batch', pairs)  21.6 us
  transfers between devices with their start and end apart: 114, of which 44 were waited for; matrix products, arithmetic and copies ran while one was open for 0% of the time, Pallas kernels for 18%

profile of v3, /device:TPU:8, one launch (start us, length us, event | category | flops | bytes accessed | tf_op | source)
XLA Modules:
  0.0 395.9 jit_solution(6394691026427185648)
XLA Ops:
  8.7 4.6 %take.3 = (bf16[96,1536]{1,0:T(8,128)(2,1)}, bf16[96,768]{1,0:T(8,128)(2,1)}, bf16[96,1536]{1,0:T(8,128)(2,1)}, bf16[96,2304]{1,0:T(8,128)(2,1)}, bf16[96,2304]{1,0:T(8,128)(2,1)}) custom-call(s32[2]{0:T(128)} %pad_add_fusion.refs_0_.refs_1_, f32[2,96,9216]{2,1,0:T(8,128)} %refs_0_.7, f32[2,96,9216]{2,1,0:T(8,128)} %refs_1_.29, bf16[96,768]{1,0:T(8,128)(2,1)} %take.2.refs_3_), custom_call_target="tpu_custom_call" | custom-call | flops 1 | bytes 1 | tf_op jit(solution)/shard_map/take/pallas_call | solution.py:729
  13.4 6.7 %momentum0.1 = (f32[2,96,9216]{2,1,0:T(8,128)}, f32[2,8448]{1,0:T(2,128)}) custom-call(f32[2,96,9216]{2,1,0:T(8,128)} %refs_0_.7, f32[2,96,9216]{2,1,0:T(8,128)} %refs_1_.29, f32[2,8448]{1,0:T(2,128)} %refs_2_.21, f32[2,8448]{1,0:T(2,128)} %refs_3_.3, bf16[96,1536]{1,0:T(8,128)(2,1)} %get-tuple-element.144.refs_4_.refs_7_), custom_call_target="tpu_custom_call" | custom-call | flops 1 | bytes 1 | tf_op jit(solution)/shard_map/momentum0/pallas_call | solution.py:729
  32.0 4.8 %collective-permute-done.18.refs_1_ = bf16[256,768]{1,0:T(8,128)(2,1)S(1)} collective-permute-done((bf16[256,768]{1,0:T(8,128)(2,1)S(1)}, bf16[256,768]{1,0:T(8,128)(2,1)S(1)}, u32[]{:S(2)}, u32[]{:S(2)}) %collective-permute-start.18) | collective-permute-done | bytes 393248 | tf_op jit(solution)/shard_map/sum_q0_first/ppermute | solution.py:43
  40.2 4.8 %collective-permute-done.4.refs_10_ = bf16[96,1536]{1,0:T(8,128)(2,1)S(1)} collective-permute-done((bf16[96,1536]{1,0:T(8,128)(2,1)S(1)}, bf16[96,1536]{1,0:T(8,128)(2,1)S(1)}, u32[]{:S(2)}, u32[]{:S(2)}) %collective-permute-start.4) | collective-permute-done | bytes 294944 | tf_op jit(solution)/shard_map/weights_unit_1/ppermute | solution.py:53
  45.5 5.0 %collective-permute-done.20.refs_9_ = bf16[96,1536]{1,0:T(8,128)(2,1)S(1)} collective-permute-done((bf16[96,1536]{1,0:T(8,128)(2,1)S(1)}, bf16[96,1536]{1,0:T(8,128)(2,1)S(1)}, u32[]{:S(2)}, u32[]{:S(2)}) %collective-permute-start.20) | collective-permute-done | bytes 294944 | tf_op jit(solution)/shard_map/weights_unit_1/ppermute | solution.py:53
  59.9 6.2 %collective-permute-done.27.refs_1_ = bf16[256,768]{1,0:T(8,128)(2,1)S(1)} collective-permute-done((bf16[256,768]{1,0:T(8,128)(2,1)S(1)}, bf16[256,768]{1,0:T(8,128)(2,1)S(1)}, u32[]{:S(2)}, u32[]{:S(2)}) %collective-permute-start.27) | collective-permute-done | bytes 393248 | tf_op jit(solution)/shard_map/sum_q1_first/ppermute | solution.py:43
  71.9 6.1 %collective-permute-done.6.refs_5_ = bf16[96,768]{1,0:T(8,128)(2,1)S(1)} collective-permute-done((bf16[96,768]{1,0:T(8,128)(2,1)S(1)}, bf16[96,768]{1,0:T(8,128)(2,1)S(1)}, u32[]{:S(2)}, u32[]{:S(2)}) %collective-permute-start.6) | collective-permute-done | bytes 147488 | tf_op jit(solution)/shard_map/weights_unit_2/ppermute | solution.py:53
  88.5 8.7 %collective-permute-start.34 = (bf16[96,1536]{1,0:T(8,128)(2,1)S(1)}, bf16[96,1536]{1,0:T(8,128)(2,1)S(1)}, u32[]{:S(2)}, u32[]{:S(2)}) collective-permute-start(bf16[96,1536]{1,0:T(8,128)(2,1)S(1)} %copy-done.13), channel_id=1, source_target_pairs={{0,4},{1,5},{2,6},{3,7},{4,0},{5,1},{6,2},{7,3},{8,12},{9,13},{10,... | collective-permute-start | bytes 884744 | tf_op jit(solution)/shard_map/weights_unit_3/ppermute | solution.py:53
  108.8 6.9 %collective-permute-done.43.refs_2_.refs_4_.refs_8_ = bf16[96,2304]{1,0:T(8,128)(2,1)S(1)} collective-permute-done((bf16[96,2304]{1,0:T(8,128)(2,1)S(1)}, bf16[96,2304]{1,0:T(8,128)(2,1)S(1)}, u32[]{:S(2)}, u32[]{:S(2)}) %collective-permute-start.43) | collective-permute-done | bytes 442400 | tf_op jit(solution)/shard_map/weights_unit_4/ppermute | solution.py:96
  139.5 7.3 %collective-permute-done.44.refs_8_ = bf16[256,768]{1,0:T(8,128)(2,1)S(1)} collective-permute-done((bf16[256,768]{1,0:T(8,128)(2,1)S(1)}, bf16[256,768]{1,0:T(8,128)(2,1)S(1)}, u32[]{:S(2)}, u32[]{:S(2)}) %collective-permute-start.44) | collective-permute-done | bytes 393248 | tf_op jit(solution)/shard_map/sum_q3_second/ppermute | solution.py:39
  177.5 5.3 %attention_back1.1 = (bf16[256,768]{1,0:T(8,128)(2,1)S(1)}, bf16[256,768]{1,0:T(8,128)(2,1)S(1)}, f32[512,768]{1,0:T(8,128)S(1)}, bf16[512,768]{1,0:T(8,128)(2,1...) custom-call(f32[2,8448]{1,0:T(2,128)S(1)} %copy-done.1, s32[2]{0:T(128)S(1)} %copy-done.11, ...), custom_call_target="tpu_custom_call" | custom-call | flops 1 | bytes 1 | tf_op jit(solution)/shard_map/attention_back1/pallas_call | solution.py:729
  185.5 6.1 %collective-permute-done.69.refs_1_ = bf16[256,768]{1,0:T(8,128)(2,1)S(1)} collective-permute-done((bf16[256,768]{1,0:T(8,128)(2,1)S(1)}, bf16[256,768]{1,0:T(8,128)(2,1)S(1)}, u32[]{:S(2)}, u32[]{:S(2)}) %collective-permute-start.69) | collective-permute-done | bytes 393248 | tf_op jit(solution)/shard_map/sum_back2_first/ppermute | solution.py:39
  202.9 5.7 %collective-permute-done.72.refs_1_ = bf16[256,768]{1,0:T(8,128)(2,1)S(1)} collective-permute-done((bf16[256,768]{1,0:T(8,128)(2,1)S(1)}, bf16[256,768]{1,0:T(8,128)(2,1)S(1)}, u32[]{:S(2)}, u32[]{:S(2)}) %collective-permute-start.72) | collective-permute-done | bytes 393248 | tf_op jit(solution)/shard_map/sum_k0_first/ppermute | solution.py:43
  210.8 6.0 %collective-permute-done.75.refs_8_ = bf16[256,768]{1,0:T(8,128)(2,1)S(1)} collective-permute-done((bf16[256,768]{1,0:T(8,128)(2,1)S(1)}, bf16[256,768]{1,0:T(8,128)(2,1)S(1)}, u32[]{:S(2)}, u32[]{:S(2)}) %collective-permute-start.75) | collective-permute-done | bytes 393248 | tf_op jit(solution)/shard_map/sum_back2_second/ppermute | solution.py:39
  234.5 4.5 %collective-permute-done.73.refs_6_ = bf16[256,768]{1,0:T(8,128)(2,1)S(1)} collective-permute-done((bf16[256,768]{1,0:T(8,128)(2,1)S(1)}, bf16[256,768]{1,0:T(8,128)(2,1)S(1)}, u32[]{:S(2)}, u32[]{:S(2)}) %collective-permute-start.73) | collective-permute-done | bytes 393248 | tf_op jit(solution)/shard_map/sum_k0_second/ppermute | solution.py:39
  248.6 5.3 %attention_back0.1 = (bf16[512,384]{1,0:T(8,128)(2,1)S(1)}, bf16[512,384]{1,0:T(8,128)(2,1)S(1)}, f32[512,768]{1,0:T(8,128)S(1)}, bf16[512,768]{1,0:T(8,128)(2,1...) custom-call(f32[2,8448]{1,0:T(2,128)S(1)} %copy-done.1, s32[2]{0:T(128)S(1)} %copy-done.11, ...), custom_call_target="tpu_custom_call" | custom-call | flops 1 | bytes 1 | tf_op jit(solution)/shard_map/attention_back0/pallas_call | solution.py:729
  267.6 9.7 %collective-permute-done.91.refs_3_.refs_18_ = bf16[96,2432]{1,0:T(8,128)(2,1)S(1)} collective-permute-done((bf16[96,2432]{1,0:T(8,128)(2,1)S(1)}, bf16[96,2432]{1,0:T(8,128)(2,1)S(1)}, u32[]{:S(2)}, u32[]{:S(2)}) %collective-permute-start.91) | collective-permute-done | bytes 466976 | tf_op jit(solution)/shard_map/grad_layer0/ppermute | solution.py:104
  295.9 4.7 %collective-permute-done.93.refs_3_.refs_2_ = bf16[96,2432]{1,0:T(8,128)(2,1)S(1)} collective-permute-done((bf16[96,2432]{1,0:T(8,128)(2,1)S(1)}, bf16[96,2432]{1,0:T(8,128)(2,1)S(1)}, u32[]{:S(2)}, u32[]{:S(2)}) %collective-permute-start.93) | collective-permute-done | bytes 466976 | tf_op jit(solution)/shard_map/grad_layer0/ppermute | solution.py:104
  309.2 4.5 %collective-permute-done.96.refs_20_.refs_2_ = bf16[96,2304]{1,0:T(8,128)(2,1)S(1)} collective-permute-done((bf16[96,2304]{1,0:T(8,128)(2,1)S(1)}, bf16[96,2304]{1,0:T(8,128)(2,1)S(1)}, u32[]{:S(2)}, u32[]{:S(2)}) %collective-permute-start.96) | collective-permute-done | bytes 442400 | tf_op jit(solution)/shard_map/place_layer1/ppermute | solution.py:39
  318.0 5.0 %collective-permute-done.82.refs_15_ = bf16[256,768]{1,0:T(8,128)(2,1)S(1)} collective-permute-done((bf16[256,768]{1,0:T(8,128)(2,1)S(1)}, bf16[256,768]{1,0:T(8,128)(2,1)S(1)}, u32[]{:S(2)}, u32[]{:S(2)}) %collective-permute-start.82) | collective-permute-done | bytes 393248 | tf_op jit(solution)/shard_map/sum_k1_second/ppermute | solution.py:43
  333.9 7.1 %collective-permute-done.100.refs_1_ = bf16[256,768]{1,0:T(8,128)(2,1)S(1)} collective-permute-done((bf16[256,768]{1,0:T(8,128)(2,1)S(1)}, bf16[256,768]{1,0:T(8,128)(2,1)S(1)}, u32[]{:S(2)}, u32[]{:S(2)}) %collective-permute-start.100) | collective-permute-done | bytes 393248 | tf_op jit(solution)/shard_map/sum_k2_first/ppermute | solution.py:43
  348.7 9.0 %collective-permute-done.106.refs_3_ = bf16[512,192]{1,0:T(8,128)(2,1)S(1)} collective-permute-done((bf16[512,192]{1,0:T(8,128)(2,1)S(1)}, bf16[512,192]{1,0:T(8,128)(2,1)S(1)}, u32[]{:S(2)}, u32[]{:S(2)}) %collective-permute-start.106) | collective-permute-done | bytes 196640 | tf_op jit(solution)/shard_map/sum_back0/ppermute | solution.py:39
  370.2 7.1 %collective-permute-done.109.refs_1_ = bf16[256,768]{1,0:T(8,128)(2,1)S(1)} collective-permute-done((bf16[256,768]{1,0:T(8,128)(2,1)S(1)}, bf16[256,768]{1,0:T(8,128)(2,1)S(1)}, u32[]{:S(2)}, u32[]{:S(2)}) %collective-permute-start.109) | collective-permute-done | bytes 393248 | tf_op jit(solution)/shard_map/sum_k3_first/ppermute | solution.py:43
  379.7 6.6 %momentum1.1 = (f32[2,96,9216]{2,1,0:T(8,128)}, f32[2,8448]{1,0:T(2,128)}) custom-call(f32[2,96,9216]{2,1,0:T(8,128)} %refs_0_.7, f32[2,96,9216]{2,1,0:T(8,128)} %refs_1_.29, f32[2,8448]{1,0:T(2,128)} %refs_2_.21, f32[2,8448]{1,0:T(2,128)} %refs_3_.3, f32[2,96,9216]{2,1,0:T(8,128)} %get-tuple-element.253.refs_4_, ...), custom_call_target="tpu_custom_call", output_to_operand_aliasing={{0}: (4, {})} | custom-call | flops 1 | bytes 1 | tf_op jit(solution)/shard_map/momentum1/pallas_call | solution.py:729
  (294 shorter events, 246.2 us)
Async XLA Ops:
  30.2 20.2 %collective-permute-start.20 = (bf16[96,1536]{1,0:T(8,128)(2,1)S(1)}, bf16[96,1536]{1,0:T(8,128)(2,1)S(1)}, u32[]{:S(2)}, u32[]{:S(2)}) collective-permute-start(bf16[96,1536]{1,0:T(8,128)(2,1)S(1)} %copy-done.8), channel_id=1, source_target_pairs={{0,4},{1,5},{2,6},{3,7},{4,0},{5,1},{6,2},{7,3},{8,12},{9,13},{10,... | collective-permute-start | bytes 884744 | tf_op jit(solution)/shard_map/weights_unit_1/ppermute | solution.py:53
  78.7 18.5 %collective-permute-start.35 = (bf16[96,1536]{1,0:T(8,128)(2,1)S(1)}, bf16[96,1536]{1,0:T(8,128)(2,1)S(1)}, u32[]{:S(2)}, u32[]{:S(2)}) collective-permute-start(bf16[96,1536]{1,0:T(8,128)(2,1)S(1)} %copy-done.13), channel_id=1, source_target_pairs={{0,6},{1,7},{2,0},{3,1},{4,2},{5,3},{6,4},{7,5},{8,14},{9,15},{10,... | collective-permute-start | bytes 884744 | tf_op jit(solution)/shard_map/weights_unit_3/ppermute | solution.py:53
  88.5 17.9 %collective-permute-start.34 = (bf16[96,1536]{1,0:T(8,128)(2,1)S(1)}, bf16[96,1536]{1,0:T(8,128)(2,1)S(1)}, u32[]{:S(2)}, u32[]{:S(2)}) collective-permute-start(bf16[96,1536]{1,0:T(8,128)(2,1)S(1)} %copy-done.13), channel_id=1, source_target_pairs={{0,4},{1,5},{2,6},{3,7},{4,0},{5,1},{6,2},{7,3},{8,12},{9,13},{10,... | collective-permute-start | bytes 884744 | tf_op jit(solution)/shard_map/weights_unit_3/ppermute | solution.py:53
  97.7 18.0 %collective-permute-start.43 = (bf16[96,2304]{1,0:T(8,128)(2,1)S(1)}, bf16[96,2304]{1,0:T(8,128)(2,1)S(1)}, u32[]{:S(2)}, u32[]{:S(2)}) collective-permute-start(bf16[96,2304]{1,0:T(8,128)(2,1)S(1)} %copy-done.5), channel_id=1, source_target_pairs={{0,2},{1,3},{2,4},{3,5},{4,6},{5,7},{8,10},{9,11},{10,12},{11,13},... | collective-permute-start | bytes 1327112 | tf_op jit(solution)/shard_map/weights_unit_4/ppermute | solution.py:96
  100.1 20.0 %collective-permute-start.46 = (bf16[96,2304]{1,0:T(8,128)(2,1)S(1)}, bf16[96,2304]{1,0:T(8,128)(2,1)S(1)}, u32[]{:S(2)}, u32[]{:S(2)}) collective-permute-start(bf16[96,2304]{1,0:T(8,128)(2,1)S(1)} %copy-done.5), channel_id=1, source_target_pairs={{2,0},{3,1},{4,2},{5,3},{6,4},{7,5},{10,8},{11,9},{12,10},{13,11},... | collective-permute-start | bytes 1327112 | tf_op jit(solution)/shard_map/weights_unit_4/ppermute | solution.py:96
  127.5 26.4 %collective-permute-start.59 = (bf16[96,2304]{1,0:T(8,128)(2,1)S(1)}, bf16[96,2304]{1,0:T(8,128)(2,1)S(1)}, u32[]{:S(2)}, u32[]{:S(2)}) collective-permute-start(bf16[96,2304]{1,0:T(8,128)(2,1)S(1)} %copy-done.5), channel_id=1, source_target_pairs={{0,1},{1,0},{2,3},{3,2},{4,5},{5,4},{6,7},{7,6},{8,9},{9,8},{10,11... | collective-permute-start | bytes 1327112 | tf_op jit(solution)/shard_map/weights_unit_4/ppermute | solution.py:48
  134.4 19.4 %collective-permute-start.48 = (bf16[96,2304]{1,0:T(8,128)(2,1)S(1)}, bf16[96,2304]{1,0:T(8,128)(2,1)S(1)}, u32[]{:S(2)}, u32[]{:S(2)}) collective-permute-start(bf16[96,2304]{1,0:T(8,128)(2,1)S(1)} %second.2.refs_6_.refs_10_), channel_id=1, source_target_pairs={{4,6},{5,7},{2,0},{3,1},{12,14},{13,15},{10,8},{11,9},{20,22},{21,... | collective-permute-start | bytes 1327112 | tf_op jit(solution)/shard_map/weights_unit_4/ppermute | solution.py:109
  198.4 22.9 %collective-permute-start.53 = (bf16[96,2304]{1,0:T(8,128)(2,1)S(1)}, bf16[96,2304]{1,0:T(8,128)(2,1)S(1)}, u32[]{:S(2)}, u32[]{:S(2)}) collective-permute-start(bf16[96,2304]{1,0:T(8,128)(2,1)S(1)} %second.3.refs_2_.refs_6_.refs_10_), channel_id=1, source_target_pairs={{4,6},{5,7},{2,0},{3,1},{12,14},{13,15},{10,8},{11,9},{20,22},{21,... | collective-permute-start | bytes 1327112 | tf_op jit(solution)/shard_map/weights_unit_5/ppermute | solution.py:109
  199.7 17.2 %collective-permute-start.75 = (bf16[256,768]{1,0:T(8,128)(2,1)S(1)}, bf16[256,768]{1,0:T(8,128)(2,1)S(1)}, u32[]{:S(2)}, u32[]{:S(2)}) collective-permute-start(bf16[256,768]{1,0:T(8,128)(2,1)S(1)} %add_parts.33.refs_3_.refs_7_.refs_10_), channel_id=1, source_target_pairs={{0,8},{8,0},{16,24},{24,16},{1,9},{9,1},{17,25},{25,17},{2,10},{10... | collective-permute-start | bytes 1179656 | tf_op jit(solution)/shard_map/sum_back2_second/ppermute | solution.py:39
  222.2 16.8 %collective-permute-start.73 = (bf16[256,768]{1,0:T(8,128)(2,1)S(1)}, bf16[256,768]{1,0:T(8,128)(2,1)S(1)}, u32[]{:S(2)}, u32[]{:S(2)}) collective-permute-start(bf16[256,768]{1,0:T(8,128)(2,1)S(1)} %add_parts.35.refs_12_.refs_5_), channel_id=1, source_target_pairs={{0,8},{8,0},{16,24},{24,16},{1,9},{9,1},{17,25},{25,17},{2,10},{10... | collective-permute-start | bytes 1179656 | tf_op jit(solution)/shard_map/sum_k0_second/ppermute | solution.py:39
  224.6 24.0 %collective-permute-start.84 = (bf16[96,2304]{1,0:T(8,128)(2,1)S(1)}, bf16[96,2304]{1,0:T(8,128)(2,1)S(1)}, u32[]{:S(2)}, u32[]{:S(2)}) collective-permute-start(bf16[96,2304]{1,0:T(8,128)(2,1)S(1)} %get-tuple-element.202), channel_id=1, source_target_pairs={{0,2},{1,3},{2,4},{3,5},{8,10},{9,11},{10,12},{11,13},{16,18},{17,... | collective-permute-start | bytes 1327112 | tf_op jit(solution)/shard_map/grad_layer1/ppermute | solution.py:104
  228.3 20.3 %collective-permute-start.85 = (bf16[96,2304]{1,0:T(8,128)(2,1)S(1)}, bf16[96,2304]{1,0:T(8,128)(2,1)S(1)}, u32[]{:S(2)}, u32[]{:S(2)}) collective-permute-start(bf16[96,2304]{1,0:T(8,128)(2,1)S(1)} %get-tuple-element.203), channel_id=1, source_target_pairs={{4,2},{5,3},{6,4},{7,5},{12,10},{13,11},{14,12},{15,13},{20,18},{2... | collective-permute-start | bytes 1327112 | tf_op jit(solution)/shard_map/grad_layer1/ppermute | solution.py:104
  264.7 19.4 %collective-permute-start.54 = (bf16[96,2304]{1,0:T(8,128)(2,1)S(1)}, bf16[96,2304]{1,0:T(8,128)(2,1)S(1)}, u32[]{:S(2)}, u32[]{:S(2)}) collective-permute-start(bf16[96,2304]{1,0:T(8,128)(2,1)S(1)} %copy-done.6), channel_id=1, source_target_pairs={{0,1},{1,0},{2,3},{3,2},{4,5},{5,4},{6,7},{7,6},{8,9},{9,8},{10,11... | collective-permute-start | bytes 1327112 | tf_op jit(solution)/shard_map/weights_unit_5/ppermute | solution.py:48
  264.9 21.2 %collective-permute-start.55 = (bf16[96,2304]{1,0:T(8,128)(2,1)S(1)}, bf16[96,2304]{1,0:T(8,128)(2,1)S(1)}, u32[]{:S(2)}, u32[]{:S(2)}) collective-permute-start(bf16[96,2304]{1,0:T(8,128)(2,1)S(1)} %collective-permute-done.49.refs_4_.refs_8_), channel_id=1, source_target_pairs={{0,1},{1,0},{2,3},{3,2},{4,5},{5,4},{6,7},{7,6},{8,9},{9,8},{10,11... | collective-permute-start | bytes 1327112 | tf_op jit(solution)/shard_map/weights_unit_5/ppermute | solution.py:48
  265.3 21.8 %collective-permute-start.83 = (bf16[256,768]{1,0:T(8,128)(2,1)S(1)}, bf16[256,768]{1,0:T(8,128)(2,1)S(1)}, u32[]{:S(2)}, u32[]{:S(2)}) collective-permute-start(bf16[256,768]{1,0:T(8,128)(2,1)S(1)} %get-tuple-element.201.refs_0_), channel_id=1, source_target_pairs={{0,16},{16,0},{8,24},{24,8},{1,17},{17,1},{9,25},{25,9},{2,18},{18... | collective-permute-start | bytes 1179656 | tf_op jit(solution)/shard_map/sum_k1_first/ppermute | solution.py:43
  305.1 17.9 %collective-permute-start.82 = (bf16[256,768]{1,0:T(8,128)(2,1)S(1)}, bf16[256,768]{1,0:T(8,128)(2,1)S(1)}, u32[]{:S(2)}, u32[]{:S(2)}) collective-permute-start(bf16[256,768]{1,0:T(8,128)(2,1)S(1)} %add_parts.38.refs_14_), channel_id=1, source_target_pairs={{0,16},{16,0},{8,24},{24,8},{1,17},{17,1},{9,25},{25,9},{2,18},{18... | collective-permute-start | bytes 1179656 | tf_op jit(solution)/shard_map/sum_k1_second/ppermute | solution.py:43
  305.9 17.2 %collective-permute-start.95 = (bf16[256,768]{1,0:T(8,128)(2,1)S(1)}, bf16[256,768]{1,0:T(8,128)(2,1)S(1)}, u32[]{:S(2)}, u32[]{:S(2)}) collective-permute-start(bf16[256,768]{1,0:T(8,128)(2,1)S(1)} %add_parts.39.refs_16_), channel_id=1, source_target_pairs={{0,8},{8,0},{16,24},{24,16},{1,9},{9,1},{17,25},{25,17},{2,10},{10... | collective-permute-start | bytes 1179656 | tf_op jit(solution)/shard_map/sum_k1_second/ppermute | solution.py:39
  306.8 22.0 %collective-permute-start.103 = (bf16[96,2432]{1,0:T(8,128)(2,1)S(1)}, bf16[96,2432]{1,0:T(8,128)(2,1)S(1)}, u32[]{:S(2)}, u32[]{:S(2)}) collective-permute-start(bf16[96,2432]{1,0:T(8,128)(2,1)S(1)} %get-tuple-element.234.refs_4_), channel_id=1, source_target_pairs={{0,2},{1,3},{2,4},{3,5},{4,6},{5,7},{8,10},{9,11},{10,12},{11,13},... | collective-permute-start | bytes 1400840 | tf_op jit(solution)/shard_map/grad_layer0/ppermute | solution.py:104
  329.0 19.7 %collective-permute-start.111 = (bf16[96,2432]{1,0:T(8,128)(2,1)S(1)}, bf16[96,2432]{1,0:T(8,128)(2,1)S(1)}, u32[]{:S(2)}, u32[]{:S(2)}) collective-permute-start(bf16[96,2432]{1,0:T(8,128)(2,1)S(1)} %total.3.refs_1_), channel_id=1, source_target_pairs={{0,8},{8,0},{16,24},{24,16},{1,9},{9,1},{17,25},{25,17},{2,10},{10... | collective-permute-start | bytes 1400840 | tf_op jit(solution)/shard_map/place_layer0/ppermute | solution.py:39
  332.5 27.2 %collective-permute-start.105 = (bf16[96,2304]{1,0:T(8,128)(2,1)S(1)}, bf16[96,2304]{1,0:T(8,128)(2,1)S(1)}, u32[]{:S(2)}, u32[]{:S(2)}) collective-permute-start(bf16[96,2304]{1,0:T(8,128)(2,1)S(1)} %collective-permute-done.96.refs_20_.refs_2_), channel_id=1, source_target_pairs={{0,16},{16,0},{8,24},{24,8},{1,17},{17,1},{9,25},{25,9},{2,18},{18... | collective-permute-start | bytes 1327112 | tf_op jit(solution)/shard_map/place_layer1/ppermute | solution.py:43
  341.0 18.6 %collective-permute-start.102 = (bf16[256,768]{1,0:T(8,128)(2,1)S(1)}, bf16[256,768]{1,0:T(8,128)(2,1)S(1)}, u32[]{:S(2)}, u32[]{:S(2)}) collective-permute-start(bf16[256,768]{1,0:T(8,128)(2,1)S(1)} %add_parts.41.refs_5_), channel_id=1, source_target_pairs={{0,8},{8,0},{16,24},{24,16},{1,9},{9,1},{17,25},{25,17},{2,10},{10... | collective-permute-start | bytes 1179656 | tf_op jit(solution)/shard_map/sum_k2_second/ppermute | solution.py:39
  342.1 17.5 %collective-permute-start.99 = (bf16[256,768]{1,0:T(8,128)(2,1)S(1)}, bf16[256,768]{1,0:T(8,128)(2,1)S(1)}, u32[]{:S(2)}, u32[]{:S(2)}) collective-permute-start(bf16[256,768]{1,0:T(8,128)(2,1)S(1)} %add_parts.40.refs_3_), channel_id=1, source_target_pairs={{0,16},{16,0},{8,24},{24,8},{1,17},{17,1},{9,25},{25,9},{2,18},{18... | collective-permute-start | bytes 1179656 | tf_op jit(solution)/shard_map/sum_k2_second/ppermute | solution.py:43
  348.7 20.2 %collective-permute-start.112 = (bf16[96,2432]{1,0:T(8,128)(2,1)S(1)}, bf16[96,2432]{1,0:T(8,128)(2,1)S(1)}, u32[]{:S(2)}, u32[]{:S(2)}) collective-permute-start(bf16[96,2432]{1,0:T(8,128)(2,1)S(1)} %total.3.refs_1_), channel_id=1, source_target_pairs={{0,16},{16,0},{8,24},{24,8},{1,17},{17,1},{9,25},{25,9},{2,18},{18... | collective-permute-start | bytes 1400840 | tf_op jit(solution)/shard_map/place_layer0/ppermute | solution.py:43
  368.8 20.3 %collective-permute-start.113 = (bf16[96,2432]{1,0:T(8,128)(2,1)S(1)}, bf16[96,2432]{1,0:T(8,128)(2,1)S(1)}, u32[]{:S(2)}, u32[]{:S(2)}) collective-permute-start(bf16[96,2432]{1,0:T(8,128)(2,1)S(1)} %collective-permute-done.111.refs_2_), channel_id=1, source_target_pairs={{0,16},{16,0},{8,24},{24,8},{1,17},{17,1},{9,25},{25,9},{2,18},{18... | collective-permute-start | bytes 1400840 | tf_op jit(solution)/shard_map/place_layer0/ppermute | solution.py:43
  (106 other events, 1281.3 us)

commit v4 on v3

--- a/solution.py
+++ b/solution.py
@@ -902,7 +902,7 @@
     chunks = [unit(0, "once")]
     chunks.append(unit(1, "twice", *landed(chunks[0]), early_step))
     for n in range(2, 4):
-        chunks.append(unit(n, "twice", *near(chunks[-1])))
+        chunks.append(unit(n, "once" if n == 2 else "twice", *near(chunks[-1])))
     for n in range(4, 6):
         chunks.append(unit(n, "line", *landed(chunks[-1])[-1:]))
     lines = [steps_of(found) for found in chunks[4:]]
@@ -940,8 +940,8 @@
     def key_steps():
         after = yield
         sums, after = yield from sum_in_steps("k0", *key_attention(0, key_tokens, None, after))
-        found.append(key_feed(0, key_tokens, sums, after))
-        yield found[0][:1]
+        found.append(sums)
+        yield ()
 
     found, steps = [], key_steps()
     next(steps)
@@ -1004,7 +1004,7 @@
     with jax.named_scope("place_layer1"):
         got_1 = gather_section(total_of([layer_sums]))
 
-    k0, k1, inputs_k = found[0]
+    k0, k1, inputs_k = key_feed(0, key_tokens, found[0], (p0,))
     mats_step, small_step = momentum(1, *both, (mats_step,), (p0,))
     sums_k, _ = sum_parts("k1", k0, k1, (), (*turn[2], *turn_0[3]))
     k0, k1, inputs_k = key_attention(1, inputs_k, sums_k, (*turn_0[0], got_1[1], sums[0]))
@@ -1013,7 +1013,7 @@
     k0, k1, inputs_k = key_feed(1, inputs_k, sums_k, (*turn_0[2], got_1[3], input_grad))
     with jax.named_scope("place_layer0"):
         got_0 = gather_section(total_of([sums_0]))
-    sums_k, _ = sum_parts("k3", k0, k1)
+    sums_k, _ = sum_parts("k3", k0, k1, (), (small_step,))
     (pooled_k,) = call(
         partial(last_kernel, LAYERS - 1),
         "last_k",

time: 403 us -> 397 us (0.985)
  waiting for transfers between devices: 164 us -> 149 us
  starting transfers between devices: 136 us -> 144 us
    ppermute x12, waiting for transfers between devices: 21.3 us -> 11.8 us  [pass_sums(): return lax.ppermute(block, 'batch', pairs)]
    ppermute x27, waiting for transfers between devices: 53 us -> 60.4 us  [swap_y(): return lax.ppermute(block, 'section', [(0, 2), (2, 0), (1, 3), (3, 1)])]
    ppermute x8, waiting for transfers between devices: 17.3 us -> 11.2 us  [pass_z(): return lax.ppermute(block, 'batch', pairs)]
  transfers between devices with their start and end apart: 114 -> 114, of which waited for: 44 -> 47; matrix products, arithmetic and copies ran while one was open for 0% -> 0% of each run, Pallas kernels for 18% -> 18%
where the time goes in v4:
time: 397 us; the launch traced here: 390 us
  waiting for transfers between devices  149 us (38%)
  starting transfers between devices  144 us (36%)
  Pallas kernels  92.9 us (23%)
    pallas_call x57, Pallas kernels, call(): pl.pallas_call(kernel, name=name, in_specs=specs + [ANY] * len(after), ou...  92.9 us
    ppermute x27, waiting for transfers between devices, swap_y(): return lax.ppermute(block, 'section', [(0, 2), (2, 0), (1, 3), (3, 1)])  60.4 us
    ppermute x25, waiting for transfers between devices, swap_x(): return lax.ppermute(block, 'section', [(0, 1), (1, 0), (2, 3), (3, 2)])  42.1 us
    ppermute x27, starting transfers between devices, swap_y(): return lax.ppermute(block, 'section', [(0, 2), (2, 0), (1, 3), (3, 1)])  32.9 us
    ppermute x12, starting transfers between devices, shift_z(): lax.ppermute(block, 'batch', [(i, (i + 2 * distance) % count) for i in ra...  30.2 us
    ppermute x25, starting transfers between devices, swap_x(): return lax.ppermute(block, 'section', [(0, 1), (1, 0), (2, 3), (3, 2)])  27.6 us
    ppermute x12, starting transfers between devices, pass_sums(): return lax.ppermute(block, 'batch', pairs)  23.8 us
    ppermute x8, starting transfers between devices, pass_z(): return lax.ppermute(block, 'batch', pairs)  21.6 us
  transfers between devices with their start and end apart: 114, of which 47 were waited for; matrix products, arithmetic and copies ran while one was open for 0% of the time, Pallas kernels for 18%

profile of v4, /device:TPU:8, one launch (start us, length us, event | category | flops | bytes accessed | tf_op | source)
XLA Modules:
  0.0 389.8 jit_solution(17805578400259714005)
XLA Ops:
  8.7 4.7 %take.3 = (bf16[96,1536]{1,0:T(8,128)(2,1)}, bf16[96,768]{1,0:T(8,128)(2,1)}, bf16[96,1536]{1,0:T(8,128)(2,1)}, bf16[96,2304]{1,0:T(8,128)(2,1)}, bf16[96,2304]{1,0:T(8,128)(2,1)}) custom-call(s32[2]{0:T(128)} %pad_add_fusion.refs_0_.refs_1_, f32[2,96,9216]{2,1,0:T(8,128)} %refs_0_.7, f32[2,96,9216]{2,1,0:T(8,128)} %refs_1_.28, bf16[96,768]{1,0:T(8,128)(2,1)} %take.2.refs_3_), custom_call_target="tpu_custom_call" | custom-call | flops 1 | bytes 1 | tf_op jit(solution)/shard_map/take/pallas_call | solution.py:729
  13.4 6.7 %momentum0.1 = (f32[2,96,9216]{2,1,0:T(8,128)}, f32[2,8448]{1,0:T(2,128)}) custom-call(f32[2,96,9216]{2,1,0:T(8,128)} %refs_0_.7, f32[2,96,9216]{2,1,0:T(8,128)} %refs_1_.28, f32[2,8448]{1,0:T(2,128)} %refs_2_.20, f32[2,8448]{1,0:T(2,128)} %refs_2_.21, bf16[96,1536]{1,0:T(8,128)(2,1)} %get-tuple-element.142.refs_4_.refs_7_), custom_call_target="tpu_custom_call" | custom-call | flops 1 | bytes 1 | tf_op jit(solution)/shard_map/momentum0/pallas_call | solution.py:729
  32.0 4.8 %collective-permute-done.18.refs_1_ = bf16[256,768]{1,0:T(8,128)(2,1)S(1)} collective-permute-done((bf16[256,768]{1,0:T(8,128)(2,1)S(1)}, bf16[256,768]{1,0:T(8,128)(2,1)S(1)}, u32[]{:S(2)}, u32[]{:S(2)}) %collective-permute-start.18) | collective-permute-done | bytes 393248 | tf_op jit(solution)/shard_map/sum_q0_first/ppermute | solution.py:43
  40.2 4.8 %collective-permute-done.4.refs_10_ = bf16[96,1536]{1,0:T(8,128)(2,1)S(1)} collective-permute-done((bf16[96,1536]{1,0:T(8,128)(2,1)S(1)}, bf16[96,1536]{1,0:T(8,128)(2,1)S(1)}, u32[]{:S(2)}, u32[]{:S(2)}) %collective-permute-start.4) | collective-permute-done | bytes 294944 | tf_op jit(solution)/shard_map/weights_unit_1/ppermute | solution.py:53
  45.5 5.0 %collective-permute-done.20.refs_9_ = bf16[96,1536]{1,0:T(8,128)(2,1)S(1)} collective-permute-done((bf16[96,1536]{1,0:T(8,128)(2,1)S(1)}, bf16[96,1536]{1,0:T(8,128)(2,1)S(1)}, u32[]{:S(2)}, u32[]{:S(2)}) %collective-permute-start.20) | collective-permute-done | bytes 294944 | tf_op jit(solution)/shard_map/weights_unit_1/ppermute | solution.py:53
  58.0 4.3 %collective-permute-start.6 = (bf16[96,768]{1,0:T(8,128)(2,1)S(1)}, bf16[96,768]{1,0:T(8,128)(2,1)S(1)}, u32[]{:S(2)}, u32[]{:S(2)}) collective-permute-start(bf16[96,768]{1,0:T(8,128)(2,1)S(1)} %copy-done.14), channel_id=1, source_target_pairs={{0,4},{1,5},{2,6},{3,7},{4,0},{5,1},{6,2},{7,3},{8,12},{9,13},{10,... | collective-permute-start | bytes 442376 | tf_op jit(solution)/shard_map/weights_unit_2/ppermute | solution.py:53
  84.8 9.3 %collective-permute-start.34 = (bf16[96,1536]{1,0:T(8,128)(2,1)S(1)}, bf16[96,1536]{1,0:T(8,128)(2,1)S(1)}, u32[]{:S(2)}, u32[]{:S(2)}) collective-permute-start(bf16[96,1536]{1,0:T(8,128)(2,1)S(1)} %copy-done.13), channel_id=1, source_target_pairs={{0,4},{1,5},{2,6},{3,7},{4,0},{5,1},{6,2},{7,3},{8,12},{9,13},{10,... | collective-permute-start | bytes 884744 | tf_op jit(solution)/shard_map/weights_unit_3/ppermute | solution.py:53
  107.7 4.5 %collective-permute-done.43.refs_2_.refs_4_.refs_8_ = bf16[96,2304]{1,0:T(8,128)(2,1)S(1)} collective-permute-done((bf16[96,2304]{1,0:T(8,128)(2,1)S(1)}, bf16[96,2304]{1,0:T(8,128)(2,1)S(1)}, u32[]{:S(2)}, u32[]{:S(2)}) %collective-permute-start.43) | collective-permute-done | bytes 442400 | tf_op jit(solution)/shard_map/weights_unit_4/ppermute | solution.py:96
  112.2 4.4 %collective-permute-start.45 = (bf16[96,2304]{1,0:T(8,128)(2,1)S(1)}, bf16[96,2304]{1,0:T(8,128)(2,1)S(1)}, u32[]{:S(2)}, u32[]{:S(2)}) collective-permute-start(bf16[96,2304]{1,0:T(8,128)(2,1)S(1)} %collective-permute-done.43.refs_2_.refs_4_.refs_8_), channel_id=1, source_target_pairs={{2,4},{3,5},{4,6},{5,7},{10,12},{11,13},{12,14},{13,15},{18,20},{1... | collective-permute-start | bytes 1327112 | tf_op jit(solution)/shard_map/weights_unit_4/ppermute | solution.py:96
  138.4 6.3 %collective-permute-done.44.refs_8_ = bf16[256,768]{1,0:T(8,128)(2,1)S(1)} collective-permute-done((bf16[256,768]{1,0:T(8,128)(2,1)S(1)}, bf16[256,768]{1,0:T(8,128)(2,1)S(1)}, u32[]{:S(2)}, u32[]{:S(2)}) %collective-permute-start.44) | collective-permute-done | bytes 393248 | tf_op jit(solution)/shard_map/sum_q3_second/ppermute | solution.py:39
  146.4 4.2 %feed_back1.1 = (bf16[256,768]{1,0:T(8,128)(2,1)S(1)}, bf16[256,768]{1,0:T(8,128)(2,1)S(1)}, f32[512,768]{1,0:T(8,128)S(1)}, bf16[512,768]{1,0:T(8,128)(2,1)S(1)...) custom-call(s32[2]{0:T(128)S(1)} %copy-done.12, ...), custom_call_target="tpu_custom_call" | custom-call | flops 1 | bytes 1 | tf_op jit(solution)/shard_map/feed_back1/pallas_call | solution.py:729
  176.2 5.3 %attention_back1.1 = (bf16[256,768]{1,0:T(8,128)(2,1)S(1)}, bf16[256,768]{1,0:T(8,128)(2,1)S(1)}, f32[512,768]{1,0:T(8,128)S(1)}, bf16[512,768]{1,0:T(8,128)(2,1...) custom-call(f32[2,8448]{1,0:T(2,128)S(1)} %copy-done.1, s32[2]{0:T(128)S(1)} %copy-done.12, ...), custom_call_target="tpu_custom_call" | custom-call | flops 1 | bytes 1 | tf_op jit(solution)/shard_map/attention_back1/pallas_call | solution.py:729
  184.1 6.1 %collective-permute-done.69.refs_1_ = bf16[256,768]{1,0:T(8,128)(2,1)S(1)} collective-permute-done((bf16[256,768]{1,0:T(8,128)(2,1)S(1)}, bf16[256,768]{1,0:T(8,128)(2,1)S(1)}, u32[]{:S(2)}, u32[]{:S(2)}) %collective-permute-start.69) | collective-permute-done | bytes 393248 | tf_op jit(solution)/shard_map/sum_back2_first/ppermute | solution.py:39
  201.8 5.6 %collective-permute-done.72.refs_1_ = bf16[256,768]{1,0:T(8,128)(2,1)S(1)} collective-permute-done((bf16[256,768]{1,0:T(8,128)(2,1)S(1)}, bf16[256,768]{1,0:T(8,128)(2,1)S(1)}, u32[]{:S(2)}, u32[]{:S(2)}) %collective-permute-start.72) | collective-permute-done | bytes 393248 | tf_op jit(solution)/shard_map/sum_k0_first/ppermute | solution.py:43
  210.0 5.5 %collective-permute-done.75.refs_8_ = bf16[256,768]{1,0:T(8,128)(2,1)S(1)} collective-permute-done((bf16[256,768]{1,0:T(8,128)(2,1)S(1)}, bf16[256,768]{1,0:T(8,128)(2,1)S(1)}, u32[]{:S(2)}, u32[]{:S(2)}) %collective-permute-start.75) | collective-permute-done | bytes 393248 | tf_op jit(solution)/shard_map/sum_back2_second/ppermute | solution.py:39
  231.5 7.7 %collective-permute-done.77.refs_5_ = bf16[256,768]{1,0:T(8,128)(2,1)S(1)} collective-permute-done((bf16[256,768]{1,0:T(8,128)(2,1)S(1)}, bf16[256,768]{1,0:T(8,128)(2,1)S(1)}, u32[]{:S(2)}, u32[]{:S(2)}) %collective-permute-start.77) | collective-permute-done | bytes 393248 | tf_op jit(solution)/shard_map/sum_back1_second/ppermute | solution.py:43
  240.3 5.3 %attention_back0.1 = (bf16[512,384]{1,0:T(8,128)(2,1)S(1)}, bf16[512,384]{1,0:T(8,128)(2,1)S(1)}, f32[512,768]{1,0:T(8,128)S(1)}, bf16[512,768]{1,0:T(8,128)(2,1...) custom-call(f32[2,8448]{1,0:T(2,128)S(1)} %copy-done.1, s32[2]{0:T(128)S(1)} %copy-done.12, ...), custom_call_target="tpu_custom_call" | custom-call | flops 1 | bytes 1 | tf_op jit(solution)/shard_map/attention_back0/pallas_call | solution.py:729
  261.4 5.6 %collective-permute-done.71.refs_4_ = bf16[256,768]{1,0:T(8,128)(2,1)S(1)} collective-permute-done((bf16[256,768]{1,0:T(8,128)(2,1)S(1)}, bf16[256,768]{1,0:T(8,128)(2,1)S(1)}, u32[]{:S(2)}, u32[]{:S(2)}) %collective-permute-start.71) | collective-permute-done | bytes 393248 | tf_op jit(solution)/shard_map/sum_k0_second/ppermute | solution.py:43
  311.9 6.0 %collective-permute-done.86.refs_15_ = bf16[256,768]{1,0:T(8,128)(2,1)S(1)} collective-permute-done((bf16[256,768]{1,0:T(8,128)(2,1)S(1)}, bf16[256,768]{1,0:T(8,128)(2,1)S(1)}, u32[]{:S(2)}, u32[]{:S(2)}) %collective-permute-start.86) | collective-permute-done | bytes 393248 | tf_op jit(solution)/shard_map/sum_k1_second/ppermute | solution.py:43
  328.7 7.0 %collective-permute-done.100.refs_1_ = bf16[256,768]{1,0:T(8,128)(2,1)S(1)} collective-permute-done((bf16[256,768]{1,0:T(8,128)(2,1)S(1)}, bf16[256,768]{1,0:T(8,128)(2,1)S(1)}, u32[]{:S(2)}, u32[]{:S(2)}) %collective-permute-start.100) | collective-permute-done | bytes 393248 | tf_op jit(solution)/shard_map/sum_k2_first/ppermute | solution.py:43
  342.5 9.0 %collective-permute-done.106.refs_3_ = bf16[512,192]{1,0:T(8,128)(2,1)S(1)} collective-permute-done((bf16[512,192]{1,0:T(8,128)(2,1)S(1)}, bf16[512,192]{1,0:T(8,128)(2,1)S(1)}, u32[]{:S(2)}, u32[]{:S(2)}) %collective-permute-start.106) | collective-permute-done | bytes 196640 | tf_op jit(solution)/shard_map/sum_back0/ppermute | solution.py:39
  359.5 4.2 %collective-permute-done.112.refs_3_ = bf16[96,2432]{1,0:T(8,128)(2,1)S(1)} collective-permute-done((bf16[96,2432]{1,0:T(8,128)(2,1)S(1)}, bf16[96,2432]{1,0:T(8,128)(2,1)S(1)}, u32[]{:S(2)}, u32[]{:S(2)}) %collective-permute-start.112) | collective-permute-done | bytes 466976 | tf_op jit(solution)/shard_map/place_layer0/ppermute | solution.py:43
  365.1 6.6 %momentum1.1 = (f32[2,96,9216]{2,1,0:T(8,128)}, f32[2,8448]{1,0:T(2,128)}) custom-call(f32[2,96,9216]{2,1,0:T(8,128)} %refs_0_.7, f32[2,96,9216]{2,1,0:T(8,128)} %refs_1_.28, f32[2,8448]{1,0:T(2,128)} %refs_2_.20, f32[2,8448]{1,0:T(2,128)} %refs_2_.21, f32[2,96,9216]{2,1,0:T(8,128)} %get-tuple-element.248.refs_4_, ...), custom_call_target="tpu_custom_call", output_to_operand_aliasing={{0}: (4, {})} | custom-call | flops 1 | bytes 1 | tf_op jit(solution)/shard_map/momentum1/pallas_call | solution.py:729
  378.0 4.2 %collective-permute-done.113.refs_4_ = bf16[96,2432]{1,0:T(8,128)(2,1)S(1)} collective-permute-done((bf16[96,2432]{1,0:T(8,128)(2,1)S(1)}, bf16[96,2432]{1,0:T(8,128)(2,1)S(1)}, u32[]{:S(2)}, u32[]{:S(2)}) %collective-permute-start.113) | collective-permute-done | bytes 466976 | tf_op jit(solution)/shard_map/place_layer0/ppermute | solution.py:43
  (296 shorter events, 251.2 us)
Async XLA Ops:
  30.3 20.2 %collective-permute-start.20 = (bf16[96,1536]{1,0:T(8,128)(2,1)S(1)}, bf16[96,1536]{1,0:T(8,128)(2,1)S(1)}, u32[]{:S(2)}, u32[]{:S(2)}) collective-permute-start(bf16[96,1536]{1,0:T(8,128)(2,1)S(1)} %copy-done.9), channel_id=1, source_target_pairs={{0,4},{1,5},{2,6},{3,7},{4,0},{5,1},{6,2},{7,3},{8,12},{9,13},{10,... | collective-permute-start | bytes 884744 | tf_op jit(solution)/shard_map/weights_unit_1/ppermute | solution.py:53
  75.6 18.6 %collective-permute-start.35 = (bf16[96,1536]{1,0:T(8,128)(2,1)S(1)}, bf16[96,1536]{1,0:T(8,128)(2,1)S(1)}, u32[]{:S(2)}, u32[]{:S(2)}) collective-permute-start(bf16[96,1536]{1,0:T(8,128)(2,1)S(1)} %copy-done.13), channel_id=1, source_target_pairs={{0,6},{1,7},{2,0},{3,1},{4,2},{5,3},{6,4},{7,5},{8,14},{9,15},{10,... | collective-permute-start | bytes 884744 | tf_op jit(solution)/shard_map/weights_unit_3/ppermute | solution.py:53
  84.8 19.1 %collective-permute-start.34 = (bf16[96,1536]{1,0:T(8,128)(2,1)S(1)}, bf16[96,1536]{1,0:T(8,128)(2,1)S(1)}, u32[]{:S(2)}, u32[]{:S(2)}) collective-permute-start(bf16[96,1536]{1,0:T(8,128)(2,1)S(1)} %copy-done.13), channel_id=1, source_target_pairs={{0,4},{1,5},{2,6},{3,7},{4,0},{5,1},{6,2},{7,3},{8,12},{9,13},{10,... | collective-permute-start | bytes 884744 | tf_op jit(solution)/shard_map/weights_unit_3/ppermute | solution.py:53
  94.7 17.5 %collective-permute-start.43 = (bf16[96,2304]{1,0:T(8,128)(2,1)S(1)}, bf16[96,2304]{1,0:T(8,128)(2,1)S(1)}, u32[]{:S(2)}, u32[]{:S(2)}) collective-permute-start(bf16[96,2304]{1,0:T(8,128)(2,1)S(1)} %copy-done.5), channel_id=1, source_target_pairs={{0,2},{1,3},{2,4},{3,5},{4,6},{5,7},{8,10},{9,11},{10,12},{11,13},... | collective-permute-start | bytes 1327112 | tf_op jit(solution)/shard_map/weights_unit_4/ppermute | solution.py:96
  96.6 20.0 %collective-permute-start.46 = (bf16[96,2304]{1,0:T(8,128)(2,1)S(1)}, bf16[96,2304]{1,0:T(8,128)(2,1)S(1)}, u32[]{:S(2)}, u32[]{:S(2)}) collective-permute-start(bf16[96,2304]{1,0:T(8,128)(2,1)S(1)} %copy-done.5), channel_id=1, source_target_pairs={{2,0},{3,1},{4,2},{5,3},{6,4},{7,5},{10,8},{11,9},{12,10},{13,11},... | collective-permute-start | bytes 1327112 | tf_op jit(solution)/shard_map/weights_unit_4/ppermute | solution.py:96
  126.4 26.2 %collective-permute-start.59 = (bf16[96,2304]{1,0:T(8,128)(2,1)S(1)}, bf16[96,2304]{1,0:T(8,128)(2,1)S(1)}, u32[]{:S(2)}, u32[]{:S(2)}) collective-permute-start(bf16[96,2304]{1,0:T(8,128)(2,1)S(1)} %copy-done.5), channel_id=1, source_target_pairs={{0,1},{1,0},{2,3},{3,2},{4,5},{5,4},{6,7},{7,6},{8,9},{9,8},{10,11... | collective-permute-start | bytes 1327112 | tf_op jit(solution)/shard_map/weights_unit_4/ppermute | solution.py:48
  129.8 22.9 %collective-permute-start.48 = (bf16[96,2304]{1,0:T(8,128)(2,1)S(1)}, bf16[96,2304]{1,0:T(8,128)(2,1)S(1)}, u32[]{:S(2)}, u32[]{:S(2)}) collective-permute-start(bf16[96,2304]{1,0:T(8,128)(2,1)S(1)} %second.2.refs_6_.refs_10_), channel_id=1, source_target_pairs={{4,6},{5,7},{2,0},{3,1},{12,14},{13,15},{10,8},{11,9},{20,22},{21,... | collective-permute-start | bytes 1327112 | tf_op jit(solution)/shard_map/weights_unit_4/ppermute | solution.py:109
  197.1 22.9 %collective-permute-start.53 = (bf16[96,2304]{1,0:T(8,128)(2,1)S(1)}, bf16[96,2304]{1,0:T(8,128)(2,1)S(1)}, u32[]{:S(2)}, u32[]{:S(2)}) collective-permute-start(bf16[96,2304]{1,0:T(8,128)(2,1)S(1)} %second.3.refs_2_.refs_6_.refs_10_), channel_id=1, source_target_pairs={{4,6},{5,7},{2,0},{3,1},{12,14},{13,15},{10,8},{11,9},{20,22},{21,... | collective-permute-start | bytes 1327112 | tf_op jit(solution)/shard_map/weights_unit_5/ppermute | solution.py:109
  198.4 17.1 %collective-permute-start.75 = (bf16[256,768]{1,0:T(8,128)(2,1)S(1)}, bf16[256,768]{1,0:T(8,128)(2,1)S(1)}, u32[]{:S(2)}, u32[]{:S(2)}) collective-permute-start(bf16[256,768]{1,0:T(8,128)(2,1)S(1)} %add_parts.33.refs_3_.refs_7_.refs_10_), channel_id=1, source_target_pairs={{0,8},{8,0},{16,24},{24,16},{1,9},{9,1},{17,25},{25,17},{2,10},{10... | collective-permute-start | bytes 1179656 | tf_op jit(solution)/shard_map/sum_back2_second/ppermute | solution.py:39
  221.7 18.5 %collective-permute-start.83 = (bf16[96,2304]{1,0:T(8,128)(2,1)S(1)}, bf16[96,2304]{1,0:T(8,128)(2,1)S(1)}, u32[]{:S(2)}, u32[]{:S(2)}) collective-permute-start(bf16[96,2304]{1,0:T(8,128)(2,1)S(1)} %get-tuple-element.205), channel_id=1, source_target_pairs={{0,2},{1,3},{2,4},{3,5},{8,10},{9,11},{10,12},{11,13},{16,18},{17,... | collective-permute-start | bytes 1327112 | tf_op jit(solution)/shard_map/grad_layer1/ppermute | solution.py:104
  254.4 17.4 %collective-permute-start.91 = (bf16[96,2432]{1,0:T(8,128)(2,1)S(1)}, bf16[96,2432]{1,0:T(8,128)(2,1)S(1)}, u32[]{:S(2)}, u32[]{:S(2)}) collective-permute-start(bf16[96,2432]{1,0:T(8,128)(2,1)S(1)} %get-tuple-element.229), channel_id=1, source_target_pairs={{0,2},{1,3},{8,10},{9,11},{16,18},{17,19},{24,26},{25,27}} | collective-permute-start | bytes 1400840 | tf_op jit(solution)/shard_map/grad_layer0/ppermute | solution.py:104
  256.6 18.1 %collective-permute-start.92 = (bf16[96,2432]{1,0:T(8,128)(2,1)S(1)}, bf16[96,2432]{1,0:T(8,128)(2,1)S(1)}, u32[]{:S(2)}, u32[]{:S(2)}) collective-permute-start(bf16[96,2432]{1,0:T(8,128)(2,1)S(1)} %get-tuple-element.230), channel_id=1, source_target_pairs={{6,4},{7,5},{14,12},{15,13},{22,20},{23,21},{30,28},{31,29}} | collective-permute-start | bytes 1400840 | tf_op jit(solution)/shard_map/grad_layer0/ppermute | solution.py:104
  257.3 21.3 %collective-permute-start.54 = (bf16[96,2304]{1,0:T(8,128)(2,1)S(1)}, bf16[96,2304]{1,0:T(8,128)(2,1)S(1)}, u32[]{:S(2)}, u32[]{:S(2)}) collective-permute-start(bf16[96,2304]{1,0:T(8,128)(2,1)S(1)} %copy-done.6), channel_id=1, source_target_pairs={{0,1},{1,0},{2,3},{3,2},{4,5},{5,4},{6,7},{7,6},{8,9},{9,8},{10,11... | collective-permute-start | bytes 1327112 | tf_op jit(solution)/shard_map/weights_unit_5/ppermute | solution.py:48
  261.4 20.1 %collective-permute-start.55 = (bf16[96,2304]{1,0:T(8,128)(2,1)S(1)}, bf16[96,2304]{1,0:T(8,128)(2,1)S(1)}, u32[]{:S(2)}, u32[]{:S(2)}) collective-permute-start(bf16[96,2304]{1,0:T(8,128)(2,1)S(1)} %collective-permute-done.49.refs_4_.refs_8_), channel_id=1, source_target_pairs={{0,1},{1,0},{2,3},{3,2},{4,5},{5,4},{6,7},{7,6},{8,9},{9,8},{10,11... | collective-permute-start | bytes 1327112 | tf_op jit(solution)/shard_map/weights_unit_5/ppermute | solution.py:48
  300.0 17.9 %collective-permute-start.86 = (bf16[256,768]{1,0:T(8,128)(2,1)S(1)}, bf16[256,768]{1,0:T(8,128)(2,1)S(1)}, u32[]{:S(2)}, u32[]{:S(2)}) collective-permute-start(bf16[256,768]{1,0:T(8,128)(2,1)S(1)} %add_parts.38.refs_14_), channel_id=1, source_target_pairs={{0,16},{16,0},{8,24},{24,8},{1,17},{17,1},{9,25},{25,9},{2,18},{18... | collective-permute-start | bytes 1179656 | tf_op jit(solution)/shard_map/sum_k1_second/ppermute | solution.py:43
  300.7 17.2 %collective-permute-start.95 = (bf16[256,768]{1,0:T(8,128)(2,1)S(1)}, bf16[256,768]{1,0:T(8,128)(2,1)S(1)}, u32[]{:S(2)}, u32[]{:S(2)}) collective-permute-start(bf16[256,768]{1,0:T(8,128)(2,1)S(1)} %add_parts.39.refs_16_), channel_id=1, source_target_pairs={{0,8},{8,0},{16,24},{24,16},{1,9},{9,1},{17,25},{25,17},{2,10},{10... | collective-permute-start | bytes 1179656 | tf_op jit(solution)/shard_map/sum_k1_second/ppermute | solution.py:39
  301.7 21.7 %collective-permute-start.103 = (bf16[96,2432]{1,0:T(8,128)(2,1)S(1)}, bf16[96,2432]{1,0:T(8,128)(2,1)S(1)}, u32[]{:S(2)}, u32[]{:S(2)}) collective-permute-start(bf16[96,2432]{1,0:T(8,128)(2,1)S(1)} %get-tuple-element.233.refs_4_), channel_id=1, source_target_pairs={{0,2},{1,3},{2,4},{3,5},{4,6},{5,7},{8,10},{9,11},{10,12},{11,13},... | collective-permute-start | bytes 1400840 | tf_op jit(solution)/shard_map/grad_layer0/ppermute | solution.py:104
  309.8 17.5 %collective-permute-start.101 = (bf16[96,2304]{1,0:T(8,128)(2,1)S(1)}, bf16[96,2304]{1,0:T(8,128)(2,1)S(1)}, u32[]{:S(2)}, u32[]{:S(2)}) collective-permute-start(bf16[96,2304]{1,0:T(8,128)(2,1)S(1)} %total.2.refs_1_), channel_id=1, source_target_pairs={{0,16},{16,0},{8,24},{24,8},{1,17},{17,1},{9,25},{25,9},{2,18},{18... | collective-permute-start | bytes 1327112 | tf_op jit(solution)/shard_map/place_layer1/ppermute | solution.py:43
  323.5 18.9 %collective-permute-start.111 = (bf16[96,2432]{1,0:T(8,128)(2,1)S(1)}, bf16[96,2432]{1,0:T(8,128)(2,1)S(1)}, u32[]{:S(2)}, u32[]{:S(2)}) collective-permute-start(bf16[96,2432]{1,0:T(8,128)(2,1)S(1)} %total.3.refs_1_), channel_id=1, source_target_pairs={{0,8},{8,0},{16,24},{24,16},{1,9},{9,1},{17,25},{25,17},{2,10},{10... | collective-permute-start | bytes 1400840 | tf_op jit(solution)/shard_map/place_layer0/ppermute | solution.py:39
  327.4 26.1 %collective-permute-start.105 = (bf16[96,2304]{1,0:T(8,128)(2,1)S(1)}, bf16[96,2304]{1,0:T(8,128)(2,1)S(1)}, u32[]{:S(2)}, u32[]{:S(2)}) collective-permute-start(bf16[96,2304]{1,0:T(8,128)(2,1)S(1)} %collective-permute-done.96.refs_20_.refs_2_), channel_id=1, source_target_pairs={{0,16},{16,0},{8,24},{24,8},{1,17},{17,1},{9,25},{25,9},{2,18},{18... | collective-permute-start | bytes 1327112 | tf_op jit(solution)/shard_map/place_layer1/ppermute | solution.py:43
  335.9 17.6 %collective-permute-start.102 = (bf16[256,768]{1,0:T(8,128)(2,1)S(1)}, bf16[256,768]{1,0:T(8,128)(2,1)S(1)}, u32[]{:S(2)}, u32[]{:S(2)}) collective-permute-start(bf16[256,768]{1,0:T(8,128)(2,1)S(1)} %add_parts.41.refs_5_), channel_id=1, source_target_pairs={{0,8},{8,0},{16,24},{24,16},{1,9},{9,1},{17,25},{25,17},{2,10},{10... | collective-permute-start | bytes 1179656 | tf_op jit(solution)/shard_map/sum_k2_second/ppermute | solution.py:39
  337.0 16.7 %collective-permute-start.99 = (bf16[256,768]{1,0:T(8,128)(2,1)S(1)}, bf16[256,768]{1,0:T(8,128)(2,1)S(1)}, u32[]{:S(2)}, u32[]{:S(2)}) collective-permute-start(bf16[256,768]{1,0:T(8,128)(2,1)S(1)} %add_parts.40.refs_3_), channel_id=1, source_target_pairs={{0,16},{16,0},{8,24},{24,8},{1,17},{17,1},{9,25},{25,9},{2,18},{18... | collective-permute-start | bytes 1179656 | tf_op jit(solution)/shard_map/sum_k2_second/ppermute | solution.py:43
  342.5 21.2 %collective-permute-start.112 = (bf16[96,2432]{1,0:T(8,128)(2,1)S(1)}, bf16[96,2432]{1,0:T(8,128)(2,1)S(1)}, u32[]{:S(2)}, u32[]{:S(2)}) collective-permute-start(bf16[96,2432]{1,0:T(8,128)(2,1)S(1)} %total.3.refs_1_), channel_id=1, source_target_pairs={{0,16},{16,0},{8,24},{24,8},{1,17},{17,1},{9,25},{25,9},{2,18},{18... | collective-permute-start | bytes 1400840 | tf_op jit(solution)/shard_map/place_layer0/ppermute | solution.py:43
  363.7 18.4 %collective-permute-start.113 = (bf16[96,2432]{1,0:T(8,128)(2,1)S(1)}, bf16[96,2432]{1,0:T(8,128)(2,1)S(1)}, u32[]{:S(2)}, u32[]{:S(2)}) collective-permute-start(bf16[96,2432]{1,0:T(8,128)(2,1)S(1)} %collective-permute-done.111.refs_2_), channel_id=1, source_target_pairs={{0,16},{16,0},{8,24},{24,8},{1,17},{17,1},{9,25},{25,9},{2,18},{18... | collective-permute-start | bytes 1400840 | tf_op jit(solution)/shard_map/place_layer0/ppermute | solution.py:43
  (107 other events, 1238.4 us)

commit v5 on v4

--- a/solution.py
+++ b/solution.py
@@ -964,7 +964,7 @@
         )
         if last:
             out_q, pooled_q = tail
-        gates = (lines[0][1], lines[0][2]) if last else (lines[1][2], turn[0])
+        gates = (lines[0][1], lines[0][2]) if last else ((), turn[0])
         sums, done = sum_parts(f"back{2 * layer + 1}", p0, p1, *gates, steps.send)
         feed_pairs = [(feed_in, grad_hidden), (branch, active)]
         q, k, v, mixed, prob = attn_kept

time: 397 us -> 396 us (level)
  transfers between devices with their start and end apart: 114 -> 114, of which waited for: 47 -> 48; matrix products, arithmetic and copies ran while one was open for 0% -> 0% of each run, Pallas kernels for 18% -> 18%
where the time goes in v5:
time: 396 us; the launch traced here: 388 us
  waiting for transfers between devices  148 us (37%)
  starting transfers between devices  143 us (36%)
  Pallas kernels  92.8 us (23%)
    pallas_call x57, Pallas kernels, call(): pl.pallas_call(kernel, name=name, in_specs=specs + [ANY] * len(after), ou...  92.8 us
    ppermute x27, waiting for transfers between devices, swap_y(): return lax.ppermute(block, 'section', [(0, 2), (2, 0), (1, 3), (3, 1)])  58 us
    ppermute x25, waiting for transfers between devices, swap_x(): return lax.ppermute(block, 'section', [(0, 1), (1, 0), (2, 3), (3, 2)])  44.6 us
    ppermute x27, starting transfers between devices, swap_y(): return lax.ppermute(block, 'section', [(0, 2), (2, 0), (1, 3), (3, 1)])  33.4 us
    ppermute x12, starting transfers between devices, shift_z(): lax.ppermute(block, 'batch', [(i, (i + 2 * distance) % count) for i in ra...  30.2 us
    ppermute x25, starting transfers between devices, swap_x(): return lax.ppermute(block, 'section', [(0, 1), (1, 0), (2, 3), (3, 2)])  26.1 us
    ppermute x12, starting transfers between devices, pass_sums(): return lax.ppermute(block, 'batch', pairs)  23.6 us
    ppermute x8, starting transfers between devices, pass_z(): return lax.ppermute(block, 'batch', pairs)  21.6 us
  transfers between devices with their start and end apart: 114, of which 48 were waited for; matrix products, arithmetic and copies ran while one was open for 0% of the time, Pallas kernels for 18%

profile of v5, /device:TPU:8, one launch (start us, length us, event | category | flops | bytes accessed | tf_op | source)
XLA Modules:
  0.0 388.5 jit_solution(6537243223059302639)
XLA Ops:
  8.7 4.7 %take.3 = (bf16[96,1536]{1,0:T(8,128)(2,1)}, bf16[96,768]{1,0:T(8,128)(2,1)}, bf16[96,1536]{1,0:T(8,128)(2,1)}, bf16[96,2304]{1,0:T(8,128)(2,1)}, bf16[96,2304]{1,0:T(8,128)(2,1)}) custom-call(s32[2]{0:T(128)} %pad_add_fusion.refs_0_.refs_1_, f32[2,96,9216]{2,1,0:T(8,128)} %refs_0_.7, f32[2,96,9216]{2,1,0:T(8,128)} %refs_1_.28, bf16[96,768]{1,0:T(8,128)(2,1)} %take.2.refs_3_), custom_call_target="tpu_custom_call" | custom-call | flops 1 | bytes 1 | tf_op jit(solution)/shard_map/take/pallas_call | solution.py:729
  13.4 6.7 %momentum0.1 = (f32[2,96,9216]{2,1,0:T(8,128)}, f32[2,8448]{1,0:T(2,128)}) custom-call(f32[2,96,9216]{2,1,0:T(8,128)} %refs_0_.7, f32[2,96,9216]{2,1,0:T(8,128)} %refs_1_.28, f32[2,8448]{1,0:T(2,128)} %refs_2_.20, f32[2,8448]{1,0:T(2,128)} %refs_2_.21, bf16[96,1536]{1,0:T(8,128)(2,1)} %get-tuple-element.141.refs_4_.refs_7_), custom_call_target="tpu_custom_call" | custom-call | flops 1 | bytes 1 | tf_op jit(solution)/shard_map/momentum0/pallas_call | solution.py:729
  32.0 4.8 %collective-permute-done.18.refs_1_ = bf16[256,768]{1,0:T(8,128)(2,1)S(1)} collective-permute-done((bf16[256,768]{1,0:T(8,128)(2,1)S(1)}, bf16[256,768]{1,0:T(8,128)(2,1)S(1)}, u32[]{:S(2)}, u32[]{:S(2)}) %collective-permute-start.18) | collective-permute-done | bytes 393248 | tf_op jit(solution)/shard_map/sum_q0_first/ppermute | solution.py:43
  40.2 4.8 %collective-permute-done.4.refs_10_ = bf16[96,1536]{1,0:T(8,128)(2,1)S(1)} collective-permute-done((bf16[96,1536]{1,0:T(8,128)(2,1)S(1)}, bf16[96,1536]{1,0:T(8,128)(2,1)S(1)}, u32[]{:S(2)}, u32[]{:S(2)}) %collective-permute-start.4) | collective-permute-done | bytes 294944 | tf_op jit(solution)/shard_map/weights_unit_1/ppermute | solution.py:53
  45.5 5.0 %collective-permute-done.20.refs_9_ = bf16[96,1536]{1,0:T(8,128)(2,1)S(1)} collective-permute-done((bf16[96,1536]{1,0:T(8,128)(2,1)S(1)}, bf16[96,1536]{1,0:T(8,128)(2,1)S(1)}, u32[]{:S(2)}, u32[]{:S(2)}) %collective-permute-start.20) | collective-permute-done | bytes 294944 | tf_op jit(solution)/shard_map/weights_unit_1/ppermute | solution.py:53
  58.0 4.3 %collective-permute-start.6 = (bf16[96,768]{1,0:T(8,128)(2,1)S(1)}, bf16[96,768]{1,0:T(8,128)(2,1)S(1)}, u32[]{:S(2)}, u32[]{:S(2)}) collective-permute-start(bf16[96,768]{1,0:T(8,128)(2,1)S(1)} %copy-done.14), channel_id=1, source_target_pairs={{0,4},{1,5},{2,6},{3,7},{4,0},{5,1},{6,2},{7,3},{8,12},{9,13},{10,... | collective-permute-start | bytes 442376 | tf_op jit(solution)/shard_map/weights_unit_2/ppermute | solution.py:53
  84.8 9.3 %collective-permute-start.34 = (bf16[96,1536]{1,0:T(8,128)(2,1)S(1)}, bf16[96,1536]{1,0:T(8,128)(2,1)S(1)}, u32[]{:S(2)}, u32[]{:S(2)}) collective-permute-start(bf16[96,1536]{1,0:T(8,128)(2,1)S(1)} %copy-done.13), channel_id=1, source_target_pairs={{0,4},{1,5},{2,6},{3,7},{4,0},{5,1},{6,2},{7,3},{8,12},{9,13},{10,... | collective-permute-start | bytes 884744 | tf_op jit(solution)/shard_map/weights_unit_3/ppermute | solution.py:53
  107.7 4.5 %collective-permute-done.43.refs_2_.refs_4_.refs_8_ = bf16[96,2304]{1,0:T(8,128)(2,1)S(1)} collective-permute-done((bf16[96,2304]{1,0:T(8,128)(2,1)S(1)}, bf16[96,2304]{1,0:T(8,128)(2,1)S(1)}, u32[]{:S(2)}, u32[]{:S(2)}) %collective-permute-start.43) | collective-permute-done | bytes 442400 | tf_op jit(solution)/shard_map/weights_unit_4/ppermute | solution.py:96
  112.2 4.4 %collective-permute-start.45 = (bf16[96,2304]{1,0:T(8,128)(2,1)S(1)}, bf16[96,2304]{1,0:T(8,128)(2,1)S(1)}, u32[]{:S(2)}, u32[]{:S(2)}) collective-permute-start(bf16[96,2304]{1,0:T(8,128)(2,1)S(1)} %collective-permute-done.43.refs_2_.refs_4_.refs_8_), channel_id=1, source_target_pairs={{2,4},{3,5},{4,6},{5,7},{10,12},{11,13},{12,14},{13,15},{18,20},{1... | collective-permute-start | bytes 1327112 | tf_op jit(solution)/shard_map/weights_unit_4/ppermute | solution.py:96
  138.4 6.3 %collective-permute-done.44.refs_8_ = bf16[256,768]{1,0:T(8,128)(2,1)S(1)} collective-permute-done((bf16[256,768]{1,0:T(8,128)(2,1)S(1)}, bf16[256,768]{1,0:T(8,128)(2,1)S(1)}, u32[]{:S(2)}, u32[]{:S(2)}) %collective-permute-start.44) | collective-permute-done | bytes 393248 | tf_op jit(solution)/shard_map/sum_q3_second/ppermute | solution.py:39
  146.4 4.2 %feed_back1.1 = (bf16[256,768]{1,0:T(8,128)(2,1)S(1)}, bf16[256,768]{1,0:T(8,128)(2,1)S(1)}, f32[512,768]{1,0:T(8,128)S(1)}, bf16[512,768]{1,0:T(8,128)(2,1)S(1)...) custom-call(s32[2]{0:T(128)S(1)} %copy-done.12, ...), custom_call_target="tpu_custom_call" | custom-call | flops 1 | bytes 1 | tf_op jit(solution)/shard_map/feed_back1/pallas_call | solution.py:729
  176.2 5.3 %attention_back1.1 = (bf16[256,768]{1,0:T(8,128)(2,1)S(1)}, bf16[256,768]{1,0:T(8,128)(2,1)S(1)}, f32[512,768]{1,0:T(8,128)S(1)}, bf16[512,768]{1,0:T(8,128)(2,1...) custom-call(f32[2,8448]{1,0:T(2,128)S(1)} %copy-done.1, s32[2]{0:T(128)S(1)} %copy-done.12, ...), custom_call_target="tpu_custom_call" | custom-call | flops 1 | bytes 1 | tf_op jit(solution)/shard_map/attention_back1/pallas_call | solution.py:729
  184.1 6.1 %collective-permute-done.69.refs_1_ = bf16[256,768]{1,0:T(8,128)(2,1)S(1)} collective-permute-done((bf16[256,768]{1,0:T(8,128)(2,1)S(1)}, bf16[256,768]{1,0:T(8,128)(2,1)S(1)}, u32[]{:S(2)}, u32[]{:S(2)}) %collective-permute-start.69) | collective-permute-done | bytes 393248 | tf_op jit(solution)/shard_map/sum_back2_first/ppermute | solution.py:39
  201.6 5.8 %collective-permute-done.72.refs_1_ = bf16[256,768]{1,0:T(8,128)(2,1)S(1)} collective-permute-done((bf16[256,768]{1,0:T(8,128)(2,1)S(1)}, bf16[256,768]{1,0:T(8,128)(2,1)S(1)}, u32[]{:S(2)}, u32[]{:S(2)}) %collective-permute-start.72) | collective-permute-done | bytes 393248 | tf_op jit(solution)/shard_map/sum_k0_first/ppermute | solution.py:43
  208.7 6.8 %collective-permute-done.75.refs_8_ = bf16[256,768]{1,0:T(8,128)(2,1)S(1)} collective-permute-done((bf16[256,768]{1,0:T(8,128)(2,1)S(1)}, bf16[256,768]{1,0:T(8,128)(2,1)S(1)}, u32[]{:S(2)}, u32[]{:S(2)}) %collective-permute-start.75) | collective-permute-done | bytes 393248 | tf_op jit(solution)/shard_map/sum_back2_second/ppermute | solution.py:39
  231.5 7.7 %collective-permute-done.77.refs_5_ = bf16[256,768]{1,0:T(8,128)(2,1)S(1)} collective-permute-done((bf16[256,768]{1,0:T(8,128)(2,1)S(1)}, bf16[256,768]{1,0:T(8,128)(2,1)S(1)}, u32[]{:S(2)}, u32[]{:S(2)}) %collective-permute-start.77) | collective-permute-done | bytes 393248 | tf_op jit(solution)/shard_map/sum_back1_second/ppermute | solution.py:43
  240.3 5.3 %attention_back0.1 = (bf16[512,384]{1,0:T(8,128)(2,1)S(1)}, bf16[512,384]{1,0:T(8,128)(2,1)S(1)}, f32[512,768]{1,0:T(8,128)S(1)}, bf16[512,768]{1,0:T(8,128)(2,1...) custom-call(f32[2,8448]{1,0:T(2,128)S(1)} %copy-done.1, s32[2]{0:T(128)S(1)} %copy-done.12, ...), custom_call_target="tpu_custom_call" | custom-call | flops 1 | bytes 1 | tf_op jit(solution)/shard_map/attention_back0/pallas_call | solution.py:729
  256.4 4.9 %collective-permute-done.73.refs_6_ = bf16[256,768]{1,0:T(8,128)(2,1)S(1)} collective-permute-done((bf16[256,768]{1,0:T(8,128)(2,1)S(1)}, bf16[256,768]{1,0:T(8,128)(2,1)S(1)}, u32[]{:S(2)}, u32[]{:S(2)}) %collective-permute-start.73) | collective-permute-done | bytes 393248 | tf_op jit(solution)/shard_map/sum_k0_second/ppermute | solution.py:39
  309.2 6.7 %collective-permute-done.86.refs_15_ = bf16[256,768]{1,0:T(8,128)(2,1)S(1)} collective-permute-done((bf16[256,768]{1,0:T(8,128)(2,1)S(1)}, bf16[256,768]{1,0:T(8,128)(2,1)S(1)}, u32[]{:S(2)}, u32[]{:S(2)}) %collective-permute-start.86) | collective-permute-done | bytes 393248 | tf_op jit(solution)/shard_map/sum_k1_second/ppermute | solution.py:43
  326.3 7.5 %collective-permute-done.100.refs_1_ = bf16[256,768]{1,0:T(8,128)(2,1)S(1)} collective-permute-done((bf16[256,768]{1,0:T(8,128)(2,1)S(1)}, bf16[256,768]{1,0:T(8,128)(2,1)S(1)}, u32[]{:S(2)}, u32[]{:S(2)}) %collective-permute-start.100) | collective-permute-done | bytes 393248 | tf_op jit(solution)/shard_map/sum_k2_first/ppermute | solution.py:43
  342.2 7.9 %collective-permute-done.106.refs_3_ = bf16[512,192]{1,0:T(8,128)(2,1)S(1)} collective-permute-done((bf16[512,192]{1,0:T(8,128)(2,1)S(1)}, bf16[512,192]{1,0:T(8,128)(2,1)S(1)}, u32[]{:S(2)}, u32[]{:S(2)}) %collective-permute-start.106) | collective-permute-done | bytes 196640 | tf_op jit(solution)/shard_map/sum_back0/ppermute | solution.py:39
  357.6 4.1 %collective-permute-done.112.refs_3_ = bf16[96,2432]{1,0:T(8,128)(2,1)S(1)} collective-permute-done((bf16[96,2432]{1,0:T(8,128)(2,1)S(1)}, bf16[96,2432]{1,0:T(8,128)(2,1)S(1)}, u32[]{:S(2)}, u32[]{:S(2)}) %collective-permute-start.112) | collective-permute-done | bytes 466976 | tf_op jit(solution)/shard_map/place_layer0/ppermute | solution.py:43
  362.6 6.6 %momentum1.1 = (f32[2,96,9216]{2,1,0:T(8,128)}, f32[2,8448]{1,0:T(2,128)}) custom-call(f32[2,96,9216]{2,1,0:T(8,128)} %refs_0_.7, f32[2,96,9216]{2,1,0:T(8,128)} %refs_1_.28, f32[2,8448]{1,0:T(2,128)} %refs_2_.20, f32[2,8448]{1,0:T(2,128)} %refs_2_.21, f32[2,96,9216]{2,1,0:T(8,128)} %get-tuple-element.246.refs_4_, ...), custom_call_target="tpu_custom_call", output_to_operand_aliasing={{0}: (4, {})} | custom-call | flops 1 | bytes 1 | tf_op jit(solution)/shard_map/momentum1/pallas_call | solution.py:729
  375.8 4.4 %collective-permute-done.113.refs_4_ = bf16[96,2432]{1,0:T(8,128)(2,1)S(1)} collective-permute-done((bf16[96,2432]{1,0:T(8,128)(2,1)S(1)}, bf16[96,2432]{1,0:T(8,128)(2,1)S(1)}, u32[]{:S(2)}, u32[]{:S(2)}) %collective-permute-start.113) | collective-permute-done | bytes 466976 | tf_op jit(solution)/shard_map/place_layer0/ppermute | solution.py:43
  (296 shorter events, 248.7 us)
Async XLA Ops:
  28.5 16.4 %collective-permute-start.4 = (bf16[96,1536]{1,0:T(8,128)(2,1)S(1)}, bf16[96,1536]{1,0:T(8,128)(2,1)S(1)}, u32[]{:S(2)}, u32[]{:S(2)}) collective-permute-start(bf16[96,1536]{1,0:T(8,128)(2,1)S(1)} %copy-done.9), channel_id=1, source_target_pairs={{0,6},{1,7},{2,0},{3,1},{4,2},{5,3},{6,4},{7,5},{8,14},{9,15},{10,... | collective-permute-start | bytes 884744 | tf_op jit(solution)/shard_map/weights_unit_1/ppermute | solution.py:53
  30.3 20.2 %collective-permute-start.20 = (bf16[96,1536]{1,0:T(8,128)(2,1)S(1)}, bf16[96,1536]{1,0:T(8,128)(2,1)S(1)}, u32[]{:S(2)}, u32[]{:S(2)}) collective-permute-start(bf16[96,1536]{1,0:T(8,128)(2,1)S(1)} %copy-done.9), channel_id=1, source_target_pairs={{0,4},{1,5},{2,6},{3,7},{4,0},{5,1},{6,2},{7,3},{8,12},{9,13},{10,... | collective-permute-start | bytes 884744 | tf_op jit(solution)/shard_map/weights_unit_1/ppermute | solution.py:53
  75.6 18.6 %collective-permute-start.35 = (bf16[96,1536]{1,0:T(8,128)(2,1)S(1)}, bf16[96,1536]{1,0:T(8,128)(2,1)S(1)}, u32[]{:S(2)}, u32[]{:S(2)}) collective-permute-start(bf16[96,1536]{1,0:T(8,128)(2,1)S(1)} %copy-done.13), channel_id=1, source_target_pairs={{0,6},{1,7},{2,0},{3,1},{4,2},{5,3},{6,4},{7,5},{8,14},{9,15},{10,... | collective-permute-start | bytes 884744 | tf_op jit(solution)/shard_map/weights_unit_3/ppermute | solution.py:53
  84.8 19.1 %collective-permute-start.34 = (bf16[96,1536]{1,0:T(8,128)(2,1)S(1)}, bf16[96,1536]{1,0:T(8,128)(2,1)S(1)}, u32[]{:S(2)}, u32[]{:S(2)}) collective-permute-start(bf16[96,1536]{1,0:T(8,128)(2,1)S(1)} %copy-done.13), channel_id=1, source_target_pairs={{0,4},{1,5},{2,6},{3,7},{4,0},{5,1},{6,2},{7,3},{8,12},{9,13},{10,... | collective-permute-start | bytes 884744 | tf_op jit(solution)/shard_map/weights_unit_3/ppermute | solution.py:53
  94.7 17.5 %collective-permute-start.43 = (bf16[96,2304]{1,0:T(8,128)(2,1)S(1)}, bf16[96,2304]{1,0:T(8,128)(2,1)S(1)}, u32[]{:S(2)}, u32[]{:S(2)}) collective-permute-start(bf16[96,2304]{1,0:T(8,128)(2,1)S(1)} %copy-done.5), channel_id=1, source_target_pairs={{0,2},{1,3},{2,4},{3,5},{4,6},{5,7},{8,10},{9,11},{10,12},{11,13},... | collective-permute-start | bytes 1327112 | tf_op jit(solution)/shard_map/weights_unit_4/ppermute | solution.py:96
  96.6 20.0 %collective-permute-start.46 = (bf16[96,2304]{1,0:T(8,128)(2,1)S(1)}, bf16[96,2304]{1,0:T(8,128)(2,1)S(1)}, u32[]{:S(2)}, u32[]{:S(2)}) collective-permute-start(bf16[96,2304]{1,0:T(8,128)(2,1)S(1)} %copy-done.5), channel_id=1, source_target_pairs={{2,0},{3,1},{4,2},{5,3},{6,4},{7,5},{10,8},{11,9},{12,10},{13,11},... | collective-permute-start | bytes 1327112 | tf_op jit(solution)/shard_map/weights_unit_4/ppermute | solution.py:96
  126.4 26.2 %collective-permute-start.59 = (bf16[96,2304]{1,0:T(8,128)(2,1)S(1)}, bf16[96,2304]{1,0:T(8,128)(2,1)S(1)}, u32[]{:S(2)}, u32[]{:S(2)}) collective-permute-start(bf16[96,2304]{1,0:T(8,128)(2,1)S(1)} %copy-done.5), channel_id=1, source_target_pairs={{0,1},{1,0},{2,3},{3,2},{4,5},{5,4},{6,7},{7,6},{8,9},{9,8},{10,11... | collective-permute-start | bytes 1327112 | tf_op jit(solution)/shard_map/weights_unit_4/ppermute | solution.py:48
  129.8 22.9 %collective-permute-start.48 = (bf16[96,2304]{1,0:T(8,128)(2,1)S(1)}, bf16[96,2304]{1,0:T(8,128)(2,1)S(1)}, u32[]{:S(2)}, u32[]{:S(2)}) collective-permute-start(bf16[96,2304]{1,0:T(8,128)(2,1)S(1)} %second.2.refs_6_.refs_10_), channel_id=1, source_target_pairs={{4,6},{5,7},{2,0},{3,1},{12,14},{13,15},{10,8},{11,9},{20,22},{21,... | collective-permute-start | bytes 1327112 | tf_op jit(solution)/shard_map/weights_unit_4/ppermute | solution.py:109
  197.1 18.4 %collective-permute-start.75 = (bf16[256,768]{1,0:T(8,128)(2,1)S(1)}, bf16[256,768]{1,0:T(8,128)(2,1)S(1)}, u32[]{:S(2)}, u32[]{:S(2)}) collective-permute-start(bf16[256,768]{1,0:T(8,128)(2,1)S(1)} %add_parts.33.refs_3_.refs_7_.refs_10_), channel_id=1, source_target_pairs={{0,8},{8,0},{16,24},{24,16},{1,9},{9,1},{17,25},{25,17},{2,10},{10... | collective-permute-start | bytes 1179656 | tf_op jit(solution)/shard_map/sum_back2_second/ppermute | solution.py:39
  197.9 17.6 %collective-permute-start.74 = (bf16[256,768]{1,0:T(8,128)(2,1)S(1)}, bf16[256,768]{1,0:T(8,128)(2,1)S(1)}, u32[]{:S(2)}, u32[]{:S(2)}) collective-permute-start(bf16[256,768]{1,0:T(8,128)(2,1)S(1)} %add_parts.32.refs_2_.refs_5_.refs_9_), channel_id=1, source_target_pairs={{0,16},{16,0},{8,24},{24,8},{1,17},{17,1},{9,25},{25,9},{2,18},{18... | collective-permute-start | bytes 1179656 | tf_op jit(solution)/shard_map/sum_back2_second/ppermute | solution.py:43
  200.3 20.6 %collective-permute-start.80 = (bf16[96,2304]{1,0:T(8,128)(2,1)S(1)}, bf16[96,2304]{1,0:T(8,128)(2,1)S(1)}, u32[]{:S(2)}, u32[]{:S(2)}) collective-permute-start(bf16[96,2304]{1,0:T(8,128)(2,1)S(1)} %get-tuple-element.195), channel_id=1, source_target_pairs={{0,2},{1,3},{8,10},{9,11},{16,18},{17,19},{24,26},{25,27}} | collective-permute-start | bytes 1327112 | tf_op jit(solution)/shard_map/grad_layer1/ppermute | solution.py:104
  221.7 18.5 %collective-permute-start.83 = (bf16[96,2304]{1,0:T(8,128)(2,1)S(1)}, bf16[96,2304]{1,0:T(8,128)(2,1)S(1)}, u32[]{:S(2)}, u32[]{:S(2)}) collective-permute-start(bf16[96,2304]{1,0:T(8,128)(2,1)S(1)} %get-tuple-element.203), channel_id=1, source_target_pairs={{0,2},{1,3},{2,4},{3,5},{8,10},{9,11},{10,12},{11,13},{16,18},{17,... | collective-permute-start | bytes 1327112 | tf_op jit(solution)/shard_map/grad_layer1/ppermute | solution.py:104
  261.5 17.4 %collective-permute-start.53 = (bf16[96,2304]{1,0:T(8,128)(2,1)S(1)}, bf16[96,2304]{1,0:T(8,128)(2,1)S(1)}, u32[]{:S(2)}, u32[]{:S(2)}) collective-permute-start(bf16[96,2304]{1,0:T(8,128)(2,1)S(1)} %second.3.refs_2_.refs_6_.refs_10_), channel_id=1, source_target_pairs={{4,6},{5,7},{2,0},{3,1},{12,14},{13,15},{10,8},{11,9},{20,22},{21,... | collective-permute-start | bytes 1327112 | tf_op jit(solution)/shard_map/weights_unit_5/ppermute | solution.py:109
  275.8 16.5 %collective-permute-start.93 = (bf16[96,2432]{1,0:T(8,128)(2,1)S(1)}, bf16[96,2432]{1,0:T(8,128)(2,1)S(1)}, u32[]{:S(2)}, u32[]{:S(2)}) collective-permute-start(bf16[96,2432]{1,0:T(8,128)(2,1)S(1)} %get-tuple-element.229), channel_id=1, source_target_pairs={{0,2},{1,3},{2,4},{3,5},{8,10},{9,11},{10,12},{11,13},{16,18},{17,... | collective-permute-start | bytes 1400840 | tf_op jit(solution)/shard_map/grad_layer0/ppermute | solution.py:104
  297.6 18.4 %collective-permute-start.86 = (bf16[256,768]{1,0:T(8,128)(2,1)S(1)}, bf16[256,768]{1,0:T(8,128)(2,1)S(1)}, u32[]{:S(2)}, u32[]{:S(2)}) collective-permute-start(bf16[256,768]{1,0:T(8,128)(2,1)S(1)} %add_parts.38.refs_14_), channel_id=1, source_target_pairs={{0,16},{16,0},{8,24},{24,8},{1,17},{17,1},{9,25},{25,9},{2,18},{18... | collective-permute-start | bytes 1179656 | tf_op jit(solution)/shard_map/sum_k1_second/ppermute | solution.py:43
  298.7 17.2 %collective-permute-start.95 = (bf16[256,768]{1,0:T(8,128)(2,1)S(1)}, bf16[256,768]{1,0:T(8,128)(2,1)S(1)}, u32[]{:S(2)}, u32[]{:S(2)}) collective-permute-start(bf16[256,768]{1,0:T(8,128)(2,1)S(1)} %add_parts.39.refs_16_), channel_id=1, source_target_pairs={{0,8},{8,0},{16,24},{24,16},{1,9},{9,1},{17,25},{25,17},{2,10},{10... | collective-permute-start | bytes 1179656 | tf_op jit(solution)/shard_map/sum_k1_second/ppermute | solution.py:39
  299.4 21.8 %collective-permute-start.103 = (bf16[96,2432]{1,0:T(8,128)(2,1)S(1)}, bf16[96,2432]{1,0:T(8,128)(2,1)S(1)}, u32[]{:S(2)}, u32[]{:S(2)}) collective-permute-start(bf16[96,2432]{1,0:T(8,128)(2,1)S(1)} %get-tuple-element.231.refs_4_), channel_id=1, source_target_pairs={{0,2},{1,3},{2,4},{3,5},{4,6},{5,7},{8,10},{9,11},{10,12},{11,13},... | collective-permute-start | bytes 1400840 | tf_op jit(solution)/shard_map/grad_layer0/ppermute | solution.py:104
  307.5 17.9 %collective-permute-start.101 = (bf16[96,2304]{1,0:T(8,128)(2,1)S(1)}, bf16[96,2304]{1,0:T(8,128)(2,1)S(1)}, u32[]{:S(2)}, u32[]{:S(2)}) collective-permute-start(bf16[96,2304]{1,0:T(8,128)(2,1)S(1)} %total.2.refs_1_), channel_id=1, source_target_pairs={{0,16},{16,0},{8,24},{24,8},{1,17},{17,1},{9,25},{25,9},{2,18},{18... | collective-permute-start | bytes 1327112 | tf_op jit(solution)/shard_map/place_layer1/ppermute | solution.py:43
  321.4 19.1 %collective-permute-start.111 = (bf16[96,2432]{1,0:T(8,128)(2,1)S(1)}, bf16[96,2432]{1,0:T(8,128)(2,1)S(1)}, u32[]{:S(2)}, u32[]{:S(2)}) collective-permute-start(bf16[96,2432]{1,0:T(8,128)(2,1)S(1)} %total.3.refs_1_), channel_id=1, source_target_pairs={{0,8},{8,0},{16,24},{24,16},{1,9},{9,1},{17,25},{25,17},{2,10},{10... | collective-permute-start | bytes 1400840 | tf_op jit(solution)/shard_map/place_layer0/ppermute | solution.py:39
  325.4 26.7 %collective-permute-start.105 = (bf16[96,2304]{1,0:T(8,128)(2,1)S(1)}, bf16[96,2304]{1,0:T(8,128)(2,1)S(1)}, u32[]{:S(2)}, u32[]{:S(2)}) collective-permute-start(bf16[96,2304]{1,0:T(8,128)(2,1)S(1)} %collective-permute-done.96.refs_20_.refs_2_), channel_id=1, source_target_pairs={{0,16},{16,0},{8,24},{24,8},{1,17},{17,1},{9,25},{25,9},{2,18},{18... | collective-permute-start | bytes 1327112 | tf_op jit(solution)/shard_map/place_layer1/ppermute | solution.py:43
  333.9 18.2 %collective-permute-start.102 = (bf16[256,768]{1,0:T(8,128)(2,1)S(1)}, bf16[256,768]{1,0:T(8,128)(2,1)S(1)}, u32[]{:S(2)}, u32[]{:S(2)}) collective-permute-start(bf16[256,768]{1,0:T(8,128)(2,1)S(1)} %add_parts.41.refs_5_), channel_id=1, source_target_pairs={{0,8},{8,0},{16,24},{24,16},{1,9},{9,1},{17,25},{25,17},{2,10},{10... | collective-permute-start | bytes 1179656 | tf_op jit(solution)/shard_map/sum_k2_second/ppermute | solution.py:39
  334.7 17.4 %collective-permute-start.99 = (bf16[256,768]{1,0:T(8,128)(2,1)S(1)}, bf16[256,768]{1,0:T(8,128)(2,1)S(1)}, u32[]{:S(2)}, u32[]{:S(2)}) collective-permute-start(bf16[256,768]{1,0:T(8,128)(2,1)S(1)} %add_parts.40.refs_3_), channel_id=1, source_target_pairs={{0,16},{16,0},{8,24},{24,8},{1,17},{17,1},{9,25},{25,9},{2,18},{18... | collective-permute-start | bytes 1179656 | tf_op jit(solution)/shard_map/sum_k2_second/ppermute | solution.py:43
  340.5 21.2 %collective-permute-start.112 = (bf16[96,2432]{1,0:T(8,128)(2,1)S(1)}, bf16[96,2432]{1,0:T(8,128)(2,1)S(1)}, u32[]{:S(2)}, u32[]{:S(2)}) collective-permute-start(bf16[96,2432]{1,0:T(8,128)(2,1)S(1)} %total.3.refs_1_), channel_id=1, source_target_pairs={{0,16},{16,0},{8,24},{24,8},{1,17},{17,1},{9,25},{25,9},{2,18},{18... | collective-permute-start | bytes 1400840 | tf_op jit(solution)/shard_map/place_layer0/ppermute | solution.py:43
  361.7 18.4 %collective-permute-start.113 = (bf16[96,2432]{1,0:T(8,128)(2,1)S(1)}, bf16[96,2432]{1,0:T(8,128)(2,1)S(1)}, u32[]{:S(2)}, u32[]{:S(2)}) collective-permute-start(bf16[96,2432]{1,0:T(8,128)(2,1)S(1)} %collective-permute-done.111.refs_2_), channel_id=1, source_target_pairs={{0,16},{16,0},{8,24},{24,8},{1,17},{17,1},{9,25},{25,9},{2,18},{18... | collective-permute-start | bytes 1400840 | tf_op jit(solution)/shard_map/place_layer0/ppermute | solution.py:43
  (107 other events, 1240.6 us)
